TPU v7x, 32 devices: a whole 2x2x4 slice. The times are simulated.
32 devices in a mesh: pts: 4 (over x, core), rows: 8 (over z, y).
Axes of the slice: x: 2, y: 2, z: 4, core: 2. Of those that a mesh axis runs over, the one named last changes fastest.
Arguments:
- solutions: bfloat16 [8, 65536, 128], P('pts', 'rows'), may hold values from -6 to 6
- probe: bfloat16 [64, 65536], P(None, 'rows'), may hold values from -0.0234375 to 0.0234375
- left_factor: float32 [256, 256], replicated, may hold values from -0.375 to 0.375
- singular: float32 [256], replicated, may hold values from 1 to 13.8, as said below
- right_factor: float32 [256, 256], replicated, may hold values from -0.375 to 0.375
- reduced_adjoint: float32 [256, 256], replicated, may hold values from -6 to 6
Outputs:
- solution_adjoint: bfloat16 [8, 65536, 128], P('pts', 'rows')
Inputs may be any that keep to these rules, and one draw needn't show every extreme that they name: `singular`: rising, each value at least 0.03 above the one before.
All inputs are finite; a program needn't handle non-finite values.
Results may differ from a plain program's by a relative error of at most 0.0049.
Values sent between devices are 32-bit elements; how exact they have to be, the bound alone decides.
No kernel may reach another device: no remote copies, remote signals or barrier semaphores. Data moves between devices by JAX's collectives and lax.ppermute only.
A program may use at most 64 MiB of HBM per device.

v0:
```python
import math

import jax
import jax.numpy as jnp
from jax import lax
from jax.sharding import PartitionSpec as P

L = 64
K = 4


def coefficients(first, count, total, orders):
    theta = math.pi * (first + jnp.arange(count, dtype=jnp.float32) + 0.5) / total
    angle = theta[:, None] * orders[None, :]
    return (jnp.cos(angle) / total, jnp.sin(angle) / total)


def matmul(first, second):
    return jnp.dot(
        first, second, precision=lax.Precision.HIGHEST, preferred_element_type=jnp.float32
    )


def svd_back(hankel, left, sing, right, adjoint):
    quot = matmul(left.T, hankel)
    prod_right = matmul(hankel, right)
    zmat = matmul(quot, right)
    zbar = adjoint / sing[None, :]
    sbar = -jnp.sum(adjoint * zmat, axis=0) / (sing * sing)
    ubar = matmul(prod_right, zbar.T)
    wbar = matmul(quot.T, zbar)
    left_term = matmul(left.T, ubar)
    right_term = matmul(right.T, wbar)
    square = sing * sing
    eye_mask = jnp.eye(sing.shape[0], dtype=bool)
    recip = jnp.where(
        eye_mask, 0.0, 1.0 / jnp.where(eye_mask, 1.0, square[None, :] - square[:, None])
    )
    core = (
        recip * (left_term - left_term.T) * sing[None, :]
        + jnp.diag(sbar)
        + sing[:, None] * (recip * (right_term - right_term.T))
    )
    return (core, zbar)


def build_hankel(moments):
    return jnp.concatenate(
        [jnp.concatenate([moments[i + j] for j in range(K)], axis=1) for i in range(K)], axis=0
    )


def per_device(solutions, probe, left_factor, singular, right_factor, reduced_adjoint):
    hi = lax.Precision.HIGHEST
    point_count = solutions.shape[0]
    total = point_count * lax.axis_size("pts")
    first = (lax.axis_index("pts") * point_count).astype(jnp.float32)
    orders = jnp.arange(1, 2 * K + 1, dtype=jnp.float32)
    cos_t, sin_t = coefficients(first, point_count, total, orders)
    gram = jnp.einsum("ln,pnc->plc", probe, solutions, preferred_element_type=jnp.float32)
    summed = lax.psum(gram, "rows")
    moments = lax.psum(
        jnp.einsum("pk,plc->klc", cos_t[:, 1:], summed[:, :, :L], precision=hi)
        - jnp.einsum("pk,plc->klc", sin_t[:, 1:], summed[:, :, L:], precision=hi),
        "pts",
    )
    hankel = build_hankel(moments)
    core, zbar = svd_back(hankel, left_factor, singular, right_factor, reduced_adjoint)
    first_bar = matmul(matmul(left_factor, core), right_factor.T)
    second_bar = matmul(matmul(left_factor, zbar), right_factor.T)
    blocks = [jnp.zeros((L, L), jnp.float32) for k in range(2 * K)]
    for i in range(K):
        for j in range(K):
            blocks[i + j] = blocks[i + j] + first_bar[i * L : (i + 1) * L, j * L : (j + 1) * L]
            blocks[i + j + 1] = (
                blocks[i + j + 1] + second_bar[i * L : (i + 1) * L, j * L : (j + 1) * L]
            )
    moment_adjoint = jnp.stack(blocks)
    weights = jnp.concatenate(
        [
            jnp.einsum("pk,klc->plc", cos_t, moment_adjoint, precision=hi),
            -jnp.einsum("pk,klc->plc", sin_t, moment_adjoint, precision=hi),
        ],
        axis=2,
    ).astype(jnp.bfloat16)
    result = jnp.einsum("ln,plc->pnc", probe, weights, preferred_element_type=jnp.float32)
    return result.astype(jnp.bfloat16)


def solution(mesh):
    in_specs = (P("pts", "rows", None), P(None, "rows"), P(), P(), P(), P())
    out_specs = P("pts", "rows", None)
    return jax.shard_map(
        per_device, mesh=mesh, in_specs=in_specs, out_specs=out_specs, check_vma=False
    )
```

profile of v0, /device:TPU:0, one launch (start us, length us, event | category | flops | bytes accessed | tf_op | source)
XLA Modules:
  0.0 143.3 jit_solution(10416773007985884967)
XLA Ops:
  6.5 0.0 copy-start
  6.5 0.0 copy-start.4
  6.5 0.0 copy-start.3
  6.5 0.0 copy-start.2
  6.5 0.0 copy-start.1
  6.5 0.0 all-reduce.3.cloned.1.call-start
  6.6 1.2 copy-done
  7.8 3.6 %convolution_bitcast_fusion = f32[2,64,128]{2,1,0:T(8,128)} fusion(bf16[2,8192,128]{2,1,0:T(8,128)(2,1)} %param.6, bf16[64,8192]{1,0:T(8,128)(2,1)S(1)} %copy-done), kind=kOutput, calls=%fused_computation.5 | convolution fusion | flops 268435456 | bytes 5308416 | tf_op jit(solution)/shard_map/ln,pnc->plc/dot_general | solution.py:60
  11.4 0.0 all-reduce.3.cloned.1.call-update
  11.4 0.0 all-reduce.5.cloned.1.call-start
  11.5 0.0 copy-done.4
  11.5 0.0 copy-done.3
  11.5 0.0 copy-done.2
  11.5 0.6 fusion.63
  12.1 0.1 fusion.51
  12.2 70.5 %all-reduce.3.cloned.1.call-done = f32[2,64,128]{2,1,0:T(8,128)} async-done(((f32[2,64,128]{2,1,0:T(8,128)}), f32[2,64,128]{2,1,0:T(8,128)}) %all-reduce.3.cloned.1.call-update) | async-done | bytes 65552 | tf_op jit(solution)/shard_map/psum | solution.py:61
  82.7 1.0 fusion.69
  83.7 0.5 fusion.31
  84.2 1.2 convolution_subtract_fusion
  85.4 0.0 all-reduce.5.cloned.1.call-update
  85.4 0.0 copy-done.1
  85.4 0.6 fusion.73
  86.0 31.4 %all-reduce.5.cloned.1.call-done = f32[7,64,64]{2,0,1:T(8,128)} async-done(((f32[7,64,64]{2,0,1:T(8,128)}), f32[7,64,64]{2,0,1:T(8,128)}) %all-reduce.5.cloned.1.call-update) | async-done | bytes 114704 | tf_op jit(solution)/shard_map/psum | solution.py:62
  117.5 2.1 %fusion.68 = (f32[1,64,64]{2,0,1:T(1,128)S(1)}, f32[1,64,64]{2,0,1:T(1,128)S(1)}, f32[1,64,64]{2,0,1:T(1,128)S(1)}, f32[1,64,64]{2,0,1:T(1,128)S(1)}, f32[1,64,6...) fusion(f32[7,64,64]{2,0,1:T(8,128)} %all-reduce.5.cloned.1.call-done), kind=kLoop, calls=%fused_computation.106 | loop fusion | bytes 229376 | tf_op jit(solution)/shard_map/slice | solution.py:49
  119.6 0.7 fusion.66
  120.3 0.6 fusion.1
  120.9 0.4 fusion.64
  121.3 0.4 fusion.67
  121.8 0.6 fusion.71
  122.4 0.4 fusion.65
  122.8 0.6 fusion.70
  123.4 0.1 copy.15
  123.6 0.1 copy.16
  123.7 0.7 fusion.7
  124.5 0.6 fusion.72
  125.1 0.1 fusion.45
  125.1 0.1 fusion.43
  125.2 0.1 fusion.41
  125.3 0.1 fusion.39
  125.4 0.1 fusion.37
  125.5 0.1 fusion.35
  125.6 0.1 fusion.33
  125.7 0.5 fusion.20
  126.2 0.5 fusion.18
  126.8 3.3 %fusion = bf16[2,8192,128]{1,2,0:T(8,128)(2,1)} fusion(bf16[64,8192]{1,0:T(8,128)(2,1)S(1)} %copy-done, bf16[2,64,64]{2,1,0:T(8,128)(2,1)S(1)} %fusion.29, bf16[2,64,64]{2,1,0:T(8,128)(2,1)S(1)} %copy.39), kind=kOutput, calls=%fused_computation.1 | convolution fusion | flops 270598144 | bytes 5275648 | tf_op jit(solution)/shard_map/ln,plc->pnc/dot_general | solution.py:86
  130.1 6.3 %copy.17 = bf16[2,8192,128]{2,1,0:T(8,128)(2,1)} copy(bf16[2,8192,128]{1,2,0:T(8,128)(2,1)} %fusion) | data formatting | bytes 8388608 | tf_op jit(solution)/shard_map/convert_element_type | solution.py:87
  (6 shorter events, 0.0 us)
Async XLA Ops:
  6.5 1.2 copy-start
  6.5 4.9 %copy-start.4 = (f32[256]{0:T(256)S(1)}, f32[256]{0:T(256)}, u32[]{:S(2)}) copy-start(f32[256]{0:T(256)} %param.9) | copy-start | bytes 3076
  6.5 5.0 %copy-start.3 = (f32[256,256]{1,0:T(8,128)S(1)}, f32[256,256]{1,0:T(8,128)}, u32[]{:S(2)}) copy-start(f32[256,256]{1,0:T(8,128)} %param.11) | copy-start | bytes 786436
  6.5 5.0 %copy-start.2 = (f32[256,256]{1,0:T(8,128)S(1)}, f32[256,256]{1,0:T(8,128)}, u32[]{:S(2)}) copy-start(f32[256,256]{1,0:T(8,128)} %param.8) | copy-start | bytes 786436
  6.5 78.9 %copy-start.1 = (f32[256,256]{1,0:T(8,128)S(1)}, f32[256,256]{1,0:T(8,128)}, u32[]{:S(2)}) copy-start(f32[256,256]{1,0:T(8,128)} %param.10) | copy-start | bytes 786436
  6.5 76.1 %all-reduce.3.cloned.1.call-start = ((), (), s32[]{:S(2)}) async-start(), calls=%async_computation | async-start | bytes 131072 | tf_op jit(solution)/shard_map/psum | solution.py:61
  11.4 106.1 %all-reduce.5.cloned.1.call-start = ((), (), s32[]{:S(2)}) async-start(), calls=%async_computation.1 | async-start | bytes 524288 | tf_op jit(solution)/shard_map/psum | solution.py:62
Sparse Core Ops, SparseCore 0:
  11.5 71.1 all-reduce.2
  85.5 31.8 all-reduce.4
where the time goes:
time: 144 us; the launch traced here: 143 us
  waiting for transfers between devices  102 us (71%)
  matrix products  16 us (11%)
  between operations  13.7 us (10%)
  local copies, waits for them, and re-layouts  10.9 us (8%)
    psum x1, waiting for transfers between devices, per_device(): summed = lax.psum(gram, 'rows')  70.5 us
    psum x1, waiting for transfers between devices, per_device(): lax.psum(jnp.einsum('pk,plc->klc', cos_t[:, 1:], summed[:, :, :L], precis...  31.4 us
    dot_general x11, matrix products, matmul(): jnp.dot(first, second, precision=lax.Precision.HIGHEST, preferred_element...  6.32 us
    convert_element_type x1, local copies, waits for them, and re-layouts, per_device(): return result.astype(jnp.bfloat16)  6.31 us
    dot_general x1, matrix products, per_device(): jnp.einsum('ln,pnc->plc', probe, solutions, preferred_element_type=jnp.fl...  3.61 us
    dot_general x1, matrix products, per_device(): jnp.einsum('ln,plc->pnc', probe, weights, preferred_element_type=jnp.floa...  3.3 us
  transfers between devices with their start and end apart: 2, of which 2 were waited for; matrix products, arithmetic and copies ran while one was open for 1% of the time, Pallas kernels for 0%

commit v1 on v0

v1 whole, which is shorter than its diff:
```python
import functools
import math

import jax
import jax.numpy as jnp
import numpy as np
from jax import lax
from jax.experimental import pallas as pl
from jax.experimental.pallas import tpu as pltpu
from jax.sharding import PartitionSpec as P

F32 = jnp.float32
BF16 = jnp.bfloat16
VMEM_BYTES = 50 * 1024 * 1024


def dot(first, second):
    return jnp.dot(first, second, preferred_element_type=F32)


def split(value):
    high = value.astype(BF16)
    return high, (value - high.astype(F32)).astype(BF16)


def left3(value):
    high, low = split(value)
    return jnp.concatenate([high, high, low], axis=1)


def right3(value):
    high, low = split(value)
    return jnp.concatenate([high, low, high], axis=0)


def moment_table(total, blocks, width):
    theta = math.pi * (np.arange(total) + 0.5) / total
    table = np.zeros((total, 2 * blocks, 2 * width), np.float32)
    for a in range(blocks):
        left = 2 * a + 2
        right = left + 1 if a < blocks - 1 else left
        cos_l, sin_l = np.cos(left * theta) / total, np.sin(left * theta) / total
        cos_r, sin_r = np.cos(right * theta) / total, np.sin(right * theta) / total
        table[:, a, :width] = cos_l[:, None]
        table[:, a, width:] = -sin_r[:, None]
        table[:, blocks + a, :width] = -sin_l[:, None]
        table[:, blocks + a, width:] = cos_r[:, None]
    return table


def phase_table(total, blocks):
    theta = math.pi * (np.arange(total)[:, None] + 0.5) / total
    half = theta * (np.arange(blocks + 1)[None, :] + 0.5)
    return np.concatenate([np.cos(half), -np.sin(half)], axis=1).astype(np.float32)


def gram_kernel(chunks, blocks, probe_hbm, sol_hbm, table_ref, keep_ref, send_ref, pbuf, sbuf, psem, ssem):
    count, local, width2 = sbuf.shape
    width = width2 // 2
    size = local // chunks
    me = lax.axis_index("pts")

    def copies(c):
        at = pl.ds(c * size, size)
        return (
            pltpu.make_async_copy(probe_hbm.at[:, at], pbuf.at[:, at], psem.at[c]),
            pltpu.make_async_copy(sol_hbm.at[:, at, :], sbuf.at[:, at, :], ssem.at[c]),
        )

    for c in range(chunks):
        for copy in copies(c):
            copy.start()
    gram = None
    for c in range(chunks):
        for copy in copies(c):
            copy.wait()
        at = pl.ds(c * size, size)
        side = jnp.concatenate([sbuf[p, at, :] for p in range(count)], axis=1)
        part = dot(pbuf[:, at], side)
        gram = part if gram is None else gram + part
    tiles = [None] * blocks
    for p in range(count):
        straight = gram[:, p * width2 : (p + 1) * width2]
        turned = pltpu.roll(straight, width, 1)
        coef = table_ref[me * count + p]
        for a in range(blocks):
            term = straight * coef[a : a + 1] + turned * coef[blocks + a : blocks + a + 1]
            tiles[a] = term if tiles[a] is None else tiles[a] + term
    rows = gram.shape[0] // 2
    lane = lax.broadcasted_iota(jnp.int32, (rows // 2, width2), 1)
    halves = []
    for h in range(2):
        cut = [tile[h * rows : (h + 1) * rows] for tile in tiles]
        last = jnp.where(lane < width, cut[-1][: rows // 2], cut[-1][rows // 2 :])
        halves.append(jnp.concatenate(cut[:-1] + [last], axis=0))
    first = me % 2 == 0
    keep_ref[...] = jnp.where(first, halves[0], halves[1])
    send_ref[...] = jnp.where(first, halves[1], halves[0])


def prep_kernel(
    count,
    blocks,
    left_ref,
    sing_ref,
    right_ref,
    adj_ref,
    phase_ref,
    ut3_ref,
    w3_ref,
    zt3_ref,
    zl3_ref,
    f1_ref,
    f2_ref,
    dg_ref,
    up3_ref,
    wc3_ref,
    y2_ref,
):
    me = lax.axis_index("pts")
    order = left_ref.shape[0]
    width = order // blocks
    left = left_ref[...]
    right = right_ref[...]
    sing = sing_ref[...]
    zbar = adj_ref[...] / sing
    ut3_ref[...] = left3(left.T)
    w3_ref[...] = right3(right)
    zbar_t = zbar.T
    zt3_ref[...] = right3(zbar_t)
    zl3_ref[...] = left3(zbar_t)
    by_column = jnp.broadcast_to(sing, (order, order))
    by_row = by_column.T
    row = lax.broadcasted_iota(jnp.int32, (order, order), 0)
    column = lax.broadcasted_iota(jnp.int32, (order, order), 1)
    eye = row == column
    recip = jnp.where(
        eye, 0.0, 1.0 / jnp.where(eye, 1.0, by_column * by_column - by_row * by_row)
    )
    f1_ref[...] = recip * by_column
    f2_ref[...] = recip * by_row
    dg_ref[...] = jnp.where(eye, -1.0 / by_column, 0.0)
    total = phase_ref.shape[0]
    up, up2 = [], []
    for p in range(count):
        def turn(source, by, sine):
            out = None
            for i in range(blocks):
                term = source[i * width : (i + 1) * width] * phase_ref[
                    me * count + p, sine * (blocks + 1) + by + i
                ]
                out = term if out is None else out + term
            return out

        up += [turn(left, 0, 0) * (1.0 / total), turn(left, 0, 1) * (1.0 / total)]
        up2 += [turn(left, 1, 0) * (1.0 / total), turn(left, 1, 1) * (1.0 / total)]
        wre, wim = turn(right, 0, 0).T, turn(right, 0, 1).T
        wc = jnp.concatenate(
            [jnp.concatenate([wre, wim], axis=1), jnp.concatenate([-wim, wre], axis=1)], axis=0
        )
        wc3_ref[p] = right3(wc)
    up3_ref[...] = left3(jnp.concatenate(up, axis=0))
    y2_ref[...] = dot(left3(jnp.concatenate(up2, axis=0)), right3(zbar))


def turn_kernel(probe_ref, out_ref):
    out_ref[...] = probe_ref[...].T


def post_kernel(
    chunks,
    blocks,
    own_ref,
    got_ref,
    ut3_ref,
    w3_ref,
    zt3_ref,
    zl3_ref,
    f1_ref,
    f2_ref,
    dg_ref,
    up3_ref,
    wc3_ref,
    y2_ref,
    probe_t_ref,
    out_hbm,
    obuf,
    osem,
):
    count, local, width2 = obuf.shape
    width = width2 // 2
    rows = width // 2
    first = lax.axis_index("pts") % 2 == 0
    own, got = own_ref[...], got_ref[...]
    halves = [jnp.where(first, own, got), jnp.where(first, got, own)]
    tiles = [
        jnp.concatenate([half[a * rows : (a + 1) * rows] for half in halves], axis=0)
        for a in range(blocks - 1)
    ]
    packed = [half[(blocks - 1) * rows :] for half in halves]
    last = jnp.concatenate(
        [piece for pack in packed for piece in (pltpu.roll(pack, width, 1), pack)], axis=0
    )
    lane = lax.broadcasted_iota(jnp.int32, (width, width2), 1)
    turned = [pltpu.roll(tile, width, 1) for tile in tiles] + [last]
    between = [jnp.where(lane < width, turned[a], turned[a + 1]) for a in range(blocks - 1)]
    every = [tile for pair in zip(tiles, between) for tile in pair]
    hankel = jnp.concatenate(
        [
            jnp.concatenate([every[i + j] for j in range(0, blocks, 2)], axis=1)
            for i in range(blocks)
        ],
        axis=0,
    )
    quot = dot(ut3_ref[...], right3(hankel))
    zmat = dot(left3(quot), w3_ref[...])
    left_term = dot(left3(zmat), zt3_ref[...])
    right_term = dot(zl3_ref[...], right3(zmat))
    core = (
        f1_ref[...] * (left_term - left_term.T)
        + f2_ref[...] * (right_term.T - right_term)
        + dg_ref[...] * right_term
    )
    prod = dot(up3_ref[...], right3(core)) + y2_ref[...]
    weights = []
    for p in range(count):
        at = 2 * p * width
        pair = jnp.concatenate([prod[at : at + width], prod[at + width : at + 2 * width]], axis=1)
        weights.append(dot(left3(pair), wc3_ref[p]).astype(BF16))
    weights = jnp.concatenate(weights, axis=1)
    size = local // chunks

    def copy(c):
        at = pl.ds(c * size, size)
        return pltpu.make_async_copy(obuf.at[:, at, :], out_hbm.at[:, at, :], osem.at[c])

    for c in range(chunks):
        at = pl.ds(c * size, size)
        part = dot(probe_t_ref[at, :], weights).astype(BF16)
        for p in range(count):
            obuf[p, at, :] = part[:, p * width2 : (p + 1) * width2]
        copy(c).start()
    for c in range(chunks):
        copy(c).wait()


def hop(value, axes, sizes, bits):
    total = math.prod(sizes)
    pairs = []
    for source in range(total):
        place, rest = [], source
        for size in reversed(sizes):
            place.append(rest % size)
            rest //= size
        place = [at ^ bit for at, bit in zip(reversed(place), bits)]
        target = 0
        for size, at in zip(sizes, place):
            target = target * size + at
        pairs.append((source, target))
    return lax.ppermute(value, axes, pairs)


def per_device(n_pts, n_rows, solutions, probe, left_factor, singular, right_factor, adjoint):
    count, local, width2 = solutions.shape
    width = probe.shape[0]
    order = left_factor.shape[0]
    blocks = order // width
    total = count * n_pts
    rows = (blocks - 1) * (width // 2) + width // 4
    chunks = 8 if local % 1024 == 0 else 1
    anyspace = pl.BlockSpec(memory_space=pl.ANY)
    vmem = pl.BlockSpec(memory_space=pltpu.VMEM)
    smem = pl.BlockSpec(memory_space=pltpu.SMEM)
    params = pltpu.CompilerParams(vmem_limit_bytes=VMEM_BYTES)
    half = jax.ShapeDtypeStruct((rows, width2), F32)
    keep, send = pl.pallas_call(
        functools.partial(gram_kernel, chunks, blocks),
        out_shape=(half, half),
        in_specs=[anyspace, anyspace, vmem],
        out_specs=(vmem, vmem),
        scratch_shapes=[
            pltpu.VMEM((width, local), BF16),
            pltpu.VMEM((count, local, width2), BF16),
            pltpu.SemaphoreType.DMA((chunks,)),
            pltpu.SemaphoreType.DMA((chunks,)),
        ],
        compiler_params=params,
        name="gram",
    )(probe, solutions, jnp.asarray(moment_table(total, blocks, width)))

    square = jax.ShapeDtypeStruct((order, order), F32)
    tall = jax.ShapeDtypeStruct((3 * order, order), BF16)
    wide = jax.ShapeDtypeStruct((order, 3 * order), BF16)
    stack = jax.ShapeDtypeStruct((2 * count * width, 3 * order), BF16)
    prep = pl.pallas_call(
        functools.partial(prep_kernel, count, blocks),
        out_shape=(
            wide,
            tall,
            tall,
            wide,
            square,
            square,
            square,
            stack,
            jax.ShapeDtypeStruct((count, 6 * order, width2), BF16),
            jax.ShapeDtypeStruct((2 * count * width, order), F32),
        ),
        in_specs=[vmem, vmem, vmem, vmem, smem],
        out_specs=(vmem,) * 10,
        compiler_params=params,
        cost_estimate=pl.CostEstimate(flops=6 * order**3, bytes_accessed=4 << 20, transcendentals=0),
        name="prep",
    )
    turn = pl.pallas_call(
        turn_kernel,
        out_shape=jax.ShapeDtypeStruct((local, width), BF16),
        in_specs=[vmem],
        out_specs=vmem,
        compiler_params=params,
        cost_estimate=pl.CostEstimate(flops=0, bytes_accessed=6 << 20, transcendentals=0),
        name="turn",
    )
    axes, sizes = ("pts", "rows"), (n_pts, n_rows)
    value = keep + hop(send, axes, sizes, (1, 0))
    phases = jnp.asarray(phase_table(total, blocks))
    value, tied = lax.optimization_barrier((value, (left_factor, singular, right_factor, adjoint)))
    ready = prep(tied[0], tied[1][None, :], tied[2], tied[3], phases)
    hops = [(1 << k, 0) for k in range(1, n_pts.bit_length() - 1)]
    hops += [(0, 1 << k) for k in range(n_rows.bit_length() - 1)]
    for at, bits in enumerate(hops):
        if at == len(hops) - 2:
            value, probe = lax.optimization_barrier((value, probe))
            probe_t = turn(probe)
        value = value + hop(value, axes, sizes, bits)
    other = hop(value, axes, sizes, (1, 0))
    return pl.pallas_call(
        functools.partial(post_kernel, chunks, blocks),
        out_shape=jax.ShapeDtypeStruct((count, local, width2), BF16),
        in_specs=[vmem] * 13,
        out_specs=anyspace,
        scratch_shapes=[
            pltpu.VMEM((count, local, width2), BF16),
            pltpu.SemaphoreType.DMA((chunks,)),
        ],
        compiler_params=params,
        name="post",
    )(value, other, *ready, probe_t)


def solution(mesh):
    in_specs = (P("pts", "rows", None), P(None, "rows"), P(), P(), P(), P())
    out_specs = P("pts", "rows", None)
    return jax.shard_map(
        functools.partial(per_device, mesh.shape["pts"], mesh.shape["rows"]),
        mesh=mesh,
        in_specs=in_specs,
        out_specs=out_specs,
        check_vma=False,
    )
```

time: 144 us -> 37.5 us (0.26)
  waiting for transfers between devices: 102 us -> 9.57 us
  matrix products: 16 us -> 0 us
  between operations: 13.7 us -> 0.11 us
  Pallas kernels: 0 us -> 11.7 us
  starting transfers between devices: 0.08 us -> 11.2 us
  local copies, waits for them, and re-layouts: 10.9 us -> 4.47 us
    psum x2 -> x0, waiting for transfers between devices: 102 us -> none  [the longest x1 70.5 us: per_device(): summed = lax.psum(gram, 'rows')]
    dot_general x17 -> x0, matrix products: 16 us -> none  [the longest x11 6.32 us: matmul(): jnp.dot(first, second, precision=lax.Precision.HIGHEST, preferred_element...]
    pallas_call x0 -> x4, Pallas kernels: none -> 11.7 us  [the longest x1 5.8 us: per_device(): pl.pallas_call(functools.partial(post_kernel, chunks, blocks), out_shape=...]
    ppermute x0 -> x6, starting transfers between devices: none -> 11.2 us  [hop(): return lax.ppermute(value, axes, pairs)]
    ppermute x0 -> x6, waiting for transfers between devices: none -> 9.57 us  [hop(): return lax.ppermute(value, axes, pairs)]
    convert_element_type x1 -> x0, local copies, waits for them, and re-layouts: 6.31 us -> none  [per_device(): return result.astype(jnp.bfloat16)]
    unnamed x11 -> x20, local copies, waits for them, and re-layouts: 1.19 us -> 4.47 us
    slice x2 -> x0, local copies, waits for them, and re-layouts: 3.08 us -> none  [the longest x1 2.09 us: build_hankel(): moments[i + j]]
  transfers between devices with their start and end apart: 2 -> 6, of which waited for: 2 -> 5; matrix products, arithmetic and copies ran while one was open for 1% -> 0% of each run, Pallas kernels for 0% -> 8%
where the time goes in v1:
time: 37.5 us; the launch traced here: 37.2 us
  Pallas kernels  11.7 us (31%)
  starting transfers between devices  11.2 us (30%)
  waiting for transfers between devices  9.57 us (26%)
  local copies, waits for them, and re-layouts  4.47 us (12%)
    ppermute x6, starting transfers between devices, hop(): return lax.ppermute(value, axes, pairs)  11.2 us
    ppermute x6, waiting for transfers between devices, hop(): return lax.ppermute(value, axes, pairs)  9.57 us
    pallas_call x1, Pallas kernels, per_device(): pl.pallas_call(functools.partial(post_kernel, chunks, blocks), out_shape=...  5.8 us
    unnamed x20, local copies, waits for them, and re-layouts  4.47 us
    pallas_call x1, Pallas kernels, per_device(): pl.pallas_call(functools.partial(gram_kernel, chunks, blocks), out_shape=...  3.1 us
    pallas_call x1, Pallas kernels, per_device(): ready = prep(tied[0], tied[1][None, :], tied[2], tied[3], phases)  2.2 us
  transfers between devices with their start and end apart: 6, of which 5 were waited for; matrix products, arithmetic and copies ran while one was open for 0% of the time, Pallas kernels for 8%

profile of v1, /device:TPU:0, one launch (start us, length us, event | category | flops | bytes accessed | tf_op | source)
XLA Modules:
  0.0 37.2 jit_solution(3049923150698222358)
XLA Ops:
  0.0 0.0 copy-start.1
  0.0 1.2 %copy-done.1 = bf16[64,8192]{1,0:T(8,128)(2,1)S(1)} copy-done((bf16[64,8192]{1,0:T(8,128)(2,1)S(1)}, bf16[64,8192]{1,0:T(8,128)(2,1)}, u32[]{:S(2)}) %copy-start.1) | copy-done | bytes 1048600
  1.2 0.0 copy-start.7
  1.2 0.8 %copy-done.7 = f32[8,8,128]{2,1,0:T(8,128)S(1)} copy-done((f32[8,8,128]{2,1,0:T(8,128)S(1)}, f32[8,8,128]{2,1,0:T(8,128)}, u32[]{:S(2)}) %copy-start.7) | copy-done | bytes 32792
  2.0 0.0 copy-start.4
  2.0 0.0 copy-start.5
  2.0 0.0 copy-start.6
  2.0 0.0 copy-start.8
  2.0 0.0 copy-start.9
  2.0 0.0 copy-start.2
  2.0 3.1 %gram.1 = (f32[112,128]{1,0:T(8,128)S(1)}, f32[112,128]{1,0:T(8,128)S(1)}) custom-call(bf16[64,8192]{1,0:T(8,128)(2,1)S(1)} %copy-done.1, bf16[2,8192,128]{2,1,0:T(8,128)(2,1)} %sol_hbm.1, f32[8,8,128]{2,1,0:T(8,128)S(1)} %copy-done.7), custom_call_target="tpu_custom_call" | custom-call | tf_op jit(solution)/shard_map/gram/pallas_call | solution.py:276
  5.1 0.5 %collective-permute-start = (f32[112,128]{1,0:T(8,128)S(1)}, f32[112,128]{1,0:T(8,128)S(1)}, u32[]{:S(2)}, u32[]{:S(2)}) collective-permute-start(f32[112,128]{1,0:T(8,128)S(1)} %get-tuple-element.25), channel_id=1, source_target_pairs={{0,8},{1,9},{2,10},{3,11},{4,12},{5,13},{6,14},{7,15},{8,0},{9,1},... | collective-permute-start | bytes 172040 | tf_op jit(solution)/shard_map/ppermute | solution.py:260
  5.6 0.9 %collective-permute-done = f32[112,128]{1,0:T(8,128)S(1)} collective-permute-done((f32[112,128]{1,0:T(8,128)S(1)}, f32[112,128]{1,0:T(8,128)S(1)}, u32[]{:S(2)}, u32[]{:S(2)}) %collective-permute-start) | collective-permute-done | bytes 57376 | tf_op jit(solution)/shard_map/ppermute | solution.py:260
  6.5 2.9 %collective-permute-start.1 = (f32[112,128]{1,0:T(8,128)S(1)}, f32[112,128]{1,0:T(8,128)S(1)}, u32[]{:S(2)}, u32[]{:S(2)}) collective-permute-start(f32[112,128]{1,0:T(8,128)S(1)} %add.15), channel_id=1, source_target_pairs={{0,16},{1,17},{2,18},{3,19},{4,20},{5,21},{6,22},{7,23},{8,24},{9,... | collective-permute-start | bytes 172040 | tf_op jit(solution)/shard_map/ppermute | solution.py:260
  9.4 2.2 %collective-permute-done.1 = f32[112,128]{1,0:T(8,128)S(1)} collective-permute-done((f32[112,128]{1,0:T(8,128)S(1)}, f32[112,128]{1,0:T(8,128)S(1)}, u32[]{:S(2)}, u32[]{:S(2)}) %collective-permute-start.1) | collective-permute-done | bytes 57376 | tf_op jit(solution)/shard_map/ppermute | solution.py:260
  11.7 2.1 %collective-permute-start.2 = (f32[112,128]{1,0:T(8,128)S(1)}, f32[112,128]{1,0:T(8,128)S(1)}, u32[]{:S(2)}, u32[]{:S(2)}) collective-permute-start(f32[112,128]{1,0:T(8,128)S(1)} %add.16), channel_id=1, source_target_pairs={{0,1},{1,0},{2,3},{3,2},{4,5},{5,4},{6,7},{7,6},{8,9},{9,8},{10,11... | collective-permute-start | bytes 172040 | tf_op jit(solution)/shard_map/ppermute | solution.py:260
  13.7 2.2 %collective-permute-done.2 = f32[112,128]{1,0:T(8,128)S(1)} collective-permute-done((f32[112,128]{1,0:T(8,128)S(1)}, f32[112,128]{1,0:T(8,128)S(1)}, u32[]{:S(2)}, u32[]{:S(2)}) %collective-permute-start.2) | collective-permute-done | bytes 57376 | tf_op jit(solution)/shard_map/ppermute | solution.py:260
  15.9 2.1 %collective-permute-start.3 = (f32[112,128]{1,0:T(8,128)S(1)}, f32[112,128]{1,0:T(8,128)S(1)}, u32[]{:S(2)}, u32[]{:S(2)}) collective-permute-start(f32[112,128]{1,0:T(8,128)S(1)} %add.17), channel_id=1, source_target_pairs={{0,2},{1,3},{2,0},{3,1},{4,6},{5,7},{6,4},{7,5},{8,10},{9,11},{10,... | collective-permute-start | bytes 172040 | tf_op jit(solution)/shard_map/ppermute | solution.py:260
  18.0 2.2 %collective-permute-done.3 = f32[112,128]{1,0:T(8,128)S(1)} collective-permute-done((f32[112,128]{1,0:T(8,128)S(1)}, f32[112,128]{1,0:T(8,128)S(1)}, u32[]{:S(2)}, u32[]{:S(2)}) %collective-permute-start.3) | collective-permute-done | bytes 57376 | tf_op jit(solution)/shard_map/ppermute | solution.py:260
  20.2 3.5 %collective-permute-start.4 = (f32[112,128]{1,0:T(8,128)S(1)}, f32[112,128]{1,0:T(8,128)S(1)}, u32[]{:S(2)}, u32[]{:S(2)}) collective-permute-start(f32[112,128]{1,0:T(8,128)S(1)} %add.18), channel_id=1, source_target_pairs={{0,4},{1,5},{2,6},{3,7},{4,0},{5,1},{6,2},{7,3},{8,12},{9,13},{10,... | collective-permute-start | bytes 172040 | tf_op jit(solution)/shard_map/ppermute | solution.py:260
  23.8 2.2 %collective-permute-done.4 = f32[112,128]{1,0:T(8,128)S(1)} collective-permute-done((f32[112,128]{1,0:T(8,128)S(1)}, f32[112,128]{1,0:T(8,128)S(1)}, u32[]{:S(2)}, u32[]{:S(2)}) %collective-permute-start.4) | collective-permute-done | bytes 57376 | tf_op jit(solution)/shard_map/ppermute | solution.py:260
  25.9 0.1 collective-permute-start.5
  26.0 0.0 copy-done.4
  26.0 0.0 copy-done.5
  26.0 0.0 copy-done.6
  26.0 0.0 copy-done.8
  26.0 0.0 copy-done.9
  26.1 2.2 %prep.1 = (bf16[256,768]{1,0:T(8,128)(2,1)S(1)}, bf16[768,256]{1,0:T(8,128)(2,1)S(1)}, bf16[768,256]{1,0:T(8,128)(2,1)S(1)}, bf16[256,768]{1,0:T(8,128)(2,1)S(1)...) custom-call(f32[256,256]{1,0:T(8,128)S(1)} %copy-done.4, ...), custom_call_target="tpu_custom_call" | custom-call | flops 100663296 | bytes 4194304 | tf_op jit(solution)/shard_map/prep/pallas_call | solution.py:328
  28.3 0.0 copy-done.2
  28.3 0.6 %turn.1.probe_t_ref = bf16[8192,64]{1,0:T(8,128)(2,1)S(1)} custom-call(bf16[64,8192]{1,0:T(8,128)(2,1)S(1)} %copy-done.2), custom_call_target="tpu_custom_call" | custom-call | bytes 6291456 | tf_op jit(solution)/shard_map/turn/pallas_call | solution.py:334
  28.9 0.0 copy-start
  28.9 1.3 %copy-done = bf16[8192,64]{1,0:T(8,128)(2,1)} copy-done((bf16[8192,64]{1,0:T(8,128)(2,1)}, bf16[8192,64]{1,0:T(8,128)(2,1)S(1)}, u32[]{:S(2)}) %copy-start) | copy-done | bytes 1048600
  30.2 0.0 collective-permute-done.5.got_ref
  30.2 0.0 copy-start.3
  30.2 1.1 %copy-done.3 = bf16[2,1536,128]{2,1,0:T(8,128)(2,1)S(1)} copy-done((bf16[2,1536,128]{2,1,0:T(8,128)(2,1)S(1)}, bf16[2,1536,128]{2,1,0:T(8,128)(2,1)}, u32[]{:S(2)}) %copy-start.3) | copy-done | bytes 786456
  31.4 5.8 %post.1 = bf16[2,8192,128]{2,1,0:T(8,128)(2,1)} custom-call(f32[112,128]{1,0:T(8,128)S(1)} %add.19.own_ref, f32[112,128]{1,0:T(8,128)S(1)} %collective-permute-done.5.got_ref, bf16[256,768]{1,0:T(8,128)(2,1)S(1)} %get-tuple-element.32.ut3_ref, bf16[768,256]{1,0:T(8,128)(2,1)S(1)} %get-tuple-element.33.w3_ref, ...), custom_call_target="tpu_custom_call" | custom-call | tf_op jit(solution)/shard_map/post/pallas_call | solution.py:337
  (5 shorter events, 0.0 us)
Async XLA Ops:
  0.0 1.2 %copy-start.1 = (bf16[64,8192]{1,0:T(8,128)(2,1)S(1)}, bf16[64,8192]{1,0:T(8,128)(2,1)}, u32[]{:S(2)}) copy-start(bf16[64,8192]{1,0:T(8,128)(2,1)} %probe_ref) | copy-start | bytes 3145732
  1.2 0.8 %copy-start.7 = (f32[8,8,128]{2,1,0:T(8,128)S(1)}, f32[8,8,128]{2,1,0:T(8,128)}, u32[]{:S(2)}) copy-start(f32[8,8,128]{2,1,0:T(8,128)} %constant.4.clone.table_ref) | copy-start | bytes 98308
  2.0 24.0 %copy-start.4 = (f32[256,256]{1,0:T(8,128)S(1)}, f32[256,256]{1,0:T(8,128)}, u32[]{:S(2)}) copy-start(f32[256,256]{1,0:T(8,128)} %left_ref) | copy-start | bytes 786436
  2.0 24.0 %copy-start.5 = (f32[256,256]{1,0:T(8,128)S(1)}, f32[256,256]{1,0:T(8,128)}, u32[]{:S(2)}) copy-start(f32[256,256]{1,0:T(8,128)} %right_ref) | copy-start | bytes 786436
  2.0 24.0 %copy-start.6 = (f32[256,256]{1,0:T(8,128)S(1)}, f32[256,256]{1,0:T(8,128)}, u32[]{:S(2)}) copy-start(f32[256,256]{1,0:T(8,128)} %adj_ref) | copy-start | bytes 786436
  2.0 24.0 %copy-start.8 = (f32[8,10]{1,0:T(8,128)S(1)}, f32[8,10]{1,0:T(8,128)}, u32[]{:S(2)}) copy-start(f32[8,10]{1,0:T(8,128)} %constant.5.clone.phase_ref) | copy-start | bytes 964
  2.0 24.1 %copy-start.9 = (f32[256]{0:T(256)S(1)}, f32[256]{0:T(256)}, u32[]{:S(2)}) copy-start(f32[256]{0:T(256)} %param.11) | copy-start | bytes 3076
  2.0 26.3 %copy-start.2 = (bf16[64,8192]{1,0:T(8,128)(2,1)S(1)}, bf16[64,8192]{1,0:T(8,128)(2,1)}, u32[]{:S(2)}) copy-start(bf16[64,8192]{1,0:T(8,128)(2,1)} %probe_ref) | copy-start | bytes 3145732
  5.1 1.4 %collective-permute-start = (f32[112,128]{1,0:T(8,128)S(1)}, f32[112,128]{1,0:T(8,128)S(1)}, u32[]{:S(2)}, u32[]{:S(2)}) collective-permute-start(f32[112,128]{1,0:T(8,128)S(1)} %get-tuple-element.25), channel_id=1, source_target_pairs={{0,8},{1,9},{2,10},{3,11},{4,12},{5,13},{6,14},{7,15},{8,0},{9,1},... | collective-permute-start | bytes 172040 | tf_op jit(solution)/shard_map/ppermute | solution.py:260
  6.5 5.1 %collective-permute-start.1 = (f32[112,128]{1,0:T(8,128)S(1)}, f32[112,128]{1,0:T(8,128)S(1)}, u32[]{:S(2)}, u32[]{:S(2)}) collective-permute-start(f32[112,128]{1,0:T(8,128)S(1)} %add.15), channel_id=1, source_target_pairs={{0,16},{1,17},{2,18},{3,19},{4,20},{5,21},{6,22},{7,23},{8,24},{9,... | collective-permute-start | bytes 172040 | tf_op jit(solution)/shard_map/ppermute | solution.py:260
  11.7 4.2 %collective-permute-start.2 = (f32[112,128]{1,0:T(8,128)S(1)}, f32[112,128]{1,0:T(8,128)S(1)}, u32[]{:S(2)}, u32[]{:S(2)}) collective-permute-start(f32[112,128]{1,0:T(8,128)S(1)} %add.16), channel_id=1, source_target_pairs={{0,1},{1,0},{2,3},{3,2},{4,5},{5,4},{6,7},{7,6},{8,9},{9,8},{10,11... | collective-permute-start | bytes 172040 | tf_op jit(solution)/shard_map/ppermute | solution.py:260
  15.9 4.3 %collective-permute-start.3 = (f32[112,128]{1,0:T(8,128)S(1)}, f32[112,128]{1,0:T(8,128)S(1)}, u32[]{:S(2)}, u32[]{:S(2)}) collective-permute-start(f32[112,128]{1,0:T(8,128)S(1)} %add.17), channel_id=1, source_target_pairs={{0,2},{1,3},{2,0},{3,1},{4,6},{5,7},{6,4},{7,5},{8,10},{9,11},{10,... | collective-permute-start | bytes 172040 | tf_op jit(solution)/shard_map/ppermute | solution.py:260
  20.2 5.7 %collective-permute-start.4 = (f32[112,128]{1,0:T(8,128)S(1)}, f32[112,128]{1,0:T(8,128)S(1)}, u32[]{:S(2)}, u32[]{:S(2)}) collective-permute-start(f32[112,128]{1,0:T(8,128)S(1)} %add.18), channel_id=1, source_target_pairs={{0,4},{1,5},{2,6},{3,7},{4,0},{5,1},{6,2},{7,3},{8,12},{9,13},{10,... | collective-permute-start | bytes 172040 | tf_op jit(solution)/shard_map/ppermute | solution.py:260
  25.9 4.3 %collective-permute-start.5 = (f32[112,128]{1,0:T(8,128)S(1)}, f32[112,128]{1,0:T(8,128)S(1)}, u32[]{:S(2)}, u32[]{:S(2)}) collective-permute-start(f32[112,128]{1,0:T(8,128)S(1)} %add.19.own_ref), channel_id=1, source_target_pairs={{0,8},{1,9},{2,10},{3,11},{4,12},{5,13},{6,14},{7,15},{8,0},{9,1},... | collective-permute-start | bytes 172040 | tf_op jit(solution)/shard_map/ppermute | solution.py:260
  28.9 1.3 %copy-start = (bf16[8192,64]{1,0:T(8,128)(2,1)}, bf16[8192,64]{1,0:T(8,128)(2,1)S(1)}, u32[]{:S(2)}) copy-start(bf16[8192,64]{1,0:T(8,128)(2,1)S(1)} %turn.1.probe_t_ref) | copy-start | bytes 3145732
  30.2 1.1 %copy-start.3 = (bf16[2,1536,128]{2,1,0:T(8,128)(2,1)S(1)}, bf16[2,1536,128]{2,1,0:T(8,128)(2,1)}, u32[]{:S(2)}) copy-start(bf16[2,1536,128]{2,1,0:T(8,128)(2,1)} %get-tuple-element.40.wc3_ref) | copy-start | bytes 2359300

commit v2 on v1

--- a/solution.py
+++ b/solution.py
@@ -11,7 +11,6 @@
 
 F32 = jnp.float32
 BF16 = jnp.bfloat16
-VMEM_BYTES = 50 * 1024 * 1024
 
 
 def dot(first, second):
@@ -54,35 +53,40 @@
     return np.concatenate([np.cos(half), -np.sin(half)], axis=1).astype(np.float32)
 
 
-def gram_kernel(chunks, blocks, probe_hbm, sol_hbm, table_ref, keep_ref, send_ref, pbuf, sbuf, psem, ssem):
+def gram_kernel(
+    sizes, blocks, probe_hbm, sol_hbm, table_hbm, keep_ref, send_ref, pbuf, sbuf, table, psem, ssem, tsem
+):
     count, local, width2 = sbuf.shape
     width = width2 // 2
-    size = local // chunks
     me = lax.axis_index("pts")
+    starts = [sum(sizes[:c]) for c in range(len(sizes))]
 
     def copies(c):
-        at = pl.ds(c * size, size)
+        at = pl.ds(starts[c], sizes[c])
         return (
             pltpu.make_async_copy(probe_hbm.at[:, at], pbuf.at[:, at], psem.at[c]),
             pltpu.make_async_copy(sol_hbm.at[:, at, :], sbuf.at[:, at, :], ssem.at[c]),
         )
 
-    for c in range(chunks):
+    for c in range(len(sizes)):
         for copy in copies(c):
             copy.start()
+    fetch = pltpu.make_async_copy(table_hbm.at[pl.ds(me * count, count)], table, tsem)
+    fetch.start()
     gram = None
-    for c in range(chunks):
+    for c in range(len(sizes)):
         for copy in copies(c):
             copy.wait()
-        at = pl.ds(c * size, size)
+        at = pl.ds(starts[c], sizes[c])
         side = jnp.concatenate([sbuf[p, at, :] for p in range(count)], axis=1)
         part = dot(pbuf[:, at], side)
         gram = part if gram is None else gram + part
+    fetch.wait()
     tiles = [None] * blocks
     for p in range(count):
         straight = gram[:, p * width2 : (p + 1) * width2]
         turned = pltpu.roll(straight, width, 1)
-        coef = table_ref[me * count + p]
+        coef = table[p]
         for a in range(blocks):
             term = straight * coef[a : a + 1] + turned * coef[blocks + a : blocks + a + 1]
             tiles[a] = term if tiles[a] is None else tiles[a] + term
@@ -106,6 +110,7 @@
     right_ref,
     adj_ref,
     phase_ref,
+    _,
     ut3_ref,
     w3_ref,
     zt3_ref,
@@ -163,7 +168,14 @@
     y2_ref[...] = dot(left3(jnp.concatenate(up2, axis=0)), right3(zbar))
 
 
-def turn_kernel(probe_ref, out_ref):
+def sum_kernel(terms, *refs):
+    total = refs[0][...]
+    for ref in refs[1:terms]:
+        total = total + ref[...]
+    refs[-1][...] = total
+
+
+def turn_kernel(probe_ref, _, out_ref):
     out_ref[...] = probe_ref[...].T
 
 
@@ -267,26 +279,31 @@
     blocks = order // width
     total = count * n_pts
     rows = (blocks - 1) * (width // 2) + width // 4
-    chunks = 8 if local % 1024 == 0 else 1
+    unit = local // 16
+    sizes = [unit, unit] + [2 * unit] * 6 + [unit, unit]
+    chunks = 8
     anyspace = pl.BlockSpec(memory_space=pl.ANY)
     vmem = pl.BlockSpec(memory_space=pltpu.VMEM)
     smem = pl.BlockSpec(memory_space=pltpu.SMEM)
-    params = pltpu.CompilerParams(vmem_limit_bytes=VMEM_BYTES)
+    params = pltpu.CompilerParams(vmem_limit_bytes=20 << 20)
+    in_hbm = functools.partial(pltpu.with_memory_space_constraint, memory_space=pltpu.HBM)
     half = jax.ShapeDtypeStruct((rows, width2), F32)
     keep, send = pl.pallas_call(
-        functools.partial(gram_kernel, chunks, blocks),
+        functools.partial(gram_kernel, sizes, blocks),
         out_shape=(half, half),
-        in_specs=[anyspace, anyspace, vmem],
+        in_specs=[anyspace] * 3,
         out_specs=(vmem, vmem),
         scratch_shapes=[
             pltpu.VMEM((width, local), BF16),
             pltpu.VMEM((count, local, width2), BF16),
-            pltpu.SemaphoreType.DMA((chunks,)),
-            pltpu.SemaphoreType.DMA((chunks,)),
+            pltpu.VMEM((count, 2 * blocks, width2), F32),
+            pltpu.SemaphoreType.DMA((len(sizes),)),
+            pltpu.SemaphoreType.DMA((len(sizes),)),
+            pltpu.SemaphoreType.DMA,
         ],
         compiler_params=params,
         name="gram",
-    )(probe, solutions, jnp.asarray(moment_table(total, blocks, width)))
+    )(*(in_hbm(v) for v in (probe, solutions, jnp.asarray(moment_table(total, blocks, width)))))
 
     square = jax.ShapeDtypeStruct((order, order), F32)
     tall = jax.ShapeDtypeStruct((3 * order, order), BF16)
@@ -306,7 +323,7 @@
             jax.ShapeDtypeStruct((count, 6 * order, width2), BF16),
             jax.ShapeDtypeStruct((2 * count * width, order), F32),
         ),
-        in_specs=[vmem, vmem, vmem, vmem, smem],
+        in_specs=[vmem, vmem, vmem, vmem, smem, anyspace],
         out_specs=(vmem,) * 10,
         compiler_params=params,
         cost_estimate=pl.CostEstimate(flops=6 * order**3, bytes_accessed=4 << 20, transcendentals=0),
@@ -315,25 +332,43 @@
     turn = pl.pallas_call(
         turn_kernel,
         out_shape=jax.ShapeDtypeStruct((local, width), BF16),
-        in_specs=[vmem],
+        in_specs=[vmem, anyspace],
         out_specs=vmem,
         compiler_params=params,
         cost_estimate=pl.CostEstimate(flops=0, bytes_accessed=6 << 20, transcendentals=0),
         name="turn",
     )
-    axes, sizes = ("pts", "rows"), (n_pts, n_rows)
-    value = keep + hop(send, axes, sizes, (1, 0))
-    phases = jnp.asarray(phase_table(total, blocks))
-    value, tied = lax.optimization_barrier((value, (left_factor, singular, right_factor, adjoint)))
-    ready = prep(tied[0], tied[1][None, :], tied[2], tied[3], phases)
-    hops = [(1 << k, 0) for k in range(1, n_pts.bit_length() - 1)]
-    hops += [(0, 1 << k) for k in range(n_rows.bit_length() - 1)]
-    for at, bits in enumerate(hops):
-        if at == len(hops) - 2:
-            value, probe = lax.optimization_barrier((value, probe))
-            probe_t = turn(probe)
-        value = value + hop(value, axes, sizes, bits)
-    other = hop(value, axes, sizes, (1, 0))
+    axes, sizes_of = ("pts", "rows"), (n_pts, n_rows)
+    def add(terms, after):
+        return pl.pallas_call(
+            functools.partial(sum_kernel, len(terms)),
+            out_shape=half,
+            in_specs=[vmem] * len(terms) + [anyspace] * len(after),
+            out_specs=vmem,
+            compiler_params=params,
+            name="sum",
+        )(*terms, *after)
+
+    value = add([keep, hop(send, axes, sizes_of, (1, 0))], [])
+    ready = prep(
+        left_factor, singular[None, :], right_factor, adjoint, jnp.asarray(phase_table(total, blocks)), value
+    )
+    bits = [(1 << k, 0) for k in range(1, n_pts.bit_length() - 1)]
+    bits += [(0, 1 << k) for k in range(n_rows.bit_length() - 1)]
+    for at in range(0, len(bits), 2):
+        step = [tuple(bit) for bit in bits[at : at + 2]]
+        if len(step) == 2:
+            step.append(tuple(p ^ q for p, q in zip(*step)))
+        got = [hop(value, axes, sizes_of, bit) for bit in step]
+        if at == 0:
+            after = ready
+        elif at == 2:
+            probe_t = turn(probe, value)
+            after = [probe_t]
+        else:
+            after = []
+        value = add([value] + got, after)
+    other = hop(value, axes, sizes_of, (1, 0))
     return pl.pallas_call(
         functools.partial(post_kernel, chunks, blocks),
         out_shape=jax.ShapeDtypeStruct((count, local, width2), BF16),

time: 37.5 us -> 27.6 us (0.74)
  local copies, waits for them, and re-layouts: 4.47 us -> 0.02 us
  Pallas kernels: 11.7 us -> 9.41 us
  starting transfers between devices: 11.2 us -> 9.56 us
  waiting for transfers between devices: 9.57 us -> 8.44 us
    unnamed x20 -> x12, local copies, waits for them, and re-layouts: 4.47 us -> 0.02 us
    ppermute x6 -> x8, starting transfers between devices: 11.2 us -> 9.56 us  [hop(): return lax.ppermute(value, axes, pairs)]
    pallas_call x1, Pallas kernels: 5.8 us -> 4.21 us  [per_device(): pl.pallas_call(functools.partial(post_kernel, chunks, blocks), out_shape=...]
    ppermute x6 -> x8, waiting for transfers between devices: 9.57 us -> 8.44 us  [hop(): return lax.ppermute(value, axes, pairs)]
    pallas_call x3 -> x6, Pallas kernels: 5.93 us -> 5.2 us  [the longest x1 3.18 us: per_device(): pl.pallas_call(functools.partial(gram_kernel, sizes, blocks), out_shape=(...]
  transfers between devices with their start and end apart: 6 -> 8, of which waited for: 5 -> 7; matrix products, arithmetic and copies ran while one was open for 0% -> 0% of each run, Pallas kernels for 8% -> 7%
where the time goes in v2:
time: 27.6 us; the launch traced here: 27.5 us
  starting transfers between devices  9.56 us (35%)
  Pallas kernels  9.41 us (34%)
  waiting for transfers between devices  8.44 us (31%)
    ppermute x8, starting transfers between devices, hop(): return lax.ppermute(value, axes, pairs)  9.56 us
    ppermute x8, waiting for transfers between devices, hop(): return lax.ppermute(value, axes, pairs)  8.44 us
    pallas_call x1, Pallas kernels, per_device(): pl.pallas_call(functools.partial(post_kernel, chunks, blocks), out_shape=...  4.21 us
    pallas_call x1, Pallas kernels, per_device(): pl.pallas_call(functools.partial(gram_kernel, sizes, blocks), out_shape=(...  3.18 us
    pallas_call x1, Pallas kernels, per_device(): prep(left_factor, singular[None, :], right_factor, adjoint, jnp.asarray(p...  1.35 us
    pallas_call x1, Pallas kernels, per_device(): probe_t = turn(probe, value)  0.63 us
  transfers between devices with their start and end apart: 8, of which 7 were waited for; matrix products, arithmetic and copies ran while one was open for 0% of the time, Pallas kernels for 7%

profile of v2, /device:TPU:0, one launch (start us, length us, event | category | flops | bytes accessed | tf_op | source)
XLA Modules:
  0.0 27.5 jit_solution(8015860274170535369)
XLA Ops:
  0.0 0.0 copy-start.4
  0.0 0.0 copy-start
  0.0 0.0 copy-start.3
  0.0 0.0 copy-start.2
  0.0 0.0 copy-start.5
  0.0 0.0 copy-start.1
  0.0 3.2 %gram.1 = (f32[112,128]{1,0:T(8,128)S(1)}, f32[112,128]{1,0:T(8,128)S(1)}) custom-call(bf16[64,8192]{1,0:T(8,128)(2,1)} %probe_ref.1, bf16[2,8192,128]{2,1,0:T(8,128)(2,1)} %sol_hbm.1, f32[8,8,128]{2,1,0:T(8,128)} %constant.4.clone.table_hbm), custom_call_target="tpu_custom_call" | custom-call | tf_op jit(solution)/shard_map/gram/pallas_call | solution.py:291
  3.2 0.5 %collective-permute-start = (f32[112,128]{1,0:T(8,128)S(1)}, f32[112,128]{1,0:T(8,128)S(1)}, u32[]{:S(2)}, u32[]{:S(2)}) collective-permute-start(f32[112,128]{1,0:T(8,128)S(1)} %get-tuple-element.18), channel_id=1, source_target_pairs={{0,8},{1,9},{2,10},{3,11},{4,12},{5,13},{6,14},{7,15},{8,0},{9,1},... | collective-permute-start | bytes 172040 | tf_op jit(solution)/shard_map/ppermute | solution.py:272
  3.7 0.9 %collective-permute-done.refs_1_ = f32[112,128]{1,0:T(8,128)S(1)} collective-permute-done((f32[112,128]{1,0:T(8,128)S(1)}, f32[112,128]{1,0:T(8,128)S(1)}, u32[]{:S(2)}, u32[]{:S(2)}) %collective-permute-start) | collective-permute-done | bytes 57376 | tf_op jit(solution)/shard_map/ppermute | solution.py:272
  4.6 3.9 %collective-permute-start.3 = (f32[112,128]{1,0:T(8,128)S(1)}, f32[112,128]{1,0:T(8,128)S(1)}, u32[]{:S(2)}, u32[]{:S(2)}) collective-permute-start(f32[112,128]{1,0:T(8,128)S(1)} %sum.3._.refs_0_), channel_id=1, source_target_pairs={{0,17},{1,16},{2,19},{3,18},{4,21},{5,20},{6,23},{7,22},{8,25},{9,... | collective-permute-start | bytes 172040 | tf_op jit(solution)/shard_map/ppermute | solution.py:272
  8.5 0.5 %collective-permute-start.2 = (f32[112,128]{1,0:T(8,128)S(1)}, f32[112,128]{1,0:T(8,128)S(1)}, u32[]{:S(2)}, u32[]{:S(2)}) collective-permute-start(f32[112,128]{1,0:T(8,128)S(1)} %sum.3._.refs_0_), channel_id=1, source_target_pairs={{0,1},{1,0},{2,3},{3,2},{4,5},{5,4},{6,7},{7,6},{8,9},{9,8},{10,11... | collective-permute-start | bytes 172040 | tf_op jit(solution)/shard_map/ppermute | solution.py:272
  9.0 0.1 collective-permute-start.1
  9.1 0.0 copy-done.4
  9.1 0.0 copy-done.3
  9.2 0.0 copy-done.2
  9.2 0.0 copy-done.5
  9.2 0.0 copy-done.1
  9.2 1.3 %prep.1 = (bf16[256,768]{1,0:T(8,128)(2,1)S(1)}, bf16[768,256]{1,0:T(8,128)(2,1)S(1)}, bf16[768,256]{1,0:T(8,128)(2,1)S(1)}, bf16[256,768]{1,0:T(8,128)(2,1)S(1)...) custom-call(f32[256,256]{1,0:T(8,128)S(1)} %copy-done.1, ...), custom_call_target="tpu_custom_call" | custom-call | flops 100663296 | bytes 4194304 | tf_op jit(solution)/shard_map/prep/pallas_call | solution.py:353
  10.5 0.2 collective-permute-done.3.refs_3_
  10.7 2.0 %collective-permute-done.2.refs_2_ = f32[112,128]{1,0:T(8,128)S(1)} collective-permute-done((f32[112,128]{1,0:T(8,128)S(1)}, f32[112,128]{1,0:T(8,128)S(1)}, u32[]{:S(2)}, u32[]{:S(2)}) %collective-permute-start.2) | collective-permute-done | bytes 57376 | tf_op jit(solution)/shard_map/ppermute | solution.py:272
  12.7 0.5 %collective-permute-done.1.refs_1_ = f32[112,128]{1,0:T(8,128)S(1)} collective-permute-done((f32[112,128]{1,0:T(8,128)S(1)}, f32[112,128]{1,0:T(8,128)S(1)}, u32[]{:S(2)}, u32[]{:S(2)}) %collective-permute-start.1) | collective-permute-done | bytes 57376 | tf_op jit(solution)/shard_map/ppermute | solution.py:272
  13.2 3.7 %collective-permute-start.6 = (f32[112,128]{1,0:T(8,128)S(1)}, f32[112,128]{1,0:T(8,128)S(1)}, u32[]{:S(2)}, u32[]{:S(2)}) collective-permute-start(f32[112,128]{1,0:T(8,128)S(1)} %sum.4._.refs_0_), channel_id=1, source_target_pairs={{0,6},{1,7},{2,4},{3,5},{4,2},{5,3},{6,0},{7,1},{8,14},{9,15},{10,... | collective-permute-start | bytes 172040 | tf_op jit(solution)/shard_map/ppermute | solution.py:272
  16.9 0.0 collective-permute-start.5
  16.9 0.8 %collective-permute-start.4 = (f32[112,128]{1,0:T(8,128)S(1)}, f32[112,128]{1,0:T(8,128)S(1)}, u32[]{:S(2)}, u32[]{:S(2)}) collective-permute-start(f32[112,128]{1,0:T(8,128)S(1)} %sum.4._.refs_0_), channel_id=1, source_target_pairs={{0,2},{1,3},{2,0},{3,1},{4,6},{5,7},{6,4},{7,5},{8,10},{9,11},{10,... | collective-permute-start | bytes 172040 | tf_op jit(solution)/shard_map/ppermute | solution.py:272
  17.7 0.0 copy-done
  17.7 0.6 %turn.1.refs_4_.probe_t_ref = bf16[8192,64]{1,0:T(8,128)(2,1)S(1)} custom-call(bf16[64,8192]{1,0:T(8,128)(2,1)S(1)} %copy-done, f32[112,128]{1,0:T(8,128)S(1)} %sum.4._.refs_0_), custom_call_target="tpu_custom_call" | custom-call | bytes 6291456 | tf_op jit(solution)/shard_map/turn/pallas_call | solution.py:366
  18.3 1.1 %collective-permute-done.6.refs_3_ = f32[112,128]{1,0:T(8,128)S(1)} collective-permute-done((f32[112,128]{1,0:T(8,128)S(1)}, f32[112,128]{1,0:T(8,128)S(1)}, u32[]{:S(2)}, u32[]{:S(2)}) %collective-permute-start.6) | collective-permute-done | bytes 57376 | tf_op jit(solution)/shard_map/ppermute | solution.py:272
  19.3 2.6 %collective-permute-done.5.refs_2_ = f32[112,128]{1,0:T(8,128)S(1)} collective-permute-done((f32[112,128]{1,0:T(8,128)S(1)}, f32[112,128]{1,0:T(8,128)S(1)}, u32[]{:S(2)}, u32[]{:S(2)}) %collective-permute-start.5) | collective-permute-done | bytes 57376 | tf_op jit(solution)/shard_map/ppermute | solution.py:272
  22.0 0.0 collective-permute-done.4.refs_1_
  22.0 0.1 collective-permute-start.7
  22.1 1.2 %collective-permute-done.7.got_ref = f32[112,128]{1,0:T(8,128)S(1)} collective-permute-done((f32[112,128]{1,0:T(8,128)S(1)}, f32[112,128]{1,0:T(8,128)S(1)}, u32[]{:S(2)}, u32[]{:S(2)}) %collective-permute-start.7) | collective-permute-done | bytes 57376 | tf_op jit(solution)/shard_map/ppermute | solution.py:272
  23.3 4.2 %post.1 = bf16[2,8192,128]{2,1,0:T(8,128)(2,1)} custom-call(f32[112,128]{1,0:T(8,128)S(1)} %sum.5.own_ref, f32[112,128]{1,0:T(8,128)S(1)} %collective-permute-done.7.got_ref, bf16[256,768]{1,0:T(8,128)(2,1)S(1)} %get-tuple-element.19.refs_4_.ut3_ref, bf16[768,256]{1,0:T(8,128)(2,1)S(1)} %get-tuple-element.20.refs_5_.w3_ref, ...), custom_call_target="tpu_custom_call" | custom-call | tf_op jit(solution)/shard_map/post/pallas_call | solution.py:372
  (3 shorter events, 0.0 us)
Async XLA Ops:
  0.0 9.1 %copy-start.4 = (f32[8,10]{1,0:T(8,128)S(1)}, f32[8,10]{1,0:T(8,128)}, u32[]{:S(2)}) copy-start(f32[8,10]{1,0:T(8,128)} %constant.5.clone.phase_ref) | copy-start | bytes 964
  0.0 17.7 %copy-start = (bf16[64,8192]{1,0:T(8,128)(2,1)S(1)}, bf16[64,8192]{1,0:T(8,128)(2,1)}, u32[]{:S(2)}) copy-start(bf16[64,8192]{1,0:T(8,128)(2,1)} %probe_ref.1) | copy-start | bytes 3145732
  0.0 9.1 %copy-start.3 = (f32[256,256]{1,0:T(8,128)S(1)}, f32[256,256]{1,0:T(8,128)}, u32[]{:S(2)}) copy-start(f32[256,256]{1,0:T(8,128)} %adj_ref.1) | copy-start | bytes 786436
  0.0 9.1 %copy-start.2 = (f32[256,256]{1,0:T(8,128)S(1)}, f32[256,256]{1,0:T(8,128)}, u32[]{:S(2)}) copy-start(f32[256,256]{1,0:T(8,128)} %right_ref.1) | copy-start | bytes 786436
  0.0 9.1 %copy-start.5 = (f32[256]{0:T(256)S(1)}, f32[256]{0:T(256)}, u32[]{:S(2)}) copy-start(f32[256]{0:T(256)} %param.11) | copy-start | bytes 3076
  0.0 9.1 %copy-start.1 = (f32[256,256]{1,0:T(8,128)S(1)}, f32[256,256]{1,0:T(8,128)}, u32[]{:S(2)}) copy-start(f32[256,256]{1,0:T(8,128)} %left_ref.1) | copy-start | bytes 786436
  3.2 1.4 %collective-permute-start = (f32[112,128]{1,0:T(8,128)S(1)}, f32[112,128]{1,0:T(8,128)S(1)}, u32[]{:S(2)}, u32[]{:S(2)}) collective-permute-start(f32[112,128]{1,0:T(8,128)S(1)} %get-tuple-element.18), channel_id=1, source_target_pairs={{0,8},{1,9},{2,10},{3,11},{4,12},{5,13},{6,14},{7,15},{8,0},{9,1},... | collective-permute-start | bytes 172040 | tf_op jit(solution)/shard_map/ppermute | solution.py:272
  4.6 6.1 %collective-permute-start.3 = (f32[112,128]{1,0:T(8,128)S(1)}, f32[112,128]{1,0:T(8,128)S(1)}, u32[]{:S(2)}, u32[]{:S(2)}) collective-permute-start(f32[112,128]{1,0:T(8,128)S(1)} %sum.3._.refs_0_), channel_id=1, source_target_pairs={{0,17},{1,16},{2,19},{3,18},{4,21},{5,20},{6,23},{7,22},{8,25},{9,... | collective-permute-start | bytes 172040 | tf_op jit(solution)/shard_map/ppermute | solution.py:272
  8.5 4.2 %collective-permute-start.2 = (f32[112,128]{1,0:T(8,128)S(1)}, f32[112,128]{1,0:T(8,128)S(1)}, u32[]{:S(2)}, u32[]{:S(2)}) collective-permute-start(f32[112,128]{1,0:T(8,128)S(1)} %sum.3._.refs_0_), channel_id=1, source_target_pairs={{0,1},{1,0},{2,3},{3,2},{4,5},{5,4},{6,7},{7,6},{8,9},{9,8},{10,11... | collective-permute-start | bytes 172040 | tf_op jit(solution)/shard_map/ppermute | solution.py:272
  9.0 4.2 %collective-permute-start.1 = (f32[112,128]{1,0:T(8,128)S(1)}, f32[112,128]{1,0:T(8,128)S(1)}, u32[]{:S(2)}, u32[]{:S(2)}) collective-permute-start(f32[112,128]{1,0:T(8,128)S(1)} %sum.3._.refs_0_), channel_id=1, source_target_pairs={{0,16},{1,17},{2,18},{3,19},{4,20},{5,21},{6,22},{7,23},{8,24},{9,... | collective-permute-start | bytes 172040 | tf_op jit(solution)/shard_map/ppermute | solution.py:272
  13.2 6.1 %collective-permute-start.6 = (f32[112,128]{1,0:T(8,128)S(1)}, f32[112,128]{1,0:T(8,128)S(1)}, u32[]{:S(2)}, u32[]{:S(2)}) collective-permute-start(f32[112,128]{1,0:T(8,128)S(1)} %sum.4._.refs_0_), channel_id=1, source_target_pairs={{0,6},{1,7},{2,4},{3,5},{4,2},{5,3},{6,0},{7,1},{8,14},{9,15},{10,... | collective-permute-start | bytes 172040 | tf_op jit(solution)/shard_map/ppermute | solution.py:272
  16.9 5.1 %collective-permute-start.5 = (f32[112,128]{1,0:T(8,128)S(1)}, f32[112,128]{1,0:T(8,128)S(1)}, u32[]{:S(2)}, u32[]{:S(2)}) collective-permute-start(f32[112,128]{1,0:T(8,128)S(1)} %sum.4._.refs_0_), channel_id=1, source_target_pairs={{0,4},{1,5},{2,6},{3,7},{4,0},{5,1},{6,2},{7,3},{8,12},{9,13},{10,... | collective-permute-start | bytes 172040 | tf_op jit(solution)/shard_map/ppermute | solution.py:272
  16.9 5.1 %collective-permute-start.4 = (f32[112,128]{1,0:T(8,128)S(1)}, f32[112,128]{1,0:T(8,128)S(1)}, u32[]{:S(2)}, u32[]{:S(2)}) collective-permute-start(f32[112,128]{1,0:T(8,128)S(1)} %sum.4._.refs_0_), channel_id=1, source_target_pairs={{0,2},{1,3},{2,0},{3,1},{4,6},{5,7},{6,4},{7,5},{8,10},{9,11},{10,... | collective-permute-start | bytes 172040 | tf_op jit(solution)/shard_map/ppermute | solution.py:272
  22.0 1.3 %collective-permute-start.7 = (f32[112,128]{1,0:T(8,128)S(1)}, f32[112,128]{1,0:T(8,128)S(1)}, u32[]{:S(2)}, u32[]{:S(2)}) collective-permute-start(f32[112,128]{1,0:T(8,128)S(1)} %sum.5.own_ref), channel_id=1, source_target_pairs={{0,8},{1,9},{2,10},{3,11},{4,12},{5,13},{6,14},{7,15},{8,0},{9,1},... | collective-permute-start | bytes 172040 | tf_op jit(solution)/shard_map/ppermute | solution.py:272

commit v3 on v2

v3 whole, which is shorter than its diff:
```python
import functools
import math

import jax
import jax.numpy as jnp
import numpy as np
from jax import lax
from jax.experimental import pallas as pl
from jax.experimental.pallas import tpu as pltpu
from jax.sharding import PartitionSpec as P

F32 = jnp.float32
BF16 = jnp.bfloat16


def dot(first, second):
    return jnp.dot(first, second, preferred_element_type=F32)


def split(value):
    high = value.astype(BF16)
    return high, (value - high.astype(F32)).astype(BF16)


def left3(value):
    high, low = split(value)
    return jnp.concatenate([high, high, low], axis=1)


def right3(value):
    high, low = split(value)
    return jnp.concatenate([high, low, high], axis=0)


def moment_table(total, blocks, width):
    theta = math.pi * (np.arange(total) + 0.5) / total
    table = np.zeros((total, 2 * blocks, 2 * width), np.float32)
    for a in range(blocks):
        left = 2 * a + 2
        right = left + 1 if a < blocks - 1 else left
        cos_l, sin_l = np.cos(left * theta) / total, np.sin(left * theta) / total
        cos_r, sin_r = np.cos(right * theta) / total, np.sin(right * theta) / total
        table[:, a, :width] = cos_l[:, None]
        table[:, a, width:] = -sin_r[:, None]
        table[:, blocks + a, :width] = -sin_l[:, None]
        table[:, blocks + a, width:] = cos_r[:, None]
    return table


def phase_table(total, blocks):
    theta = math.pi * (np.arange(total)[:, None] + 0.5) / total
    half = theta * (np.arange(blocks + 1)[None, :] + 0.5)
    return np.concatenate([np.cos(half), -np.sin(half)], axis=1).astype(np.float32)


def gram_kernel(sizes, probe_hbm, sol_hbm, out_ref, pbuf, sbuf, psem, ssem):
    count = sbuf.shape[0]
    starts = [sum(sizes[:c]) for c in range(len(sizes))]

    def copies(c):
        at = pl.ds(starts[c], sizes[c])
        return (
            pltpu.make_async_copy(probe_hbm.at[:, at], pbuf.at[:, at], psem.at[c]),
            pltpu.make_async_copy(sol_hbm.at[:, at, :], sbuf.at[:, at, :], ssem.at[c]),
        )

    for c in range(len(sizes)):
        for copy in copies(c):
            copy.start()
    gram = None
    for c in range(len(sizes)):
        for copy in copies(c):
            copy.wait()
        at = pl.ds(starts[c], sizes[c])
        side = jnp.concatenate([sbuf[p, at, :] for p in range(count)], axis=1)
        part = dot(pbuf[:, at], side)
        gram = part if gram is None else gram + part
    out_ref[...] = gram


def prep_kernel(
    count,
    blocks,
    left_ref,
    sing_ref,
    right_ref,
    adj_ref,
    phase_ref,
    _,
    ut3_ref,
    w3_ref,
    zt3_ref,
    zl3_ref,
    f1_ref,
    f2_ref,
    dg_ref,
    up3_ref,
    wc3_ref,
    y2_ref,
):
    me = lax.axis_index("pts")
    order = left_ref.shape[0]
    width = order // blocks
    left = left_ref[...]
    right = right_ref[...]
    sing = sing_ref[...]
    zbar = adj_ref[...] / sing
    ut3_ref[...] = left3(left.T)
    w3_ref[...] = right3(right)
    zbar_t = zbar.T
    zt3_ref[...] = right3(zbar_t)
    zl3_ref[...] = left3(zbar_t)
    by_column = jnp.broadcast_to(sing, (order, order))
    by_row = by_column.T
    row = lax.broadcasted_iota(jnp.int32, (order, order), 0)
    column = lax.broadcasted_iota(jnp.int32, (order, order), 1)
    eye = row == column
    recip = jnp.where(
        eye, 0.0, 1.0 / jnp.where(eye, 1.0, by_column * by_column - by_row * by_row)
    )
    f1_ref[...] = recip * by_column
    f2_ref[...] = recip * by_row
    dg_ref[...] = jnp.where(eye, -1.0 / by_column, 0.0)
    total = phase_ref.shape[0]
    up, up2 = [], []
    for p in range(count):
        def turn(source, by, sine):
            out = None
            for i in range(blocks):
                term = source[i * width : (i + 1) * width] * phase_ref[
                    me * count + p, sine * (blocks + 1) + by + i
                ]
                out = term if out is None else out + term
            return out

        up += [turn(left, 0, 0) * (1.0 / total), turn(left, 0, 1) * (1.0 / total)]
        up2 += [turn(left, 1, 0) * (1.0 / total), turn(left, 1, 1) * (1.0 / total)]
        wre, wim = turn(right, 0, 0).T, turn(right, 0, 1).T
        wc = jnp.concatenate(
            [jnp.concatenate([wre, wim], axis=1), jnp.concatenate([-wim, wre], axis=1)], axis=0
        )
        wc3_ref[p] = right3(wc)
    up3_ref[...] = left3(jnp.concatenate(up, axis=0))
    y2_ref[...] = dot(left3(jnp.concatenate(up2, axis=0)), right3(zbar))


def sum_kernel(terms, *refs):
    total = refs[0][...]
    for ref in refs[1:terms]:
        total = total + ref[...]
    refs[-1][...] = total


def turn_kernel(probe_ref, _, out_ref):
    out_ref[...] = probe_ref[...].T


def hankel_of(grams, places, blocks, table_ref):
    width2 = table_ref.shape[2]
    width = width2 // 2
    tiles = [None] * blocks
    for gram, place in zip(grams, places):
        count = gram.shape[1] // width2
        for p in range(count):
            straight = gram[:, p * width2 : (p + 1) * width2]
            turned = pltpu.roll(straight, width, 1)
            coef = table_ref[place * count + p]
            for a in range(blocks):
                term = straight * coef[a : a + 1] + turned * coef[blocks + a : blocks + a + 1]
                tiles[a] = term if tiles[a] is None else tiles[a] + term
    lane = lax.broadcasted_iota(jnp.int32, (width, width2), 1)
    turned = [pltpu.roll(tile, width, 1) for tile in tiles[:-1]] + [tiles[-1]]
    between = [jnp.where(lane < width, turned[a], turned[a + 1]) for a in range(blocks - 1)]
    every = [tile for pair in zip(tiles, between) for tile in pair]
    return jnp.concatenate(
        [
            jnp.concatenate([every[i + j] for j in range(0, blocks, 2)], axis=1)
            for i in range(blocks)
        ],
        axis=0,
    )


def post_kernel(
    sizes,
    blocks,
    masks,
    table_ref,
    ut3_ref,
    w3_ref,
    zt3_ref,
    zl3_ref,
    f1_ref,
    f2_ref,
    dg_ref,
    up3_ref,
    wc3_ref,
    y2_ref,
    probe_t_ref,
    *refs,
):
    gram_refs, (out_hbm, obuf, osem) = refs[: len(masks)], refs[len(masks) :]
    count, _, width2 = obuf.shape
    width = width2 // 2
    me = lax.axis_index("pts")
    places = [jnp.bitwise_xor(me, mask) for mask in masks]
    hankel = hankel_of([ref[...] for ref in gram_refs], places, blocks, table_ref)
    quot = dot(ut3_ref[...], right3(hankel))
    zmat = dot(left3(quot), w3_ref[...])
    left_term = dot(left3(zmat), zt3_ref[...])
    right_term = dot(zl3_ref[...], right3(zmat))
    core = right3(
        f1_ref[...] * (left_term - left_term.T)
        + f2_ref[...] * (right_term.T - right_term)
        + dg_ref[...] * right_term
    )
    starts = [sum(sizes[:c]) for c in range(len(sizes))]

    def copy(p, c):
        at = pl.ds(starts[c], sizes[c])
        sem = osem.at[p * len(sizes) + c]
        return pltpu.make_async_copy(obuf.at[p, at, :], out_hbm.at[p, at, :], sem)

    prods = []
    for p in range(count):
        at = pl.ds(2 * p * width, 2 * width)
        prods.append(dot(up3_ref[at, :], core) + y2_ref[at, :])
    for p in range(count):
        pair = jnp.concatenate([prods[p][:width], prods[p][width:]], axis=1)
        weights = dot(left3(pair), wc3_ref[p]).astype(BF16)
        for c in range(len(sizes)):
            at = pl.ds(starts[c], sizes[c])
            obuf[p, at, :] = dot(probe_t_ref[at, :], weights).astype(BF16)
            copy(p, c).start()
    for p in range(count):
        for c in range(len(sizes)):
            copy(p, c).wait()


def hop(value, axis, size, mask):
    return lax.ppermute(value, axis, [(at, at ^ mask) for at in range(size)])


def per_device(n_pts, n_rows, solutions, probe, left_factor, singular, right_factor, adjoint):
    count, local, width2 = solutions.shape
    width = probe.shape[0]
    order = left_factor.shape[0]
    blocks = order // width
    total = count * n_pts
    unit = local // 16
    anyspace = pl.BlockSpec(memory_space=pl.ANY)
    vmem = pl.BlockSpec(memory_space=pltpu.VMEM)
    smem = pl.BlockSpec(memory_space=pltpu.SMEM)
    params = pltpu.CompilerParams(vmem_limit_bytes=20 << 20)
    in_hbm = functools.partial(pltpu.with_memory_space_constraint, memory_space=pltpu.HBM)
    sizes_in = [unit, unit] + [2 * unit] * 6 + [unit, unit]
    summed = jax.ShapeDtypeStruct((width, count * width2), F32)
    value = pl.pallas_call(
        functools.partial(gram_kernel, sizes_in),
        out_shape=summed,
        in_specs=[anyspace] * 2,
        out_specs=vmem,
        scratch_shapes=[
            pltpu.VMEM((width, local), BF16),
            pltpu.VMEM((count, local, width2), BF16),
            pltpu.SemaphoreType.DMA((len(sizes_in),)),
            pltpu.SemaphoreType.DMA((len(sizes_in),)),
        ],
        compiler_params=params,
        name="gram",
    )(in_hbm(probe), in_hbm(solutions))

    square = jax.ShapeDtypeStruct((order, order), F32)
    tall = jax.ShapeDtypeStruct((3 * order, order), BF16)
    wide = jax.ShapeDtypeStruct((order, 3 * order), BF16)
    stack = jax.ShapeDtypeStruct((2 * count * width, 3 * order), BF16)
    prep = pl.pallas_call(
        functools.partial(prep_kernel, count, blocks),
        out_shape=(
            wide,
            tall,
            tall,
            wide,
            square,
            square,
            square,
            stack,
            jax.ShapeDtypeStruct((count, 6 * order, width2), BF16),
            jax.ShapeDtypeStruct((2 * count * width, order), F32),
        ),
        in_specs=[vmem, vmem, vmem, vmem, smem, anyspace],
        out_specs=(vmem,) * 10,
        compiler_params=params,
        cost_estimate=pl.CostEstimate(flops=6 * order**3, bytes_accessed=4 << 20, transcendentals=0),
        name="prep",
    )
    turn = pl.pallas_call(
        turn_kernel,
        out_shape=jax.ShapeDtypeStruct((local, width), BF16),
        in_specs=[vmem, anyspace],
        out_specs=vmem,
        compiler_params=params,
        cost_estimate=pl.CostEstimate(flops=0, bytes_accessed=6 << 20, transcendentals=0),
        name="turn",
    )

    def add(terms, after):
        return pl.pallas_call(
            functools.partial(sum_kernel, len(terms)),
            out_shape=summed,
            in_specs=[vmem] * len(terms) + [anyspace] * len(after),
            out_specs=vmem,
            compiler_params=params,
            name="sum",
        )(*terms, *after)

    phases = jnp.asarray(phase_table(total, blocks))
    ready, probe_t = None, None
    bits = [1 << k for k in range(n_rows.bit_length() - 1)]
    for at in range(0, len(bits), 2):
        step = bits[at : at + 2]
        if len(step) == 2:
            step = [step[0], step[0] ^ step[1], step[1]]
        got = [hop(value, "rows", n_rows, bit) for bit in step]
        after = []
        if ready is None:
            ready = prep(left_factor, singular[None, :], right_factor, adjoint, phases, value)
            after = ready
        elif probe_t is None:
            probe_t = turn(probe, value)
            after = [probe_t]
        value = add([value] + got, after)
    masks = [0, n_pts - 1] + list(range(1, n_pts - 1))
    grams = [value] + [hop(value, "pts", n_pts, mask) for mask in masks[1:]]
    sizes_out = [unit, unit] + [2 * unit] + [4 * unit] * 3
    return pl.pallas_call(
        functools.partial(post_kernel, sizes_out, blocks, masks),
        out_shape=jax.ShapeDtypeStruct((count, local, width2), BF16),
        in_specs=[vmem] * (12 + len(masks)),
        out_specs=anyspace,
        scratch_shapes=[
            pltpu.VMEM((count, local, width2), BF16),
            pltpu.SemaphoreType.DMA((count * len(sizes_out),)),
        ],
        compiler_params=params,
        name="post",
    )(jnp.asarray(moment_table(total, blocks, width)), *ready, probe_t, *grams)


def solution(mesh):
    in_specs = (P("pts", "rows", None), P(None, "rows"), P(), P(), P(), P())
    out_specs = P("pts", "rows", None)
    return jax.shard_map(
        functools.partial(per_device, mesh.shape["pts"], mesh.shape["rows"]),
        mesh=mesh,
        in_specs=in_specs,
        out_specs=out_specs,
        check_vma=False,
    )
```

time: 27.6 us -> 27.2 us (0.986)
  waiting for transfers between devices: 8.44 us -> 8.1 us
    ppermute x8 -> x7, waiting for transfers between devices: 8.44 us -> 8.1 us  [hop(): return lax.ppermute(value, axis, [(at, at ^ mask) for at in range(size)])]
    pallas_call x6 -> x5, Pallas kernels: 8.78 us -> 8.72 us  [the longest x1 4.29 us: per_device(): pl.pallas_call(functools.partial(post_kernel, sizes_out, blocks, masks),...]
    ppermute x8 -> x7, starting transfers between devices: 9.56 us -> 9.5 us  [hop(): return lax.ppermute(value, axis, [(at, at ^ mask) for at in range(size)])]
  transfers between devices with their start and end apart: 8 -> 7, of which waited for: 7 -> 5; matrix products, arithmetic and copies ran while one was open for 0% -> 0% of each run, Pallas kernels for 7% -> 7%
where the time goes in v3:
time: 27.2 us; the launch traced here: 27 us
  starting transfers between devices  9.5 us (35%)
  Pallas kernels  9.35 us (34%)
  waiting for transfers between devices  8.1 us (30%)
    ppermute x7, starting transfers between devices, hop(): return lax.ppermute(value, axis, [(at, at ^ mask) for at in range(size)])  9.5 us
    ppermute x7, waiting for transfers between devices, hop(): return lax.ppermute(value, axis, [(at, at ^ mask) for at in range(size)])  8.1 us
    pallas_call x1, Pallas kernels, per_device(): pl.pallas_call(functools.partial(post_kernel, sizes_out, blocks, masks),...  4.29 us
    pallas_call x1, Pallas kernels, per_device(): pl.pallas_call(functools.partial(gram_kernel, sizes_in), out_shape=summed...  3.07 us
    pallas_call x1, Pallas kernels, per_device(): prep(left_factor, singular[None, :], right_factor, adjoint, phases, value)  1.33 us
    pallas_call x1, Pallas kernels, per_device(): probe_t = turn(probe, value)  0.63 us
  transfers between devices with their start and end apart: 7, of which 5 were waited for; matrix products, arithmetic and copies ran while one was open for 0% of the time, Pallas kernels for 7%

profile of v3, /device:TPU:0, one launch (start us, length us, event | category | flops | bytes accessed | tf_op | source)
XLA Modules:
  0.0 27.0 jit_solution(6694979227689897903)
XLA Ops:
  0.0 0.0 copy-start.5
  0.0 0.0 copy-start
  0.0 0.0 copy-start.3
  0.0 0.0 copy-start.2
  0.0 0.0 copy-start.6
  0.0 0.0 copy-start.1
  0.0 3.1 %gram.1._.refs_0_ = f32[64,256]{1,0:T(8,128)S(1)} custom-call(bf16[64,8192]{1,0:T(8,128)(2,1)} %probe_ref.1, bf16[2,8192,128]{2,1,0:T(8,128)(2,1)} %sol_hbm.1), custom_call_target="tpu_custom_call" | custom-call | tf_op jit(solution)/shard_map/gram/pallas_call | solution.py:258
  3.1 3.1 %collective-permute-start.2 = (f32[64,256]{1,0:T(8,128)S(1)}, f32[64,256]{1,0:T(8,128)S(1)}, u32[]{:S(2)}, u32[]{:S(2)}) collective-permute-start(f32[64,256]{1,0:T(8,128)S(1)} %gram.1._.refs_0_), channel_id=1, source_target_pairs={{0,2},{1,3},{2,0},{3,1},{4,6},{5,7},{6,4},{7,5},{8,10},{9,11},{10,... | collective-permute-start | bytes 196616 | tf_op jit(solution)/shard_map/ppermute | solution.py:241
  6.2 1.4 %collective-permute-start.1 = (f32[64,256]{1,0:T(8,128)S(1)}, f32[64,256]{1,0:T(8,128)S(1)}, u32[]{:S(2)}, u32[]{:S(2)}) collective-permute-start(f32[64,256]{1,0:T(8,128)S(1)} %gram.1._.refs_0_), channel_id=1, source_target_pairs={{0,3},{1,2},{2,1},{3,0},{4,7},{5,6},{6,5},{7,4},{8,11},{9,10},{10,... | collective-permute-start | bytes 196616 | tf_op jit(solution)/shard_map/ppermute | solution.py:241
  7.6 0.1 collective-permute-start
  7.7 0.0 copy-done.5
  7.7 0.0 copy-done.3
  7.7 0.0 copy-done.2
  7.8 0.0 copy-done.6
  7.8 0.0 copy-done.1
  7.8 1.3 %prep.1 = (bf16[256,768]{1,0:T(8,128)(2,1)S(1)}, bf16[768,256]{1,0:T(8,128)(2,1)S(1)}, bf16[768,256]{1,0:T(8,128)(2,1)S(1)}, bf16[256,768]{1,0:T(8,128)(2,1)S(1)...) custom-call(f32[256,256]{1,0:T(8,128)S(1)} %copy-done.1, ...), custom_call_target="tpu_custom_call" | custom-call | flops 100663296 | bytes 4194304 | tf_op jit(solution)/shard_map/prep/pallas_call | solution.py:327
  9.1 0.0 collective-permute-done.2.refs_3_
  9.1 2.3 %collective-permute-done.1.refs_2_ = f32[64,256]{1,0:T(8,128)S(1)} collective-permute-done((f32[64,256]{1,0:T(8,128)S(1)}, f32[64,256]{1,0:T(8,128)S(1)}, u32[]{:S(2)}, u32[]{:S(2)}) %collective-permute-start.1) | collective-permute-done | bytes 65568 | tf_op jit(solution)/shard_map/ppermute | solution.py:241
  11.4 0.8 %collective-permute-done.refs_1_ = f32[64,256]{1,0:T(8,128)S(1)} collective-permute-done((f32[64,256]{1,0:T(8,128)S(1)}, f32[64,256]{1,0:T(8,128)S(1)}, u32[]{:S(2)}, u32[]{:S(2)}) %collective-permute-start) | collective-permute-done | bytes 65568 | tf_op jit(solution)/shard_map/ppermute | solution.py:241
  12.2 0.0 copy-start.4
  12.2 2.7 %collective-permute-start.3 = (f32[64,256]{1,0:T(8,128)S(1)}, f32[64,256]{1,0:T(8,128)S(1)}, u32[]{:S(2)}, u32[]{:S(2)}) collective-permute-start(f32[64,256]{1,0:T(8,128)S(1)} %sum.2._.refs_0_), channel_id=1, source_target_pairs={{0,4},{1,5},{2,6},{3,7},{4,0},{5,1},{6,2},{7,3},{8,12},{9,13},{10,... | collective-permute-start | bytes 196616 | tf_op jit(solution)/shard_map/ppermute | solution.py:241
  14.8 0.0 copy-done
  14.9 0.6 %turn.1.refs_2_.probe_t_ref = bf16[8192,64]{1,0:T(8,128)(2,1)S(1)} custom-call(bf16[64,8192]{1,0:T(8,128)(2,1)S(1)} %copy-done, f32[64,256]{1,0:T(8,128)S(1)} %sum.2._.refs_0_), custom_call_target="tpu_custom_call" | custom-call | bytes 6291456 | tf_op jit(solution)/shard_map/turn/pallas_call | solution.py:330
  15.5 1.9 %collective-permute-done.3.refs_1_ = f32[64,256]{1,0:T(8,128)S(1)} collective-permute-done((f32[64,256]{1,0:T(8,128)S(1)}, f32[64,256]{1,0:T(8,128)S(1)}, u32[]{:S(2)}, u32[]{:S(2)}) %collective-permute-start.3) | collective-permute-done | bytes 65568 | tf_op jit(solution)/shard_map/ppermute | solution.py:241
  17.4 1.6 %collective-permute-start.6 = (f32[64,256]{1,0:T(8,128)S(1)}, f32[64,256]{1,0:T(8,128)S(1)}, u32[]{:S(2)}, u32[]{:S(2)}) collective-permute-start(f32[64,256]{1,0:T(8,128)S(1)} %sum.3.refs_0_), channel_id=1, source_target_pairs={{0,16},{8,24},{16,0},{24,8},{1,17},{9,25},{17,1},{25,9},{2,18},{10... | collective-permute-start | bytes 196616 | tf_op jit(solution)/shard_map/ppermute | solution.py:241
  19.0 0.0 collective-permute-start.5
  19.0 0.6 %collective-permute-start.4 = (f32[64,256]{1,0:T(8,128)S(1)}, f32[64,256]{1,0:T(8,128)S(1)}, u32[]{:S(2)}, u32[]{:S(2)}) collective-permute-start(f32[64,256]{1,0:T(8,128)S(1)} %sum.3.refs_0_), channel_id=1, source_target_pairs={{0,24},{8,16},{16,8},{24,0},{1,25},{9,17},{17,9},{25,1},{2,26},{10... | collective-permute-start | bytes 196616 | tf_op jit(solution)/shard_map/ppermute | solution.py:241
  19.6 2.1 %collective-permute-done.6.refs_3_ = f32[64,256]{1,0:T(8,128)S(1)} collective-permute-done((f32[64,256]{1,0:T(8,128)S(1)}, f32[64,256]{1,0:T(8,128)S(1)}, u32[]{:S(2)}, u32[]{:S(2)}) %collective-permute-start.6) | collective-permute-done | bytes 65568 | tf_op jit(solution)/shard_map/ppermute | solution.py:241
  21.8 0.0 collective-permute-done.5.refs_2_
  21.8 1.0 %collective-permute-done.4.refs_1_ = f32[64,256]{1,0:T(8,128)S(1)} collective-permute-done((f32[64,256]{1,0:T(8,128)S(1)}, f32[64,256]{1,0:T(8,128)S(1)}, u32[]{:S(2)}, u32[]{:S(2)}) %collective-permute-start.4) | collective-permute-done | bytes 65568 | tf_op jit(solution)/shard_map/ppermute | solution.py:241
  22.7 0.0 copy-done.4
  22.7 4.3 %post.1 = bf16[2,8192,128]{2,1,0:T(8,128)(2,1)} custom-call(f32[8,8,128]{2,1,0:T(8,128)S(1)} %copy-done.4, bf16[256,768]{1,0:T(8,128)(2,1)S(1)} %get-tuple-element.15.refs_4_.ut3_ref, bf16[768,256]{1,0:T(8,128)(2,1)S(1)} %get-tuple-element.16.refs_5_.w3_ref, bf16[768,256]{1,0:T(8,128)(2,1)S(1)} %get-tuple-element.17.refs_6_.zt3_ref, ...), custom_call_target="tpu_custom_call" | custom-call | tf_op jit(solution)/shard_map/post/pallas_call | solution.py:336
  (2 shorter events, 0.0 us)
Async XLA Ops:
  0.0 7.7 %copy-start.5 = (f32[8,10]{1,0:T(8,128)S(1)}, f32[8,10]{1,0:T(8,128)}, u32[]{:S(2)}) copy-start(f32[8,10]{1,0:T(8,128)} %constant.4.clone.phase_ref) | copy-start | bytes 964
  0.0 14.8 %copy-start = (bf16[64,8192]{1,0:T(8,128)(2,1)S(1)}, bf16[64,8192]{1,0:T(8,128)(2,1)}, u32[]{:S(2)}) copy-start(bf16[64,8192]{1,0:T(8,128)(2,1)} %probe_ref.1) | copy-start | bytes 3145732
  0.0 7.7 %copy-start.3 = (f32[256,256]{1,0:T(8,128)S(1)}, f32[256,256]{1,0:T(8,128)}, u32[]{:S(2)}) copy-start(f32[256,256]{1,0:T(8,128)} %adj_ref.1) | copy-start | bytes 786436
  0.0 7.7 %copy-start.2 = (f32[256,256]{1,0:T(8,128)S(1)}, f32[256,256]{1,0:T(8,128)}, u32[]{:S(2)}) copy-start(f32[256,256]{1,0:T(8,128)} %right_ref.1) | copy-start | bytes 786436
  0.0 7.7 %copy-start.6 = (f32[256]{0:T(256)S(1)}, f32[256]{0:T(256)}, u32[]{:S(2)}) copy-start(f32[256]{0:T(256)} %param.11) | copy-start | bytes 3076
  0.0 7.7 %copy-start.1 = (f32[256,256]{1,0:T(8,128)S(1)}, f32[256,256]{1,0:T(8,128)}, u32[]{:S(2)}) copy-start(f32[256,256]{1,0:T(8,128)} %left_ref.1) | copy-start | bytes 786436
  3.1 6.0 %collective-permute-start.2 = (f32[64,256]{1,0:T(8,128)S(1)}, f32[64,256]{1,0:T(8,128)S(1)}, u32[]{:S(2)}, u32[]{:S(2)}) collective-permute-start(f32[64,256]{1,0:T(8,128)S(1)} %gram.1._.refs_0_), channel_id=1, source_target_pairs={{0,2},{1,3},{2,0},{3,1},{4,6},{5,7},{6,4},{7,5},{8,10},{9,11},{10,... | collective-permute-start | bytes 196616 | tf_op jit(solution)/shard_map/ppermute | solution.py:241
  6.2 5.2 %collective-permute-start.1 = (f32[64,256]{1,0:T(8,128)S(1)}, f32[64,256]{1,0:T(8,128)S(1)}, u32[]{:S(2)}, u32[]{:S(2)}) collective-permute-start(f32[64,256]{1,0:T(8,128)S(1)} %gram.1._.refs_0_), channel_id=1, source_target_pairs={{0,3},{1,2},{2,1},{3,0},{4,7},{5,6},{6,5},{7,4},{8,11},{9,10},{10,... | collective-permute-start | bytes 196616 | tf_op jit(solution)/shard_map/ppermute | solution.py:241
  7.6 4.6 %collective-permute-start = (f32[64,256]{1,0:T(8,128)S(1)}, f32[64,256]{1,0:T(8,128)S(1)}, u32[]{:S(2)}, u32[]{:S(2)}) collective-permute-start(f32[64,256]{1,0:T(8,128)S(1)} %gram.1._.refs_0_), channel_id=1, source_target_pairs={{0,1},{1,0},{2,3},{3,2},{4,5},{5,4},{6,7},{7,6},{8,9},{9,8},{10,11... | collective-permute-start | bytes 196616 | tf_op jit(solution)/shard_map/ppermute | solution.py:241
  12.2 10.6 %copy-start.4 = (f32[8,8,128]{2,1,0:T(8,128)S(1)}, f32[8,8,128]{2,1,0:T(8,128)}, u32[]{:S(2)}) copy-start(f32[8,8,128]{2,1,0:T(8,128)} %constant.5.clone.table_ref) | copy-start | bytes 98308
  12.2 5.2 %collective-permute-start.3 = (f32[64,256]{1,0:T(8,128)S(1)}, f32[64,256]{1,0:T(8,128)S(1)}, u32[]{:S(2)}, u32[]{:S(2)}) collective-permute-start(f32[64,256]{1,0:T(8,128)S(1)} %sum.2._.refs_0_), channel_id=1, source_target_pairs={{0,4},{1,5},{2,6},{3,7},{4,0},{5,1},{6,2},{7,3},{8,12},{9,13},{10,... | collective-permute-start | bytes 196616 | tf_op jit(solution)/shard_map/ppermute | solution.py:241
  17.4 4.3 %collective-permute-start.6 = (f32[64,256]{1,0:T(8,128)S(1)}, f32[64,256]{1,0:T(8,128)S(1)}, u32[]{:S(2)}, u32[]{:S(2)}) collective-permute-start(f32[64,256]{1,0:T(8,128)S(1)} %sum.3.refs_0_), channel_id=1, source_target_pairs={{0,16},{8,24},{16,0},{24,8},{1,17},{9,25},{17,1},{25,9},{2,18},{10... | collective-permute-start | bytes 196616 | tf_op jit(solution)/shard_map/ppermute | solution.py:241
  19.0 2.8 %collective-permute-start.5 = (f32[64,256]{1,0:T(8,128)S(1)}, f32[64,256]{1,0:T(8,128)S(1)}, u32[]{:S(2)}, u32[]{:S(2)}) collective-permute-start(f32[64,256]{1,0:T(8,128)S(1)} %sum.3.refs_0_), channel_id=1, source_target_pairs={{0,8},{8,0},{16,24},{24,16},{1,9},{9,1},{17,25},{25,17},{2,10},{10... | collective-permute-start | bytes 196616 | tf_op jit(solution)/shard_map/ppermute | solution.py:241
  19.0 3.7 %collective-permute-start.4 = (f32[64,256]{1,0:T(8,128)S(1)}, f32[64,256]{1,0:T(8,128)S(1)}, u32[]{:S(2)}, u32[]{:S(2)}) collective-permute-start(f32[64,256]{1,0:T(8,128)S(1)} %sum.3.refs_0_), channel_id=1, source_target_pairs={{0,24},{8,16},{16,8},{24,0},{1,25},{9,17},{17,9},{25,1},{2,26},{10... | collective-permute-start | bytes 196616 | tf_op jit(solution)/shard_map/ppermute | solution.py:241

commit v4 on v3

--- a/solution.py
+++ b/solution.py
@@ -155,21 +155,36 @@
     out_ref[...] = probe_ref[...].T
 
 
-def hankel_of(grams, places, blocks, table_ref):
+def mix_kernel(blocks, masks, table_ref, *refs):
+    out_ref = refs[-1]
     width2 = table_ref.shape[2]
     width = width2 // 2
+    me = lax.axis_index("pts")
     tiles = [None] * blocks
-    for gram, place in zip(grams, places):
+    for mask, ref in zip(masks, refs[:-1]):
+        gram = ref[...]
         count = gram.shape[1] // width2
         for p in range(count):
             straight = gram[:, p * width2 : (p + 1) * width2]
             turned = pltpu.roll(straight, width, 1)
-            coef = table_ref[place * count + p]
+            coef = table_ref[jnp.bitwise_xor(me, mask) * count + p]
             for a in range(blocks):
                 term = straight * coef[a : a + 1] + turned * coef[blocks + a : blocks + a + 1]
                 tiles[a] = term if tiles[a] is None else tiles[a] + term
+    rows = width // 2
+    lane = lax.broadcasted_iota(jnp.int32, (rows, width2), 1)
+    last = jnp.where(lane < width, tiles[-1][:rows], tiles[-1][rows:])
+    out_ref[...] = jnp.concatenate(tiles[:-1] + [last], axis=0)
+
+
+def hankel_of(moments, blocks):
+    width2 = moments.shape[1]
+    width = width2 // 2
+    tiles = [moments[a * width : (a + 1) * width] for a in range(blocks - 1)]
+    packed = moments[(blocks - 1) * width :]
+    last = jnp.concatenate([pltpu.roll(packed, width, 1), packed], axis=0)
     lane = lax.broadcasted_iota(jnp.int32, (width, width2), 1)
-    turned = [pltpu.roll(tile, width, 1) for tile in tiles[:-1]] + [tiles[-1]]
+    turned = [pltpu.roll(tile, width, 1) for tile in tiles] + [last]
     between = [jnp.where(lane < width, turned[a], turned[a + 1]) for a in range(blocks - 1)]
     every = [tile for pair in zip(tiles, between) for tile in pair]
     return jnp.concatenate(
@@ -184,8 +199,8 @@
 def post_kernel(
     sizes,
     blocks,
-    masks,
-    table_ref,
+    own_ref,
+    got_ref,
     ut3_ref,
     w3_ref,
     zt3_ref,
@@ -197,14 +212,13 @@
     wc3_ref,
     y2_ref,
     probe_t_ref,
-    *refs,
+    out_hbm,
+    obuf,
+    osem,
 ):
-    gram_refs, (out_hbm, obuf, osem) = refs[: len(masks)], refs[len(masks) :]
     count, _, width2 = obuf.shape
     width = width2 // 2
-    me = lax.axis_index("pts")
-    places = [jnp.bitwise_xor(me, mask) for mask in masks]
-    hankel = hankel_of([ref[...] for ref in gram_refs], places, blocks, table_ref)
+    hankel = hankel_of(own_ref[...] + got_ref[...], blocks)
     quot = dot(ut3_ref[...], right3(hankel))
     zmat = dot(left3(quot), w3_ref[...])
     left_term = dot(left3(zmat), zt3_ref[...])
@@ -237,8 +251,13 @@
             copy(p, c).wait()
 
 
-def hop(value, axis, size, mask):
-    return lax.ppermute(value, axis, [(at, at ^ mask) for at in range(size)])
+def hop(value, n_pts, n_rows, mask):
+    pairs = [
+        (pts * n_rows + row, (pts ^ mask[0]) * n_rows + (row ^ mask[1]))
+        for pts in range(n_pts)
+        for row in range(n_rows)
+    ]
+    return lax.ppermute(value, ("pts", "rows"), pairs)
 
 
 def per_device(n_pts, n_rows, solutions, probe, left_factor, singular, right_factor, adjoint):
@@ -315,28 +334,38 @@
         )(*terms, *after)
 
     phases = jnp.asarray(phase_table(total, blocks))
-    ready, probe_t = None, None
-    bits = [1 << k for k in range(n_rows.bit_length() - 1)]
+    ready = None
+    bits = [1 << k for k in range(1, n_rows.bit_length() - 1)]
     for at in range(0, len(bits), 2):
         step = bits[at : at + 2]
         if len(step) == 2:
-            step = [step[0], step[0] ^ step[1], step[1]]
-        got = [hop(value, "rows", n_rows, bit) for bit in step]
+            step = [step[0], step[1], step[0] ^ step[1]]
+        got = [hop(value, n_pts, n_rows, (0, bit)) for bit in step]
         after = []
         if ready is None:
             ready = prep(left_factor, singular[None, :], right_factor, adjoint, phases, value)
             after = ready
-        elif probe_t is None:
-            probe_t = turn(probe, value)
-            after = [probe_t]
         value = add([value] + got, after)
-    masks = [0, n_pts - 1] + list(range(1, n_pts - 1))
-    grams = [value] + [hop(value, "pts", n_pts, mask) for mask in masks[1:]]
+    others = [(pts, 0) for pts in range(2, n_pts, 2)]
+    if n_rows > 1:
+        others = [(1, 1)] + others + [(pts ^ 1, 1) for pts, _ in others]
+    grams = [value] + [hop(value, n_pts, n_rows, mask) for mask in others]
+    probe_t = turn(probe, value)
+    rows = (blocks - 1) * width + width // 2
+    moments = pl.pallas_call(
+        functools.partial(mix_kernel, blocks, [0] + [mask[0] for mask in others]),
+        out_shape=jax.ShapeDtypeStruct((rows, width2), F32),
+        in_specs=[vmem] * (1 + len(grams)) + [anyspace],
+        out_specs=vmem,
+        compiler_params=params,
+        name="mix",
+    )(jnp.asarray(moment_table(total, blocks, width)), *grams, probe_t)
+    other = hop(moments, n_pts, n_rows, (1, 0))
     sizes_out = [unit, unit] + [2 * unit] + [4 * unit] * 3
     return pl.pallas_call(
-        functools.partial(post_kernel, sizes_out, blocks, masks),
+        functools.partial(post_kernel, sizes_out, blocks),
         out_shape=jax.ShapeDtypeStruct((count, local, width2), BF16),
-        in_specs=[vmem] * (12 + len(masks)),
+        in_specs=[vmem] * 13,
         out_specs=anyspace,
         scratch_shapes=[
             pltpu.VMEM((count, local, width2), BF16),
@@ -344,7 +373,7 @@
         ],
         compiler_params=params,
         name="post",
-    )(jnp.asarray(moment_table(total, blocks, width)), *ready, probe_t, *grams)
+    )(moments, other, *ready, probe_t)
 
 
 def solution(mesh):

time: 27.2 us -> 26.5 us (0.974)
  starting transfers between devices: 9.5 us -> 8.94 us
    ppermute x7, starting transfers between devices: 9.5 us -> 8.94 us  [hop(): return lax.ppermute(value, ('pts', 'rows'), pairs)]
    pallas_call x1 -> x2, Pallas kernels: 4.29 us -> 4.3 us  [the longest x1 4.12 us: per_device(): pl.pallas_call(functools.partial(post_kernel, sizes_out, blocks), out_sha...]
where the time goes in v4:
time: 26.5 us; the launch traced here: 26.4 us
  Pallas kernels  9.35 us (35%)
  starting transfers between devices  8.94 us (34%)
  waiting for transfers between devices  8 us (30%)
    ppermute x7, starting transfers between devices, hop(): return lax.ppermute(value, ('pts', 'rows'), pairs)  8.94 us
    ppermute x7, waiting for transfers between devices, hop(): return lax.ppermute(value, ('pts', 'rows'), pairs)  8 us
    pallas_call x1, Pallas kernels, per_device(): pl.pallas_call(functools.partial(post_kernel, sizes_out, blocks), out_sha...  4.12 us
    pallas_call x1, Pallas kernels, per_device(): pl.pallas_call(functools.partial(gram_kernel, sizes_in), out_shape=summed...  3.07 us
    pallas_call x1, Pallas kernels, per_device(): prep(left_factor, singular[None, :], right_factor, adjoint, phases, value)  1.33 us
    pallas_call x1, Pallas kernels, per_device(): probe_t = turn(probe, value)  0.63 us
  transfers between devices with their start and end apart: 7, of which 5 were waited for; matrix products, arithmetic and copies ran while one was open for 0% of the time, Pallas kernels for 7%

profile of v4, /device:TPU:0, one launch (start us, length us, event | category | flops | bytes accessed | tf_op | source)
XLA Modules:
  0.0 26.4 jit_solution(2547174019879862518)
XLA Ops:
  0.0 0.0 copy-start.5
  0.0 0.0 copy-start
  0.0 0.0 copy-start.3
  0.0 0.0 copy-start.2
  0.0 0.0 copy-start.6
  0.0 0.0 copy-start.1
  0.0 3.1 %gram.1._.refs_0_ = f32[64,256]{1,0:T(8,128)S(1)} custom-call(bf16[64,8192]{1,0:T(8,128)(2,1)} %probe_ref.1, bf16[2,8192,128]{2,1,0:T(8,128)(2,1)} %sol_hbm.1), custom_call_target="tpu_custom_call" | custom-call | tf_op jit(solution)/shard_map/gram/pallas_call | solution.py:277
  3.1 0.0 copy-start.4
  3.1 5.1 %collective-permute-start.2 = (f32[64,256]{1,0:T(8,128)S(1)}, f32[64,256]{1,0:T(8,128)S(1)}, u32[]{:S(2)}, u32[]{:S(2)}) collective-permute-start(f32[64,256]{1,0:T(8,128)S(1)} %gram.1._.refs_0_), channel_id=1, source_target_pairs={{0,6},{1,7},{2,4},{3,5},{4,2},{5,3},{6,0},{7,1},{8,14},{9,15},{10,... | collective-permute-start | bytes 196616 | tf_op jit(solution)/shard_map/ppermute | solution.py:260
  8.2 0.0 collective-permute-start.1
  8.2 0.6 %collective-permute-start = (f32[64,256]{1,0:T(8,128)S(1)}, f32[64,256]{1,0:T(8,128)S(1)}, u32[]{:S(2)}, u32[]{:S(2)}) collective-permute-start(f32[64,256]{1,0:T(8,128)S(1)} %gram.1._.refs_0_), channel_id=1, source_target_pairs={{0,2},{1,3},{2,0},{3,1},{4,6},{5,7},{6,4},{7,5},{8,10},{9,11},{10,... | collective-permute-start | bytes 196616 | tf_op jit(solution)/shard_map/ppermute | solution.py:260
  8.9 0.0 copy-done.5
  8.9 0.0 copy-done.3
  8.9 0.0 copy-done.2
  8.9 0.0 copy-done.6
  8.9 0.0 copy-done.1
  8.9 1.3 %prep.1 = (bf16[256,768]{1,0:T(8,128)(2,1)S(1)}, bf16[768,256]{1,0:T(8,128)(2,1)S(1)}, bf16[768,256]{1,0:T(8,128)(2,1)S(1)}, bf16[256,768]{1,0:T(8,128)(2,1)S(1)...) custom-call(f32[256,256]{1,0:T(8,128)S(1)} %copy-done.1, ...), custom_call_target="tpu_custom_call" | custom-call | flops 100663296 | bytes 4194304 | tf_op jit(solution)/shard_map/prep/pallas_call | solution.py:346
  10.2 0.6 %collective-permute-done.2.refs_3_ = f32[64,256]{1,0:T(8,128)S(1)} collective-permute-done((f32[64,256]{1,0:T(8,128)S(1)}, f32[64,256]{1,0:T(8,128)S(1)}, u32[]{:S(2)}, u32[]{:S(2)}) %collective-permute-start.2) | collective-permute-done | bytes 65568 | tf_op jit(solution)/shard_map/ppermute | solution.py:260
  10.8 3.0 %collective-permute-done.1.refs_2_ = f32[64,256]{1,0:T(8,128)S(1)} collective-permute-done((f32[64,256]{1,0:T(8,128)S(1)}, f32[64,256]{1,0:T(8,128)S(1)}, u32[]{:S(2)}, u32[]{:S(2)}) %collective-permute-start.1) | collective-permute-done | bytes 65568 | tf_op jit(solution)/shard_map/ppermute | solution.py:260
  13.8 0.0 collective-permute-done.refs_1_
  13.9 2.0 %collective-permute-start.5 = (f32[64,256]{1,0:T(8,128)S(1)}, f32[64,256]{1,0:T(8,128)S(1)}, u32[]{:S(2)}, u32[]{:S(2)}) collective-permute-start(f32[64,256]{1,0:T(8,128)S(1)} %sum.1._.refs_0_), channel_id=1, source_target_pairs={{0,25},{1,24},{2,27},{3,26},{4,29},{5,28},{6,31},{7,30},{8,17},{9,... | collective-permute-start | bytes 196616 | tf_op jit(solution)/shard_map/ppermute | solution.py:260
  15.8 0.5 %collective-permute-start.4 = (f32[64,256]{1,0:T(8,128)S(1)}, f32[64,256]{1,0:T(8,128)S(1)}, u32[]{:S(2)}, u32[]{:S(2)}) collective-permute-start(f32[64,256]{1,0:T(8,128)S(1)} %sum.1._.refs_0_), channel_id=1, source_target_pairs={{0,16},{1,17},{2,18},{3,19},{4,20},{5,21},{6,22},{7,23},{8,24},{9,... | collective-permute-start | bytes 196616 | tf_op jit(solution)/shard_map/ppermute | solution.py:260
  16.4 0.5 %collective-permute-start.3 = (f32[64,256]{1,0:T(8,128)S(1)}, f32[64,256]{1,0:T(8,128)S(1)}, u32[]{:S(2)}, u32[]{:S(2)}) collective-permute-start(f32[64,256]{1,0:T(8,128)S(1)} %sum.1._.refs_0_), channel_id=1, source_target_pairs={{0,9},{1,8},{2,11},{3,10},{4,13},{5,12},{6,15},{7,14},{8,1},{9,0},... | collective-permute-start | bytes 196616 | tf_op jit(solution)/shard_map/ppermute | solution.py:260
  16.9 0.0 copy-done
  16.9 0.6 %turn.1.refs_4_.probe_t_ref = bf16[8192,64]{1,0:T(8,128)(2,1)S(1)} custom-call(bf16[64,8192]{1,0:T(8,128)(2,1)S(1)} %copy-done, f32[64,256]{1,0:T(8,128)S(1)} %sum.1._.refs_0_), custom_call_target="tpu_custom_call" | custom-call | bytes 6291456 | tf_op jit(solution)/shard_map/turn/pallas_call | solution.py:353
  17.5 1.6 %collective-permute-done.5.refs_3_ = f32[64,256]{1,0:T(8,128)S(1)} collective-permute-done((f32[64,256]{1,0:T(8,128)S(1)}, f32[64,256]{1,0:T(8,128)S(1)}, u32[]{:S(2)}, u32[]{:S(2)}) %collective-permute-start.5) | collective-permute-done | bytes 65568 | tf_op jit(solution)/shard_map/ppermute | solution.py:260
  19.1 1.6 %collective-permute-done.4.refs_2_ = f32[64,256]{1,0:T(8,128)S(1)} collective-permute-done((f32[64,256]{1,0:T(8,128)S(1)}, f32[64,256]{1,0:T(8,128)S(1)}, u32[]{:S(2)}, u32[]{:S(2)}) %collective-permute-start.4) | collective-permute-done | bytes 65568 | tf_op jit(solution)/shard_map/ppermute | solution.py:260
  20.7 0.0 collective-permute-done.3.refs_1_
  20.7 0.0 copy-done.4
  20.7 0.2 mix.1.own_ref
  20.9 0.2 collective-permute-start.6
  21.1 1.2 %collective-permute-done.6.got_ref = f32[224,128]{1,0:T(8,128)S(1)} collective-permute-done((f32[224,128]{1,0:T(8,128)S(1)}, f32[224,128]{1,0:T(8,128)S(1)}, u32[]{:S(2)}, u32[]{:S(2)}) %collective-permute-start.6) | collective-permute-done | bytes 114720 | tf_op jit(solution)/shard_map/ppermute | solution.py:260
  22.3 4.1 %post.1 = bf16[2,8192,128]{2,1,0:T(8,128)(2,1)} custom-call(f32[224,128]{1,0:T(8,128)S(1)} %mix.1.own_ref, f32[224,128]{1,0:T(8,128)S(1)} %collective-permute-done.6.got_ref, bf16[256,768]{1,0:T(8,128)(2,1)S(1)} %get-tuple-element.15.refs_4_.ut3_ref, bf16[768,256]{1,0:T(8,128)(2,1)S(1)} %get-tuple-element.16.refs_5_.w3_ref, ...), custom_call_target="tpu_custom_call" | custom-call | tf_op jit(solution)/shard_map/post/pallas_call | solution.py:365
  (1 shorter events, 0.0 us)
Async XLA Ops:
  0.0 8.9 %copy-start.5 = (f32[8,10]{1,0:T(8,128)S(1)}, f32[8,10]{1,0:T(8,128)}, u32[]{:S(2)}) copy-start(f32[8,10]{1,0:T(8,128)} %constant.4.clone.phase_ref) | copy-start | bytes 964
  0.0 16.9 %copy-start = (bf16[64,8192]{1,0:T(8,128)(2,1)S(1)}, bf16[64,8192]{1,0:T(8,128)(2,1)}, u32[]{:S(2)}) copy-start(bf16[64,8192]{1,0:T(8,128)(2,1)} %probe_ref.1) | copy-start | bytes 3145732
  0.0 8.9 %copy-start.3 = (f32[256,256]{1,0:T(8,128)S(1)}, f32[256,256]{1,0:T(8,128)}, u32[]{:S(2)}) copy-start(f32[256,256]{1,0:T(8,128)} %adj_ref.1) | copy-start | bytes 786436
  0.0 8.9 %copy-start.2 = (f32[256,256]{1,0:T(8,128)S(1)}, f32[256,256]{1,0:T(8,128)}, u32[]{:S(2)}) copy-start(f32[256,256]{1,0:T(8,128)} %right_ref.1) | copy-start | bytes 786436
  0.0 8.9 %copy-start.6 = (f32[256]{0:T(256)S(1)}, f32[256]{0:T(256)}, u32[]{:S(2)}) copy-start(f32[256]{0:T(256)} %param.11) | copy-start | bytes 3076
  0.0 8.9 %copy-start.1 = (f32[256,256]{1,0:T(8,128)S(1)}, f32[256,256]{1,0:T(8,128)}, u32[]{:S(2)}) copy-start(f32[256,256]{1,0:T(8,128)} %left_ref.1) | copy-start | bytes 786436
  3.1 17.6 %copy-start.4 = (f32[8,8,128]{2,1,0:T(8,128)S(1)}, f32[8,8,128]{2,1,0:T(8,128)}, u32[]{:S(2)}) copy-start(f32[8,8,128]{2,1,0:T(8,128)} %constant.5.clone.table_ref) | copy-start | bytes 98308
  3.1 7.7 %collective-permute-start.2 = (f32[64,256]{1,0:T(8,128)S(1)}, f32[64,256]{1,0:T(8,128)S(1)}, u32[]{:S(2)}, u32[]{:S(2)}) collective-permute-start(f32[64,256]{1,0:T(8,128)S(1)} %gram.1._.refs_0_), channel_id=1, source_target_pairs={{0,6},{1,7},{2,4},{3,5},{4,2},{5,3},{6,0},{7,1},{8,14},{9,15},{10,... | collective-permute-start | bytes 196616 | tf_op jit(solution)/shard_map/ppermute | solution.py:260
  8.2 5.6 %collective-permute-start.1 = (f32[64,256]{1,0:T(8,128)S(1)}, f32[64,256]{1,0:T(8,128)S(1)}, u32[]{:S(2)}, u32[]{:S(2)}) collective-permute-start(f32[64,256]{1,0:T(8,128)S(1)} %gram.1._.refs_0_), channel_id=1, source_target_pairs={{0,4},{1,5},{2,6},{3,7},{4,0},{5,1},{6,2},{7,3},{8,12},{9,13},{10,... | collective-permute-start | bytes 196616 | tf_op jit(solution)/shard_map/ppermute | solution.py:260
  8.2 5.6 %collective-permute-start = (f32[64,256]{1,0:T(8,128)S(1)}, f32[64,256]{1,0:T(8,128)S(1)}, u32[]{:S(2)}, u32[]{:S(2)}) collective-permute-start(f32[64,256]{1,0:T(8,128)S(1)} %gram.1._.refs_0_), channel_id=1, source_target_pairs={{0,2},{1,3},{2,0},{3,1},{4,6},{5,7},{6,4},{7,5},{8,10},{9,11},{10,... | collective-permute-start | bytes 196616 | tf_op jit(solution)/shard_map/ppermute | solution.py:260
  13.9 5.3 %collective-permute-start.5 = (f32[64,256]{1,0:T(8,128)S(1)}, f32[64,256]{1,0:T(8,128)S(1)}, u32[]{:S(2)}, u32[]{:S(2)}) collective-permute-start(f32[64,256]{1,0:T(8,128)S(1)} %sum.1._.refs_0_), channel_id=1, source_target_pairs={{0,25},{1,24},{2,27},{3,26},{4,29},{5,28},{6,31},{7,30},{8,17},{9,... | collective-permute-start | bytes 196616 | tf_op jit(solution)/shard_map/ppermute | solution.py:260
  15.8 4.8 %collective-permute-start.4 = (f32[64,256]{1,0:T(8,128)S(1)}, f32[64,256]{1,0:T(8,128)S(1)}, u32[]{:S(2)}, u32[]{:S(2)}) collective-permute-start(f32[64,256]{1,0:T(8,128)S(1)} %sum.1._.refs_0_), channel_id=1, source_target_pairs={{0,16},{1,17},{2,18},{3,19},{4,20},{5,21},{6,22},{7,23},{8,24},{9,... | collective-permute-start | bytes 196616 | tf_op jit(solution)/shard_map/ppermute | solution.py:260
  16.4 4.3 %collective-permute-start.3 = (f32[64,256]{1,0:T(8,128)S(1)}, f32[64,256]{1,0:T(8,128)S(1)}, u32[]{:S(2)}, u32[]{:S(2)}) collective-permute-start(f32[64,256]{1,0:T(8,128)S(1)} %sum.1._.refs_0_), channel_id=1, source_target_pairs={{0,9},{1,8},{2,11},{3,10},{4,13},{5,12},{6,15},{7,14},{8,1},{9,0},... | collective-permute-start | bytes 196616 | tf_op jit(solution)/shard_map/ppermute | solution.py:260
  20.9 1.4 %collective-permute-start.6 = (f32[224,128]{1,0:T(8,128)S(1)}, f32[224,128]{1,0:T(8,128)S(1)}, u32[]{:S(2)}, u32[]{:S(2)}) collective-permute-start(f32[224,128]{1,0:T(8,128)S(1)} %mix.1.own_ref), channel_id=1, source_target_pairs={{0,8},{1,9},{2,10},{3,11},{4,12},{5,13},{6,14},{7,15},{8,0},{9,1},... | collective-permute-start | bytes 344072 | tf_op jit(solution)/shard_map/ppermute | solution.py:260

commit v5 on v4

--- a/solution.py
+++ b/solution.py
@@ -339,7 +339,7 @@
     for at in range(0, len(bits), 2):
         step = bits[at : at + 2]
         if len(step) == 2:
-            step = [step[0], step[1], step[0] ^ step[1]]
+            step = [step[0], step[0] ^ step[1], step[1]]
         got = [hop(value, n_pts, n_rows, (0, bit)) for bit in step]
         after = []
         if ready is None:

time: 26.5 us -> 25.6 us (0.966)
  waiting for transfers between devices: 8 us -> 6.77 us
  starting transfers between devices: 8.94 us -> 9.27 us
    ppermute x7, waiting for transfers between devices: 8 us -> 6.77 us  [hop(): return lax.ppermute(value, ('pts', 'rows'), pairs)]
    ppermute x7, starting transfers between devices: 8.94 us -> 9.27 us  [hop(): return lax.ppermute(value, ('pts', 'rows'), pairs)]
  transfers between devices with their start and end apart: 7 -> 7, of which waited for: 5 -> 7; matrix products, arithmetic and copies ran while one was open for 0% -> 0% of each run, Pallas kernels for 7% -> 8%
where the time goes in v5:
time: 25.6 us; the launch traced here: 25.5 us
  Pallas kernels  9.35 us (37%)
  starting transfers between devices  9.27 us (36%)
  waiting for transfers between devices  6.77 us (26%)
    ppermute x7, starting transfers between devices, hop(): return lax.ppermute(value, ('pts', 'rows'), pairs)  9.27 us
    ppermute x7, waiting for transfers between devices, hop(): return lax.ppermute(value, ('pts', 'rows'), pairs)  6.77 us
    pallas_call x1, Pallas kernels, per_device(): pl.pallas_call(functools.partial(post_kernel, sizes_out, blocks), out_sha...  4.12 us
    pallas_call x1, Pallas kernels, per_device(): pl.pallas_call(functools.partial(gram_kernel, sizes_in), out_shape=summed...  3.07 us
    pallas_call x1, Pallas kernels, per_device(): prep(left_factor, singular[None, :], right_factor, adjoint, phases, value)  1.33 us
    pallas_call x1, Pallas kernels, per_device(): probe_t = turn(probe, value)  0.63 us
  transfers between devices with their start and end apart: 7, of which 7 were waited for; matrix products, arithmetic and copies ran while one was open for 0% of the time, Pallas kernels for 8%

profile of v5, /device:TPU:0, one launch (start us, length us, event | category | flops | bytes accessed | tf_op | source)
XLA Modules:
  0.0 25.5 jit_solution(4430914189920903770)
XLA Ops:
  0.0 0.0 copy-start.5
  0.0 0.0 copy-start
  0.0 0.0 copy-start.3
  0.0 0.0 copy-start.2
  0.0 0.0 copy-start.6
  0.0 0.0 copy-start.1
  0.0 3.1 %gram.1._.refs_0_ = f32[64,256]{1,0:T(8,128)S(1)} custom-call(bf16[64,8192]{1,0:T(8,128)(2,1)} %probe_ref.1, bf16[2,8192,128]{2,1,0:T(8,128)(2,1)} %sol_hbm.1), custom_call_target="tpu_custom_call" | custom-call | tf_op jit(solution)/shard_map/gram/pallas_call | solution.py:277
  3.1 0.0 copy-start.4
  3.1 4.1 %collective-permute-start.2 = (f32[64,256]{1,0:T(8,128)S(1)}, f32[64,256]{1,0:T(8,128)S(1)}, u32[]{:S(2)}, u32[]{:S(2)}) collective-permute-start(f32[64,256]{1,0:T(8,128)S(1)} %gram.1._.refs_0_), channel_id=1, source_target_pairs={{0,4},{1,5},{2,6},{3,7},{4,0},{5,1},{6,2},{7,3},{8,12},{9,13},{10,... | collective-permute-start | bytes 196616 | tf_op jit(solution)/shard_map/ppermute | solution.py:260
  7.2 1.3 %collective-permute-start.1 = (f32[64,256]{1,0:T(8,128)S(1)}, f32[64,256]{1,0:T(8,128)S(1)}, u32[]{:S(2)}, u32[]{:S(2)}) collective-permute-start(f32[64,256]{1,0:T(8,128)S(1)} %gram.1._.refs_0_), channel_id=1, source_target_pairs={{0,6},{1,7},{2,4},{3,5},{4,2},{5,3},{6,0},{7,1},{8,14},{9,15},{10,... | collective-permute-start | bytes 196616 | tf_op jit(solution)/shard_map/ppermute | solution.py:260
  8.6 0.2 collective-permute-start
  8.8 0.0 copy-done.5
  8.8 0.0 copy-done.3
  8.8 0.0 copy-done.2
  8.8 0.0 copy-done.6
  8.8 0.0 copy-done.1
  8.8 1.3 %prep.1 = (bf16[256,768]{1,0:T(8,128)(2,1)S(1)}, bf16[768,256]{1,0:T(8,128)(2,1)S(1)}, bf16[768,256]{1,0:T(8,128)(2,1)S(1)}, bf16[256,768]{1,0:T(8,128)(2,1)S(1)...) custom-call(f32[256,256]{1,0:T(8,128)S(1)} %copy-done.1, ...), custom_call_target="tpu_custom_call" | custom-call | flops 100663296 | bytes 4194304 | tf_op jit(solution)/shard_map/prep/pallas_call | solution.py:346
  10.2 0.8 %collective-permute-done.2.refs_3_ = f32[64,256]{1,0:T(8,128)S(1)} collective-permute-done((f32[64,256]{1,0:T(8,128)S(1)}, f32[64,256]{1,0:T(8,128)S(1)}, u32[]{:S(2)}, u32[]{:S(2)}) %collective-permute-start.2) | collective-permute-done | bytes 65568 | tf_op jit(solution)/shard_map/ppermute | solution.py:260
  11.0 2.5 %collective-permute-done.1.refs_2_ = f32[64,256]{1,0:T(8,128)S(1)} collective-permute-done((f32[64,256]{1,0:T(8,128)S(1)}, f32[64,256]{1,0:T(8,128)S(1)}, u32[]{:S(2)}, u32[]{:S(2)}) %collective-permute-start.1) | collective-permute-done | bytes 65568 | tf_op jit(solution)/shard_map/ppermute | solution.py:260
  13.5 0.1 collective-permute-done.refs_1_
  13.6 0.7 %collective-permute-start.5 = (f32[64,256]{1,0:T(8,128)S(1)}, f32[64,256]{1,0:T(8,128)S(1)}, u32[]{:S(2)}, u32[]{:S(2)}) collective-permute-start(f32[64,256]{1,0:T(8,128)S(1)} %sum.1._.refs_0_), channel_id=1, source_target_pairs={{0,25},{1,24},{2,27},{3,26},{4,29},{5,28},{6,31},{7,30},{8,17},{9,... | collective-permute-start | bytes 196616 | tf_op jit(solution)/shard_map/ppermute | solution.py:260
  14.3 0.9 %collective-permute-start.4 = (f32[64,256]{1,0:T(8,128)S(1)}, f32[64,256]{1,0:T(8,128)S(1)}, u32[]{:S(2)}, u32[]{:S(2)}) collective-permute-start(f32[64,256]{1,0:T(8,128)S(1)} %sum.1._.refs_0_), channel_id=1, source_target_pairs={{0,16},{1,17},{2,18},{3,19},{4,20},{5,21},{6,22},{7,23},{8,24},{9,... | collective-permute-start | bytes 196616 | tf_op jit(solution)/shard_map/ppermute | solution.py:260
  15.2 1.4 %collective-permute-start.3 = (f32[64,256]{1,0:T(8,128)S(1)}, f32[64,256]{1,0:T(8,128)S(1)}, u32[]{:S(2)}, u32[]{:S(2)}) collective-permute-start(f32[64,256]{1,0:T(8,128)S(1)} %sum.1._.refs_0_), channel_id=1, source_target_pairs={{0,9},{1,8},{2,11},{3,10},{4,13},{5,12},{6,15},{7,14},{8,1},{9,0},... | collective-permute-start | bytes 196616 | tf_op jit(solution)/shard_map/ppermute | solution.py:260
  16.6 0.0 copy-done
  16.6 0.6 %turn.1.refs_4_.probe_t_ref = bf16[8192,64]{1,0:T(8,128)(2,1)S(1)} custom-call(bf16[64,8192]{1,0:T(8,128)(2,1)S(1)} %copy-done, f32[64,256]{1,0:T(8,128)S(1)} %sum.1._.refs_0_), custom_call_target="tpu_custom_call" | custom-call | bytes 6291456 | tf_op jit(solution)/shard_map/turn/pallas_call | solution.py:353
  17.2 1.7 %collective-permute-done.5.refs_3_ = f32[64,256]{1,0:T(8,128)S(1)} collective-permute-done((f32[64,256]{1,0:T(8,128)S(1)}, f32[64,256]{1,0:T(8,128)S(1)}, u32[]{:S(2)}, u32[]{:S(2)}) %collective-permute-start.5) | collective-permute-done | bytes 65568 | tf_op jit(solution)/shard_map/ppermute | solution.py:260
  18.9 0.3 %collective-permute-done.4.refs_2_ = f32[64,256]{1,0:T(8,128)S(1)} collective-permute-done((f32[64,256]{1,0:T(8,128)S(1)}, f32[64,256]{1,0:T(8,128)S(1)}, u32[]{:S(2)}, u32[]{:S(2)}) %collective-permute-start.4) | collective-permute-done | bytes 65568 | tf_op jit(solution)/shard_map/ppermute | solution.py:260
  19.2 0.4 %collective-permute-done.3.refs_1_ = f32[64,256]{1,0:T(8,128)S(1)} collective-permute-done((f32[64,256]{1,0:T(8,128)S(1)}, f32[64,256]{1,0:T(8,128)S(1)}, u32[]{:S(2)}, u32[]{:S(2)}) %collective-permute-start.3) | collective-permute-done | bytes 65568 | tf_op jit(solution)/shard_map/ppermute | solution.py:260
  19.6 0.0 copy-done.4
  19.6 0.2 mix.1.own_ref
  19.8 0.6 %collective-permute-start.6 = (f32[224,128]{1,0:T(8,128)S(1)}, f32[224,128]{1,0:T(8,128)S(1)}, u32[]{:S(2)}, u32[]{:S(2)}) collective-permute-start(f32[224,128]{1,0:T(8,128)S(1)} %mix.1.own_ref), channel_id=1, source_target_pairs={{0,8},{1,9},{2,10},{3,11},{4,12},{5,13},{6,14},{7,15},{8,0},{9,1},... | collective-permute-start | bytes 344072 | tf_op jit(solution)/shard_map/ppermute | solution.py:260
  20.4 1.0 %collective-permute-done.6.got_ref = f32[224,128]{1,0:T(8,128)S(1)} collective-permute-done((f32[224,128]{1,0:T(8,128)S(1)}, f32[224,128]{1,0:T(8,128)S(1)}, u32[]{:S(2)}, u32[]{:S(2)}) %collective-permute-start.6) | collective-permute-done | bytes 114720 | tf_op jit(solution)/shard_map/ppermute | solution.py:260
  21.4 4.1 %post.1 = bf16[2,8192,128]{2,1,0:T(8,128)(2,1)} custom-call(f32[224,128]{1,0:T(8,128)S(1)} %mix.1.own_ref, f32[224,128]{1,0:T(8,128)S(1)} %collective-permute-done.6.got_ref, bf16[256,768]{1,0:T(8,128)(2,1)S(1)} %get-tuple-element.15.refs_4_.ut3_ref, bf16[768,256]{1,0:T(8,128)(2,1)S(1)} %get-tuple-element.16.refs_5_.w3_ref, ...), custom_call_target="tpu_custom_call" | custom-call | tf_op jit(solution)/shard_map/post/pallas_call | solution.py:365
  (1 shorter events, 0.0 us)
Async XLA Ops:
  0.0 8.8 %copy-start.5 = (f32[8,10]{1,0:T(8,128)S(1)}, f32[8,10]{1,0:T(8,128)}, u32[]{:S(2)}) copy-start(f32[8,10]{1,0:T(8,128)} %constant.4.clone.phase_ref) | copy-start | bytes 964
  0.0 16.6 %copy-start = (bf16[64,8192]{1,0:T(8,128)(2,1)S(1)}, bf16[64,8192]{1,0:T(8,128)(2,1)}, u32[]{:S(2)}) copy-start(bf16[64,8192]{1,0:T(8,128)(2,1)} %probe_ref.1) | copy-start | bytes 3145732
  0.0 8.8 %copy-start.3 = (f32[256,256]{1,0:T(8,128)S(1)}, f32[256,256]{1,0:T(8,128)}, u32[]{:S(2)}) copy-start(f32[256,256]{1,0:T(8,128)} %adj_ref.1) | copy-start | bytes 786436
  0.0 8.8 %copy-start.2 = (f32[256,256]{1,0:T(8,128)S(1)}, f32[256,256]{1,0:T(8,128)}, u32[]{:S(2)}) copy-start(f32[256,256]{1,0:T(8,128)} %right_ref.1) | copy-start | bytes 786436
  0.0 8.8 %copy-start.6 = (f32[256]{0:T(256)S(1)}, f32[256]{0:T(256)}, u32[]{:S(2)}) copy-start(f32[256]{0:T(256)} %param.11) | copy-start | bytes 3076
  0.0 8.8 %copy-start.1 = (f32[256,256]{1,0:T(8,128)S(1)}, f32[256,256]{1,0:T(8,128)}, u32[]{:S(2)}) copy-start(f32[256,256]{1,0:T(8,128)} %left_ref.1) | copy-start | bytes 786436
  3.1 16.5 %copy-start.4 = (f32[8,8,128]{2,1,0:T(8,128)S(1)}, f32[8,8,128]{2,1,0:T(8,128)}, u32[]{:S(2)}) copy-start(f32[8,8,128]{2,1,0:T(8,128)} %constant.5.clone.table_ref) | copy-start | bytes 98308
  3.1 7.9 %collective-permute-start.2 = (f32[64,256]{1,0:T(8,128)S(1)}, f32[64,256]{1,0:T(8,128)S(1)}, u32[]{:S(2)}, u32[]{:S(2)}) collective-permute-start(f32[64,256]{1,0:T(8,128)S(1)} %gram.1._.refs_0_), channel_id=1, source_target_pairs={{0,4},{1,5},{2,6},{3,7},{4,0},{5,1},{6,2},{7,3},{8,12},{9,13},{10,... | collective-permute-start | bytes 196616 | tf_op jit(solution)/shard_map/ppermute | solution.py:260
  7.2 6.2 %collective-permute-start.1 = (f32[64,256]{1,0:T(8,128)S(1)}, f32[64,256]{1,0:T(8,128)S(1)}, u32[]{:S(2)}, u32[]{:S(2)}) collective-permute-start(f32[64,256]{1,0:T(8,128)S(1)} %gram.1._.refs_0_), channel_id=1, source_target_pairs={{0,6},{1,7},{2,4},{3,5},{4,2},{5,3},{6,0},{7,1},{8,14},{9,15},{10,... | collective-permute-start | bytes 196616 | tf_op jit(solution)/shard_map/ppermute | solution.py:260
  8.6 5.0 %collective-permute-start = (f32[64,256]{1,0:T(8,128)S(1)}, f32[64,256]{1,0:T(8,128)S(1)}, u32[]{:S(2)}, u32[]{:S(2)}) collective-permute-start(f32[64,256]{1,0:T(8,128)S(1)} %gram.1._.refs_0_), channel_id=1, source_target_pairs={{0,2},{1,3},{2,0},{3,1},{4,6},{5,7},{6,4},{7,5},{8,10},{9,11},{10,... | collective-permute-start | bytes 196616 | tf_op jit(solution)/shard_map/ppermute | solution.py:260
  13.6 5.3 %collective-permute-start.5 = (f32[64,256]{1,0:T(8,128)S(1)}, f32[64,256]{1,0:T(8,128)S(1)}, u32[]{:S(2)}, u32[]{:S(2)}) collective-permute-start(f32[64,256]{1,0:T(8,128)S(1)} %sum.1._.refs_0_), channel_id=1, source_target_pairs={{0,25},{1,24},{2,27},{3,26},{4,29},{5,28},{6,31},{7,30},{8,17},{9,... | collective-permute-start | bytes 196616 | tf_op jit(solution)/shard_map/ppermute | solution.py:260
  14.3 4.9 %collective-permute-start.4 = (f32[64,256]{1,0:T(8,128)S(1)}, f32[64,256]{1,0:T(8,128)S(1)}, u32[]{:S(2)}, u32[]{:S(2)}) collective-permute-start(f32[64,256]{1,0:T(8,128)S(1)} %sum.1._.refs_0_), channel_id=1, source_target_pairs={{0,16},{1,17},{2,18},{3,19},{4,20},{5,21},{6,22},{7,23},{8,24},{9,... | collective-permute-start | bytes 196616 | tf_op jit(solution)/shard_map/ppermute | solution.py:260
  15.2 4.4 %collective-permute-start.3 = (f32[64,256]{1,0:T(8,128)S(1)}, f32[64,256]{1,0:T(8,128)S(1)}, u32[]{:S(2)}, u32[]{:S(2)}) collective-permute-start(f32[64,256]{1,0:T(8,128)S(1)} %sum.1._.refs_0_), channel_id=1, source_target_pairs={{0,9},{1,8},{2,11},{3,10},{4,13},{5,12},{6,15},{7,14},{8,1},{9,0},... | collective-permute-start | bytes 196616 | tf_op jit(solution)/shard_map/ppermute | solution.py:260
  19.8 1.6 %collective-permute-start.6 = (f32[224,128]{1,0:T(8,128)S(1)}, f32[224,128]{1,0:T(8,128)S(1)}, u32[]{:S(2)}, u32[]{:S(2)}) collective-permute-start(f32[224,128]{1,0:T(8,128)S(1)} %mix.1.own_ref), channel_id=1, source_target_pairs={{0,8},{1,9},{2,10},{3,11},{4,12},{5,13},{6,14},{7,15},{8,0},{9,1},... | collective-permute-start | bytes 344072 | tf_op jit(solution)/shard_map/ppermute | solution.py:260

commit v6 on v5

--- a/solution.py
+++ b/solution.py
@@ -81,10 +81,10 @@
 def prep_kernel(
     count,
     blocks,
-    left_ref,
-    sing_ref,
-    right_ref,
-    adj_ref,
+    left_hbm,
+    sing_hbm,
+    right_hbm,
+    adj_hbm,
     phase_ref,
     _,
     ut3_ref,
@@ -97,9 +97,24 @@
     up3_ref,
     wc3_ref,
     y2_ref,
+    left_ref,
+    sing_ref,
+    right_ref,
+    adj_ref,
+    sem,
 ):
     me = lax.axis_index("pts")
     order = left_ref.shape[0]
+    fetches = [
+        pltpu.make_async_copy(source, held, sem.at[at])
+        for at, (source, held) in enumerate(
+            [(left_hbm, left_ref), (sing_hbm, sing_ref), (right_hbm, right_ref), (adj_hbm, adj_ref)]
+        )
+    ]
+    for fetch in fetches:
+        fetch.start()
+    for fetch in fetches:
+        fetch.wait()
     width = order // blocks
     left = left_ref[...]
     right = right_ref[...]
@@ -274,13 +289,12 @@
     in_hbm = functools.partial(pltpu.with_memory_space_constraint, memory_space=pltpu.HBM)
     sizes_in = [unit, unit] + [2 * unit] * 6 + [unit, unit]
     summed = jax.ShapeDtypeStruct((width, count * width2), F32)
-    value = pl.pallas_call(
+    value, held = pl.pallas_call(
         functools.partial(gram_kernel, sizes_in),
-        out_shape=summed,
+        out_shape=(summed, jax.ShapeDtypeStruct((width, local), BF16)),
         in_specs=[anyspace] * 2,
-        out_specs=vmem,
+        out_specs=(vmem, vmem),
         scratch_shapes=[
-            pltpu.VMEM((width, local), BF16),
             pltpu.VMEM((count, local, width2), BF16),
             pltpu.SemaphoreType.DMA((len(sizes_in),)),
             pltpu.SemaphoreType.DMA((len(sizes_in),)),
@@ -307,8 +321,15 @@
             jax.ShapeDtypeStruct((count, 6 * order, width2), BF16),
             jax.ShapeDtypeStruct((2 * count * width, order), F32),
         ),
-        in_specs=[vmem, vmem, vmem, vmem, smem, anyspace],
+        in_specs=[anyspace] * 4 + [smem, anyspace],
         out_specs=(vmem,) * 10,
+        scratch_shapes=[
+            pltpu.VMEM((order, order), F32),
+            pltpu.VMEM((1, order), F32),
+            pltpu.VMEM((order, order), F32),
+            pltpu.VMEM((order, order), F32),
+            pltpu.SemaphoreType.DMA((4,)),
+        ],
         compiler_params=params,
         cost_estimate=pl.CostEstimate(flops=6 * order**3, bytes_accessed=4 << 20, transcendentals=0),
         name="prep",
@@ -343,14 +364,15 @@
         got = [hop(value, n_pts, n_rows, (0, bit)) for bit in step]
         after = []
         if ready is None:
-            ready = prep(left_factor, singular[None, :], right_factor, adjoint, phases, value)
+            factors = (left_factor, singular[None, :], right_factor, adjoint)
+            ready = prep(*(in_hbm(v) for v in factors), phases, value)
             after = ready
         value = add([value] + got, after)
     others = [(pts, 0) for pts in range(2, n_pts, 2)]
     if n_rows > 1:
         others = [(1, 1)] + others + [(pts ^ 1, 1) for pts, _ in others]
     grams = [value] + [hop(value, n_pts, n_rows, mask) for mask in others]
-    probe_t = turn(probe, value)
+    probe_t = turn(held, value)
     rows = (blocks - 1) * width + width // 2
     moments = pl.pallas_call(
         functools.partial(mix_kernel, blocks, [0] + [mask[0] for mask in others]),

time: 25.6 us -> 25.5 us (level)
  waiting for transfers between devices: 6.77 us -> 5.67 us
  Pallas kernels: 9.35 us -> 10.3 us
    ppermute x7, waiting for transfers between devices: 6.77 us -> 5.67 us  [hop(): return lax.ppermute(value, ('pts', 'rows'), pairs)]
    pallas_call x3, Pallas kernels: 5.03 us -> 6.02 us  [the longest x1 2.95 us: per_device(): pl.pallas_call(functools.partial(gram_kernel, sizes_in), out_shape=(summe...]
  transfers between devices with their start and end apart: 7 -> 7, of which waited for: 7 -> 6; matrix products, arithmetic and copies ran while one was open for 0% -> 0% of each run, Pallas kernels for 8% -> 12%
where the time goes in v6:
time: 25.5 us; the launch traced here: 25.3 us
  Pallas kernels  10.3 us (40%)
  starting transfers between devices  9.27 us (36%)
  waiting for transfers between devices  5.67 us (22%)
    ppermute x7, starting transfers between devices, hop(): return lax.ppermute(value, ('pts', 'rows'), pairs)  9.27 us
    ppermute x7, waiting for transfers between devices, hop(): return lax.ppermute(value, ('pts', 'rows'), pairs)  5.67 us
    pallas_call x1, Pallas kernels, per_device(): pl.pallas_call(functools.partial(post_kernel, sizes_out, blocks), out_sha...  4.11 us
    pallas_call x1, Pallas kernels, per_device(): pl.pallas_call(functools.partial(gram_kernel, sizes_in), out_shape=(summe...  2.95 us
    pallas_call x1, Pallas kernels, per_device(): ready = prep(*(in_hbm(v) for v in factors), phases, value)  2.45 us
    pallas_call x1, Pallas kernels, per_device(): probe_t = turn(held, value)  0.63 us
  transfers between devices with their start and end apart: 7, of which 6 were waited for; matrix products, arithmetic and copies ran while one was open for 0% of the time, Pallas kernels for 12%

profile of v6, /device:TPU:0, one launch (start us, length us, event | category | flops | bytes accessed | tf_op | source)
XLA Modules:
  0.0 25.3 jit_solution(3752618473336957013)
XLA Ops:
  0.0 0.0 copy-start.1
  0.0 3.0 %gram.1 = (f32[64,256]{1,0:T(8,128)S(1)}, bf16[64,8192]{1,0:T(8,128)(2,1)S(1)}) custom-call(bf16[64,8192]{1,0:T(8,128)(2,1)} %probe_hbm.1, bf16[2,8192,128]{2,1,0:T(8,128)(2,1)} %sol_hbm.1), custom_call_target="tpu_custom_call" | custom-call | tf_op jit(solution)/shard_map/gram/pallas_call | solution.py:292
  3.0 0.0 copy-start
  3.0 4.1 %collective-permute-start.2 = (f32[64,256]{1,0:T(8,128)S(1)}, f32[64,256]{1,0:T(8,128)S(1)}, u32[]{:S(2)}, u32[]{:S(2)}) collective-permute-start(f32[64,256]{1,0:T(8,128)S(1)} %get-tuple-element.17._.refs_0_), channel_id=1, source_target_pairs={{0,4},{1,5},{2,6},{3,7},{4,0},{5,1},{6,2},{7,3},{8,12},{9,13},{10,... | collective-permute-start | bytes 196616 | tf_op jit(solution)/shard_map/ppermute | solution.py:275
  7.1 1.3 %collective-permute-start.1 = (f32[64,256]{1,0:T(8,128)S(1)}, f32[64,256]{1,0:T(8,128)S(1)}, u32[]{:S(2)}, u32[]{:S(2)}) collective-permute-start(f32[64,256]{1,0:T(8,128)S(1)} %get-tuple-element.17._.refs_0_), channel_id=1, source_target_pairs={{0,6},{1,7},{2,4},{3,5},{4,2},{5,3},{6,0},{7,1},{8,14},{9,15},{10,... | collective-permute-start | bytes 196616 | tf_op jit(solution)/shard_map/ppermute | solution.py:275
  8.4 0.2 collective-permute-start
  8.7 0.0 copy-done.1
  8.7 2.4 %prep.1 = (bf16[256,768]{1,0:T(8,128)(2,1)S(1)}, bf16[768,256]{1,0:T(8,128)(2,1)S(1)}, bf16[768,256]{1,0:T(8,128)(2,1)S(1)}, bf16[256,768]{1,0:T(8,128)(2,1)S(1)...) custom-call(f32[256,256]{1,0:T(8,128)} %left_hbm.1, ...), custom_call_target="tpu_custom_call" | custom-call | flops 100663296 | bytes 4194304 | tf_op jit(solution)/shard_map/prep/pallas_call | solution.py:368
  11.1 0.0 collective-permute-done.2.refs_3_
  11.1 2.2 %collective-permute-done.1.refs_2_ = f32[64,256]{1,0:T(8,128)S(1)} collective-permute-done((f32[64,256]{1,0:T(8,128)S(1)}, f32[64,256]{1,0:T(8,128)S(1)}, u32[]{:S(2)}, u32[]{:S(2)}) %collective-permute-start.1) | collective-permute-done | bytes 65568 | tf_op jit(solution)/shard_map/ppermute | solution.py:275
  13.3 0.1 collective-permute-done.refs_1_
  13.4 0.7 %collective-permute-start.5 = (f32[64,256]{1,0:T(8,128)S(1)}, f32[64,256]{1,0:T(8,128)S(1)}, u32[]{:S(2)}, u32[]{:S(2)}) collective-permute-start(f32[64,256]{1,0:T(8,128)S(1)} %sum.1._.refs_0_), channel_id=1, source_target_pairs={{0,25},{1,24},{2,27},{3,26},{4,29},{5,28},{6,31},{7,30},{8,17},{9,... | collective-permute-start | bytes 196616 | tf_op jit(solution)/shard_map/ppermute | solution.py:275
  14.1 0.9 %collective-permute-start.4 = (f32[64,256]{1,0:T(8,128)S(1)}, f32[64,256]{1,0:T(8,128)S(1)}, u32[]{:S(2)}, u32[]{:S(2)}) collective-permute-start(f32[64,256]{1,0:T(8,128)S(1)} %sum.1._.refs_0_), channel_id=1, source_target_pairs={{0,16},{1,17},{2,18},{3,19},{4,20},{5,21},{6,22},{7,23},{8,24},{9,... | collective-permute-start | bytes 196616 | tf_op jit(solution)/shard_map/ppermute | solution.py:275
  15.1 1.4 %collective-permute-start.3 = (f32[64,256]{1,0:T(8,128)S(1)}, f32[64,256]{1,0:T(8,128)S(1)}, u32[]{:S(2)}, u32[]{:S(2)}) collective-permute-start(f32[64,256]{1,0:T(8,128)S(1)} %sum.1._.refs_0_), channel_id=1, source_target_pairs={{0,9},{1,8},{2,11},{3,10},{4,13},{5,12},{6,15},{7,14},{8,1},{9,0},... | collective-permute-start | bytes 196616 | tf_op jit(solution)/shard_map/ppermute | solution.py:275
  16.4 0.6 %turn.1.refs_4_.probe_t_ref = bf16[8192,64]{1,0:T(8,128)(2,1)S(1)} custom-call(bf16[64,8192]{1,0:T(8,128)(2,1)S(1)} %get-tuple-element.28.probe_ref, f32[64,256]{1,0:T(8,128)S(1)} %sum.1._.refs_0_), custom_call_target="tpu_custom_call" | custom-call | bytes 6291456 | tf_op jit(solution)/shard_map/turn/pallas_call | solution.py:375
  17.0 1.7 %collective-permute-done.5.refs_3_ = f32[64,256]{1,0:T(8,128)S(1)} collective-permute-done((f32[64,256]{1,0:T(8,128)S(1)}, f32[64,256]{1,0:T(8,128)S(1)}, u32[]{:S(2)}, u32[]{:S(2)}) %collective-permute-start.5) | collective-permute-done | bytes 65568 | tf_op jit(solution)/shard_map/ppermute | solution.py:275
  18.7 0.3 %collective-permute-done.4.refs_2_ = f32[64,256]{1,0:T(8,128)S(1)} collective-permute-done((f32[64,256]{1,0:T(8,128)S(1)}, f32[64,256]{1,0:T(8,128)S(1)}, u32[]{:S(2)}, u32[]{:S(2)}) %collective-permute-start.4) | collective-permute-done | bytes 65568 | tf_op jit(solution)/shard_map/ppermute | solution.py:275
  19.0 0.4 %collective-permute-done.3.refs_1_ = f32[64,256]{1,0:T(8,128)S(1)} collective-permute-done((f32[64,256]{1,0:T(8,128)S(1)}, f32[64,256]{1,0:T(8,128)S(1)}, u32[]{:S(2)}, u32[]{:S(2)}) %collective-permute-start.3) | collective-permute-done | bytes 65568 | tf_op jit(solution)/shard_map/ppermute | solution.py:275
  19.5 0.0 copy-done
  19.5 0.2 mix.1.own_ref
  19.7 0.6 %collective-permute-start.6 = (f32[224,128]{1,0:T(8,128)S(1)}, f32[224,128]{1,0:T(8,128)S(1)}, u32[]{:S(2)}, u32[]{:S(2)}) collective-permute-start(f32[224,128]{1,0:T(8,128)S(1)} %mix.1.own_ref), channel_id=1, source_target_pairs={{0,8},{1,9},{2,10},{3,11},{4,12},{5,13},{6,14},{7,15},{8,0},{9,1},... | collective-permute-start | bytes 344072 | tf_op jit(solution)/shard_map/ppermute | solution.py:275
  20.3 1.0 %collective-permute-done.6.got_ref = f32[224,128]{1,0:T(8,128)S(1)} collective-permute-done((f32[224,128]{1,0:T(8,128)S(1)}, f32[224,128]{1,0:T(8,128)S(1)}, u32[]{:S(2)}, u32[]{:S(2)}) %collective-permute-start.6) | collective-permute-done | bytes 114720 | tf_op jit(solution)/shard_map/ppermute | solution.py:275
  21.2 4.1 %post.1 = bf16[2,8192,128]{2,1,0:T(8,128)(2,1)} custom-call(f32[224,128]{1,0:T(8,128)S(1)} %mix.1.own_ref, f32[224,128]{1,0:T(8,128)S(1)} %collective-permute-done.6.got_ref, bf16[256,768]{1,0:T(8,128)(2,1)S(1)} %get-tuple-element.18.refs_4_.ut3_ref, bf16[768,256]{1,0:T(8,128)(2,1)S(1)} %get-tuple-element.19.refs_5_.w3_ref, ...), custom_call_target="tpu_custom_call" | custom-call | tf_op jit(solution)/shard_map/post/pallas_call | solution.py:387
  (1 shorter events, 0.0 us)
Async XLA Ops:
  0.0 8.7 %copy-start.1 = (f32[8,10]{1,0:T(8,128)S(1)}, f32[8,10]{1,0:T(8,128)}, u32[]{:S(2)}) copy-start(f32[8,10]{1,0:T(8,128)} %constant.4.clone.phase_ref) | copy-start | bytes 964
  3.0 16.5 %copy-start = (f32[8,8,128]{2,1,0:T(8,128)S(1)}, f32[8,8,128]{2,1,0:T(8,128)}, u32[]{:S(2)}) copy-start(f32[8,8,128]{2,1,0:T(8,128)} %constant.5.clone.table_ref) | copy-start | bytes 98308
  3.0 8.1 %collective-permute-start.2 = (f32[64,256]{1,0:T(8,128)S(1)}, f32[64,256]{1,0:T(8,128)S(1)}, u32[]{:S(2)}, u32[]{:S(2)}) collective-permute-start(f32[64,256]{1,0:T(8,128)S(1)} %get-tuple-element.17._.refs_0_), channel_id=1, source_target_pairs={{0,4},{1,5},{2,6},{3,7},{4,0},{5,1},{6,2},{7,3},{8,12},{9,13},{10,... | collective-permute-start | bytes 196616 | tf_op jit(solution)/shard_map/ppermute | solution.py:275
  7.1 6.2 %collective-permute-start.1 = (f32[64,256]{1,0:T(8,128)S(1)}, f32[64,256]{1,0:T(8,128)S(1)}, u32[]{:S(2)}, u32[]{:S(2)}) collective-permute-start(f32[64,256]{1,0:T(8,128)S(1)} %get-tuple-element.17._.refs_0_), channel_id=1, source_target_pairs={{0,6},{1,7},{2,4},{3,5},{4,2},{5,3},{6,0},{7,1},{8,14},{9,15},{10,... | collective-permute-start | bytes 196616 | tf_op jit(solution)/shard_map/ppermute | solution.py:275
  8.4 5.0 %collective-permute-start = (f32[64,256]{1,0:T(8,128)S(1)}, f32[64,256]{1,0:T(8,128)S(1)}, u32[]{:S(2)}, u32[]{:S(2)}) collective-permute-start(f32[64,256]{1,0:T(8,128)S(1)} %get-tuple-element.17._.refs_0_), channel_id=1, source_target_pairs={{0,2},{1,3},{2,0},{3,1},{4,6},{5,7},{6,4},{7,5},{8,10},{9,11},{10,... | collective-permute-start | bytes 196616 | tf_op jit(solution)/shard_map/ppermute | solution.py:275
  13.4 5.3 %collective-permute-start.5 = (f32[64,256]{1,0:T(8,128)S(1)}, f32[64,256]{1,0:T(8,128)S(1)}, u32[]{:S(2)}, u32[]{:S(2)}) collective-permute-start(f32[64,256]{1,0:T(8,128)S(1)} %sum.1._.refs_0_), channel_id=1, source_target_pairs={{0,25},{1,24},{2,27},{3,26},{4,29},{5,28},{6,31},{7,30},{8,17},{9,... | collective-permute-start | bytes 196616 | tf_op jit(solution)/shard_map/ppermute | solution.py:275
  14.1 4.9 %collective-permute-start.4 = (f32[64,256]{1,0:T(8,128)S(1)}, f32[64,256]{1,0:T(8,128)S(1)}, u32[]{:S(2)}, u32[]{:S(2)}) collective-permute-start(f32[64,256]{1,0:T(8,128)S(1)} %sum.1._.refs_0_), channel_id=1, source_target_pairs={{0,16},{1,17},{2,18},{3,19},{4,20},{5,21},{6,22},{7,23},{8,24},{9,... | collective-permute-start | bytes 196616 | tf_op jit(solution)/shard_map/ppermute | solution.py:275
  15.1 4.4 %collective-permute-start.3 = (f32[64,256]{1,0:T(8,128)S(1)}, f32[64,256]{1,0:T(8,128)S(1)}, u32[]{:S(2)}, u32[]{:S(2)}) collective-permute-start(f32[64,256]{1,0:T(8,128)S(1)} %sum.1._.refs_0_), channel_id=1, source_target_pairs={{0,9},{1,8},{2,11},{3,10},{4,13},{5,12},{6,15},{7,14},{8,1},{9,0},... | collective-permute-start | bytes 196616 | tf_op jit(solution)/shard_map/ppermute | solution.py:275
  19.7 1.6 %collective-permute-start.6 = (f32[224,128]{1,0:T(8,128)S(1)}, f32[224,128]{1,0:T(8,128)S(1)}, u32[]{:S(2)}, u32[]{:S(2)}) collective-permute-start(f32[224,128]{1,0:T(8,128)S(1)} %mix.1.own_ref), channel_id=1, source_target_pairs={{0,8},{1,9},{2,10},{3,11},{4,12},{5,13},{6,14},{7,15},{8,0},{9,1},... | collective-permute-start | bytes 344072 | tf_op jit(solution)/shard_map/ppermute | solution.py:275

commit v7 on v6

--- a/solution.py
+++ b/solution.py
@@ -56,6 +56,7 @@
 def gram_kernel(sizes, probe_hbm, sol_hbm, out_ref, pbuf, sbuf, psem, ssem):
     count = sbuf.shape[0]
     starts = [sum(sizes[:c]) for c in range(len(sizes))]
+    step = min(sizes)
 
     def copies(c):
         at = pl.ds(starts[c], sizes[c])
@@ -71,10 +72,11 @@
     for c in range(len(sizes)):
         for copy in copies(c):
             copy.wait()
-        at = pl.ds(starts[c], sizes[c])
-        side = jnp.concatenate([sbuf[p, at, :] for p in range(count)], axis=1)
-        part = dot(pbuf[:, at], side)
-        gram = part if gram is None else gram + part
+        for first in range(starts[c], starts[c] + sizes[c], step):
+            at = pl.ds(first, step)
+            side = jnp.concatenate([sbuf[p, at, :] for p in range(count)], axis=1)
+            part = dot(pbuf[:, at], side)
+            gram = part if gram is None else gram + part
     out_ref[...] = gram
 
 
@@ -287,7 +289,7 @@
     smem = pl.BlockSpec(memory_space=pltpu.SMEM)
     params = pltpu.CompilerParams(vmem_limit_bytes=20 << 20)
     in_hbm = functools.partial(pltpu.with_memory_space_constraint, memory_space=pltpu.HBM)
-    sizes_in = [unit, unit] + [2 * unit] * 6 + [unit, unit]
+    sizes_in = [2 * unit] * 7 + [unit, unit]
     summed = jax.ShapeDtypeStruct((width, count * width2), F32)
     value, held = pl.pallas_call(
         functools.partial(gram_kernel, sizes_in),
@@ -383,7 +385,7 @@
         name="mix",
     )(jnp.asarray(moment_table(total, blocks, width)), *grams, probe_t)
     other = hop(moments, n_pts, n_rows, (1, 0))
-    sizes_out = [unit, unit] + [2 * unit] + [4 * unit] * 3
+    sizes_out = [unit, unit] + [2 * unit] * 7
     return pl.pallas_call(
         functools.partial(post_kernel, sizes_out, blocks),
         out_shape=jax.ShapeDtypeStruct((count, local, width2), BF16),

time: 25.5 us -> 25.4 us (level)
  no operation moved by 1% of the time
where the time goes in v7:
time: 25.4 us; the launch traced here: 25.2 us
  Pallas kernels  10.2 us (40%)
  starting transfers between devices  9.26 us (36%)
  waiting for transfers between devices  5.67 us (22%)
    ppermute x7, starting transfers between devices, hop(): return lax.ppermute(value, ('pts', 'rows'), pairs)  9.26 us
    ppermute x7, waiting for transfers between devices, hop(): return lax.ppermute(value, ('pts', 'rows'), pairs)  5.67 us
    pallas_call x1, Pallas kernels, per_device(): pl.pallas_call(functools.partial(post_kernel, sizes_out, blocks), out_sha...  4.04 us
    pallas_call x1, Pallas kernels, per_device(): pl.pallas_call(functools.partial(gram_kernel, sizes_in), out_shape=(summe...  2.94 us
    pallas_call x1, Pallas kernels, per_device(): ready = prep(*(in_hbm(v) for v in factors), phases, value)  2.45 us
    pallas_call x1, Pallas kernels, per_device(): probe_t = turn(held, value)  0.63 us
  transfers between devices with their start and end apart: 7, of which 6 were waited for; matrix products, arithmetic and copies ran while one was open for 0% of the time, Pallas kernels for 12%

profile of v7, /device:TPU:0, one launch (start us, length us, event | category | flops | bytes accessed | tf_op | source)
XLA Modules:
  0.0 25.2 jit_solution(18316033193951493889)
XLA Ops:
  0.0 0.0 copy-start.1
  0.0 2.9 %gram.1 = (f32[64,256]{1,0:T(8,128)S(1)}, bf16[64,8192]{1,0:T(8,128)(2,1)S(1)}) custom-call(bf16[64,8192]{1,0:T(8,128)(2,1)} %probe_hbm.1, bf16[2,8192,128]{2,1,0:T(8,128)(2,1)} %sol_hbm.1), custom_call_target="tpu_custom_call" | custom-call | tf_op jit(solution)/shard_map/gram/pallas_call | solution.py:294
  2.9 0.0 copy-start
  3.0 4.1 %collective-permute-start.2 = (f32[64,256]{1,0:T(8,128)S(1)}, f32[64,256]{1,0:T(8,128)S(1)}, u32[]{:S(2)}, u32[]{:S(2)}) collective-permute-start(f32[64,256]{1,0:T(8,128)S(1)} %get-tuple-element.17._.refs_0_), channel_id=1, source_target_pairs={{0,4},{1,5},{2,6},{3,7},{4,0},{5,1},{6,2},{7,3},{8,12},{9,13},{10,... | collective-permute-start | bytes 196616 | tf_op jit(solution)/shard_map/ppermute | solution.py:277
  7.1 1.3 %collective-permute-start.1 = (f32[64,256]{1,0:T(8,128)S(1)}, f32[64,256]{1,0:T(8,128)S(1)}, u32[]{:S(2)}, u32[]{:S(2)}) collective-permute-start(f32[64,256]{1,0:T(8,128)S(1)} %get-tuple-element.17._.refs_0_), channel_id=1, source_target_pairs={{0,6},{1,7},{2,4},{3,5},{4,2},{5,3},{6,0},{7,1},{8,14},{9,15},{10,... | collective-permute-start | bytes 196616 | tf_op jit(solution)/shard_map/ppermute | solution.py:277
  8.4 0.2 collective-permute-start
  8.6 0.0 copy-done.1
  8.6 2.4 %prep.1 = (bf16[256,768]{1,0:T(8,128)(2,1)S(1)}, bf16[768,256]{1,0:T(8,128)(2,1)S(1)}, bf16[768,256]{1,0:T(8,128)(2,1)S(1)}, bf16[256,768]{1,0:T(8,128)(2,1)S(1)...) custom-call(f32[256,256]{1,0:T(8,128)} %left_hbm.1, ...), custom_call_target="tpu_custom_call" | custom-call | flops 100663296 | bytes 4194304 | tf_op jit(solution)/shard_map/prep/pallas_call | solution.py:370
  11.1 0.0 collective-permute-done.2.refs_3_
  11.1 2.2 %collective-permute-done.1.refs_2_ = f32[64,256]{1,0:T(8,128)S(1)} collective-permute-done((f32[64,256]{1,0:T(8,128)S(1)}, f32[64,256]{1,0:T(8,128)S(1)}, u32[]{:S(2)}, u32[]{:S(2)}) %collective-permute-start.1) | collective-permute-done | bytes 65568 | tf_op jit(solution)/shard_map/ppermute | solution.py:277
  13.3 0.1 collective-permute-done.refs_1_
  13.4 0.7 %collective-permute-start.5 = (f32[64,256]{1,0:T(8,128)S(1)}, f32[64,256]{1,0:T(8,128)S(1)}, u32[]{:S(2)}, u32[]{:S(2)}) collective-permute-start(f32[64,256]{1,0:T(8,128)S(1)} %sum.1._.refs_0_), channel_id=1, source_target_pairs={{0,25},{1,24},{2,27},{3,26},{4,29},{5,28},{6,31},{7,30},{8,17},{9,... | collective-permute-start | bytes 196616 | tf_op jit(solution)/shard_map/ppermute | solution.py:277
  14.1 0.9 %collective-permute-start.4 = (f32[64,256]{1,0:T(8,128)S(1)}, f32[64,256]{1,0:T(8,128)S(1)}, u32[]{:S(2)}, u32[]{:S(2)}) collective-permute-start(f32[64,256]{1,0:T(8,128)S(1)} %sum.1._.refs_0_), channel_id=1, source_target_pairs={{0,16},{1,17},{2,18},{3,19},{4,20},{5,21},{6,22},{7,23},{8,24},{9,... | collective-permute-start | bytes 196616 | tf_op jit(solution)/shard_map/ppermute | solution.py:277
  15.0 1.4 %collective-permute-start.3 = (f32[64,256]{1,0:T(8,128)S(1)}, f32[64,256]{1,0:T(8,128)S(1)}, u32[]{:S(2)}, u32[]{:S(2)}) collective-permute-start(f32[64,256]{1,0:T(8,128)S(1)} %sum.1._.refs_0_), channel_id=1, source_target_pairs={{0,9},{1,8},{2,11},{3,10},{4,13},{5,12},{6,15},{7,14},{8,1},{9,0},... | collective-permute-start | bytes 196616 | tf_op jit(solution)/shard_map/ppermute | solution.py:277
  16.4 0.6 %turn.1.refs_4_.probe_t_ref = bf16[8192,64]{1,0:T(8,128)(2,1)S(1)} custom-call(bf16[64,8192]{1,0:T(8,128)(2,1)S(1)} %get-tuple-element.28.probe_ref, f32[64,256]{1,0:T(8,128)S(1)} %sum.1._.refs_0_), custom_call_target="tpu_custom_call" | custom-call | bytes 6291456 | tf_op jit(solution)/shard_map/turn/pallas_call | solution.py:377
  17.0 1.7 %collective-permute-done.5.refs_3_ = f32[64,256]{1,0:T(8,128)S(1)} collective-permute-done((f32[64,256]{1,0:T(8,128)S(1)}, f32[64,256]{1,0:T(8,128)S(1)}, u32[]{:S(2)}, u32[]{:S(2)}) %collective-permute-start.5) | collective-permute-done | bytes 65568 | tf_op jit(solution)/shard_map/ppermute | solution.py:277
  18.7 0.3 %collective-permute-done.4.refs_2_ = f32[64,256]{1,0:T(8,128)S(1)} collective-permute-done((f32[64,256]{1,0:T(8,128)S(1)}, f32[64,256]{1,0:T(8,128)S(1)}, u32[]{:S(2)}, u32[]{:S(2)}) %collective-permute-start.4) | collective-permute-done | bytes 65568 | tf_op jit(solution)/shard_map/ppermute | solution.py:277
  19.0 0.4 %collective-permute-done.3.refs_1_ = f32[64,256]{1,0:T(8,128)S(1)} collective-permute-done((f32[64,256]{1,0:T(8,128)S(1)}, f32[64,256]{1,0:T(8,128)S(1)}, u32[]{:S(2)}, u32[]{:S(2)}) %collective-permute-start.3) | collective-permute-done | bytes 65568 | tf_op jit(solution)/shard_map/ppermute | solution.py:277
  19.5 0.0 copy-done
  19.5 0.2 mix.1.own_ref
  19.6 0.6 %collective-permute-start.6 = (f32[224,128]{1,0:T(8,128)S(1)}, f32[224,128]{1,0:T(8,128)S(1)}, u32[]{:S(2)}, u32[]{:S(2)}) collective-permute-start(f32[224,128]{1,0:T(8,128)S(1)} %mix.1.own_ref), channel_id=1, source_target_pairs={{0,8},{1,9},{2,10},{3,11},{4,12},{5,13},{6,14},{7,15},{8,0},{9,1},... | collective-permute-start | bytes 344072 | tf_op jit(solution)/shard_map/ppermute | solution.py:277
  20.2 1.0 %collective-permute-done.6.got_ref = f32[224,128]{1,0:T(8,128)S(1)} collective-permute-done((f32[224,128]{1,0:T(8,128)S(1)}, f32[224,128]{1,0:T(8,128)S(1)}, u32[]{:S(2)}, u32[]{:S(2)}) %collective-permute-start.6) | collective-permute-done | bytes 114720 | tf_op jit(solution)/shard_map/ppermute | solution.py:277
  21.2 4.0 %post.1 = bf16[2,8192,128]{2,1,0:T(8,128)(2,1)} custom-call(f32[224,128]{1,0:T(8,128)S(1)} %mix.1.own_ref, f32[224,128]{1,0:T(8,128)S(1)} %collective-permute-done.6.got_ref, bf16[256,768]{1,0:T(8,128)(2,1)S(1)} %get-tuple-element.18.refs_4_.ut3_ref, bf16[768,256]{1,0:T(8,128)(2,1)S(1)} %get-tuple-element.19.refs_5_.w3_ref, ...), custom_call_target="tpu_custom_call" | custom-call | tf_op jit(solution)/shard_map/post/pallas_call | solution.py:389
  (1 shorter events, 0.0 us)
Async XLA Ops:
  0.0 8.6 %copy-start.1 = (f32[8,10]{1,0:T(8,128)S(1)}, f32[8,10]{1,0:T(8,128)}, u32[]{:S(2)}) copy-start(f32[8,10]{1,0:T(8,128)} %constant.4.clone.phase_ref) | copy-start | bytes 964
  2.9 16.5 %copy-start = (f32[8,8,128]{2,1,0:T(8,128)S(1)}, f32[8,8,128]{2,1,0:T(8,128)}, u32[]{:S(2)}) copy-start(f32[8,8,128]{2,1,0:T(8,128)} %constant.5.clone.table_ref) | copy-start | bytes 98308
  3.0 8.1 %collective-permute-start.2 = (f32[64,256]{1,0:T(8,128)S(1)}, f32[64,256]{1,0:T(8,128)S(1)}, u32[]{:S(2)}, u32[]{:S(2)}) collective-permute-start(f32[64,256]{1,0:T(8,128)S(1)} %get-tuple-element.17._.refs_0_), channel_id=1, source_target_pairs={{0,4},{1,5},{2,6},{3,7},{4,0},{5,1},{6,2},{7,3},{8,12},{9,13},{10,... | collective-permute-start | bytes 196616 | tf_op jit(solution)/shard_map/ppermute | solution.py:277
  7.1 6.2 %collective-permute-start.1 = (f32[64,256]{1,0:T(8,128)S(1)}, f32[64,256]{1,0:T(8,128)S(1)}, u32[]{:S(2)}, u32[]{:S(2)}) collective-permute-start(f32[64,256]{1,0:T(8,128)S(1)} %get-tuple-element.17._.refs_0_), channel_id=1, source_target_pairs={{0,6},{1,7},{2,4},{3,5},{4,2},{5,3},{6,0},{7,1},{8,14},{9,15},{10,... | collective-permute-start | bytes 196616 | tf_op jit(solution)/shard_map/ppermute | solution.py:277
  8.4 5.0 %collective-permute-start = (f32[64,256]{1,0:T(8,128)S(1)}, f32[64,256]{1,0:T(8,128)S(1)}, u32[]{:S(2)}, u32[]{:S(2)}) collective-permute-start(f32[64,256]{1,0:T(8,128)S(1)} %get-tuple-element.17._.refs_0_), channel_id=1, source_target_pairs={{0,2},{1,3},{2,0},{3,1},{4,6},{5,7},{6,4},{7,5},{8,10},{9,11},{10,... | collective-permute-start | bytes 196616 | tf_op jit(solution)/shard_map/ppermute | solution.py:277
  13.4 5.3 %collective-permute-start.5 = (f32[64,256]{1,0:T(8,128)S(1)}, f32[64,256]{1,0:T(8,128)S(1)}, u32[]{:S(2)}, u32[]{:S(2)}) collective-permute-start(f32[64,256]{1,0:T(8,128)S(1)} %sum.1._.refs_0_), channel_id=1, source_target_pairs={{0,25},{1,24},{2,27},{3,26},{4,29},{5,28},{6,31},{7,30},{8,17},{9,... | collective-permute-start | bytes 196616 | tf_op jit(solution)/shard_map/ppermute | solution.py:277
  14.1 4.9 %collective-permute-start.4 = (f32[64,256]{1,0:T(8,128)S(1)}, f32[64,256]{1,0:T(8,128)S(1)}, u32[]{:S(2)}, u32[]{:S(2)}) collective-permute-start(f32[64,256]{1,0:T(8,128)S(1)} %sum.1._.refs_0_), channel_id=1, source_target_pairs={{0,16},{1,17},{2,18},{3,19},{4,20},{5,21},{6,22},{7,23},{8,24},{9,... | collective-permute-start | bytes 196616 | tf_op jit(solution)/shard_map/ppermute | solution.py:277
  15.0 4.4 %collective-permute-start.3 = (f32[64,256]{1,0:T(8,128)S(1)}, f32[64,256]{1,0:T(8,128)S(1)}, u32[]{:S(2)}, u32[]{:S(2)}) collective-permute-start(f32[64,256]{1,0:T(8,128)S(1)} %sum.1._.refs_0_), channel_id=1, source_target_pairs={{0,9},{1,8},{2,11},{3,10},{4,13},{5,12},{6,15},{7,14},{8,1},{9,0},... | collective-permute-start | bytes 196616 | tf_op jit(solution)/shard_map/ppermute | solution.py:277
  19.6 1.6 %collective-permute-start.6 = (f32[224,128]{1,0:T(8,128)S(1)}, f32[224,128]{1,0:T(8,128)S(1)}, u32[]{:S(2)}, u32[]{:S(2)}) collective-permute-start(f32[224,128]{1,0:T(8,128)S(1)} %mix.1.own_ref), channel_id=1, source_target_pairs={{0,8},{1,9},{2,10},{3,11},{4,12},{5,13},{6,14},{7,15},{8,0},{9,1},... | collective-permute-start | bytes 344072 | tf_op jit(solution)/shard_map/ppermute | solution.py:277

commit v8 on v7

--- a/solution.py
+++ b/solution.py
@@ -277,6 +277,17 @@
     return lax.ppermute(value, ("pts", "rows"), pairs)
 
 
+def ring(value, n_pts, n_rows, low, high, step):
+    order = [0, low, low | high, high]
+    pairs = []
+    for pts in range(n_pts):
+        for row in range(n_rows):
+            rest = row & ~(low | high)
+            target = order[(order.index(row & (low | high)) + step) % 4] | rest
+            pairs.append((pts * n_rows + row, pts * n_rows + target))
+    return lax.ppermute(value, ("pts", "rows"), pairs)
+
+
 def per_device(n_pts, n_rows, solutions, probe, left_factor, singular, right_factor, adjoint):
     count, local, width2 = solutions.shape
     width = probe.shape[0]
@@ -362,8 +373,14 @@
     for at in range(0, len(bits), 2):
         step = bits[at : at + 2]
         if len(step) == 2:
-            step = [step[0], step[0] ^ step[1], step[1]]
-        got = [hop(value, n_pts, n_rows, (0, bit)) for bit in step]
+            low, high = step
+            got = [
+                ring(value, n_pts, n_rows, low, high, -1),
+                hop(value, n_pts, n_rows, (0, low ^ high)),
+                ring(value, n_pts, n_rows, low, high, 1),
+            ]
+        else:
+            got = [hop(value, n_pts, n_rows, (0, step[0]))]
         after = []
         if ready is None:
             factors = (left_factor, singular[None, :], right_factor, adjoint)

time: 25.4 us -> 25.2 us (level)
  waiting for transfers between devices: 5.67 us -> 4.06 us
  starting transfers between devices: 9.26 us -> 10.7 us
    ppermute x0 -> x2, starting transfers between devices: none -> 4.65 us  [ring(): return lax.ppermute(value, ('pts', 'rows'), pairs)]
    ppermute x7 -> x5, starting transfers between devices: 9.26 us -> 6.06 us  [hop(): return lax.ppermute(value, ('pts', 'rows'), pairs)]
    ppermute x7 -> x5, waiting for transfers between devices: 5.67 us -> 3.83 us  [hop(): return lax.ppermute(value, ('pts', 'rows'), pairs)]
where the time goes in v8:
time: 25.2 us; the launch traced here: 25.1 us
  starting transfers between devices  10.7 us (42%)
  Pallas kernels  10.2 us (40%)
  waiting for transfers between devices  4.06 us (16%)
    ppermute x5, starting transfers between devices, hop(): return lax.ppermute(value, ('pts', 'rows'), pairs)  6.06 us
    ppermute x2, starting transfers between devices, ring(): return lax.ppermute(value, ('pts', 'rows'), pairs)  4.65 us
    pallas_call x1, Pallas kernels, per_device(): pl.pallas_call(functools.partial(post_kernel, sizes_out, blocks), out_sha...  4.04 us
    ppermute x5, waiting for transfers between devices, hop(): return lax.ppermute(value, ('pts', 'rows'), pairs)  3.83 us
    pallas_call x1, Pallas kernels, per_device(): pl.pallas_call(functools.partial(gram_kernel, sizes_in), out_shape=(summe...  2.94 us
    pallas_call x1, Pallas kernels, per_device(): ready = prep(*(in_hbm(v) for v in factors), phases, value)  2.45 us
    pallas_call x1, Pallas kernels, per_device(): probe_t = turn(held, value)  0.63 us
  transfers between devices with their start and end apart: 7, of which 6 were waited for; matrix products, arithmetic and copies ran while one was open for 0% of the time, Pallas kernels for 12%

profile of v8, /device:TPU:0, one launch (start us, length us, event | category | flops | bytes accessed | tf_op | source)
XLA Modules:
  0.0 25.1 jit_solution(11518880066172575184)
XLA Ops:
  0.0 0.0 copy-start.1
  0.0 2.9 %gram.1 = (f32[64,256]{1,0:T(8,128)S(1)}, bf16[64,8192]{1,0:T(8,128)(2,1)S(1)}) custom-call(bf16[64,8192]{1,0:T(8,128)(2,1)} %probe_hbm.1, bf16[2,8192,128]{2,1,0:T(8,128)(2,1)} %sol_hbm.1), custom_call_target="tpu_custom_call" | custom-call | tf_op jit(solution)/shard_map/gram/pallas_call | solution.py:305
  2.9 0.0 copy-start
  3.0 3.1 %collective-permute-start.2 = (f32[64,256]{1,0:T(8,128)S(1)}, f32[64,256]{1,0:T(8,128)S(1)}, u32[]{:S(2)}, u32[]{:S(2)}) collective-permute-start(f32[64,256]{1,0:T(8,128)S(1)} %get-tuple-element.17._.refs_0_), channel_id=1, source_target_pairs={{0,2},{1,3},{2,6},{3,7},{4,0},{5,1},{6,4},{7,5},{8,10},{9,11},{10,... | collective-permute-start | bytes 196616 | tf_op jit(solution)/shard_map/ppermute | solution.py:288
  6.0 2.5 %collective-permute-start.1 = (f32[64,256]{1,0:T(8,128)S(1)}, f32[64,256]{1,0:T(8,128)S(1)}, u32[]{:S(2)}, u32[]{:S(2)}) collective-permute-start(f32[64,256]{1,0:T(8,128)S(1)} %get-tuple-element.17._.refs_0_), channel_id=1, source_target_pairs={{0,6},{1,7},{2,4},{3,5},{4,2},{5,3},{6,0},{7,1},{8,14},{9,15},{10,... | collective-permute-start | bytes 196616 | tf_op jit(solution)/shard_map/ppermute | solution.py:277
  8.5 1.6 %collective-permute-start = (f32[64,256]{1,0:T(8,128)S(1)}, f32[64,256]{1,0:T(8,128)S(1)}, u32[]{:S(2)}, u32[]{:S(2)}) collective-permute-start(f32[64,256]{1,0:T(8,128)S(1)} %get-tuple-element.17._.refs_0_), channel_id=1, source_target_pairs={{0,4},{1,5},{2,0},{3,1},{4,6},{5,7},{6,2},{7,3},{8,12},{9,13},{10,... | collective-permute-start | bytes 196616 | tf_op jit(solution)/shard_map/ppermute | solution.py:288
  10.1 0.0 copy-done.1
  10.1 2.5 %prep.1 = (bf16[256,768]{1,0:T(8,128)(2,1)S(1)}, bf16[768,256]{1,0:T(8,128)(2,1)S(1)}, bf16[768,256]{1,0:T(8,128)(2,1)S(1)}, bf16[256,768]{1,0:T(8,128)(2,1)S(1)...) custom-call(f32[256,256]{1,0:T(8,128)} %left_hbm.1, ...), custom_call_target="tpu_custom_call" | custom-call | flops 100663296 | bytes 4194304 | tf_op jit(solution)/shard_map/prep/pallas_call | solution.py:387
  12.5 0.0 collective-permute-done.2.refs_3_
  12.6 0.4 %collective-permute-done.1.refs_2_ = f32[64,256]{1,0:T(8,128)S(1)} collective-permute-done((f32[64,256]{1,0:T(8,128)S(1)}, f32[64,256]{1,0:T(8,128)S(1)}, u32[]{:S(2)}, u32[]{:S(2)}) %collective-permute-start.1) | collective-permute-done | bytes 65568 | tf_op jit(solution)/shard_map/ppermute | solution.py:277
  13.0 0.2 collective-permute-done.refs_1_
  13.2 0.6 %collective-permute-start.5 = (f32[64,256]{1,0:T(8,128)S(1)}, f32[64,256]{1,0:T(8,128)S(1)}, u32[]{:S(2)}, u32[]{:S(2)}) collective-permute-start(f32[64,256]{1,0:T(8,128)S(1)} %sum.1._.refs_0_), channel_id=1, source_target_pairs={{0,25},{1,24},{2,27},{3,26},{4,29},{5,28},{6,31},{7,30},{8,17},{9,... | collective-permute-start | bytes 196616 | tf_op jit(solution)/shard_map/ppermute | solution.py:277
  13.8 1.0 %collective-permute-start.4 = (f32[64,256]{1,0:T(8,128)S(1)}, f32[64,256]{1,0:T(8,128)S(1)}, u32[]{:S(2)}, u32[]{:S(2)}) collective-permute-start(f32[64,256]{1,0:T(8,128)S(1)} %sum.1._.refs_0_), channel_id=1, source_target_pairs={{0,16},{1,17},{2,18},{3,19},{4,20},{5,21},{6,22},{7,23},{8,24},{9,... | collective-permute-start | bytes 196616 | tf_op jit(solution)/shard_map/ppermute | solution.py:277
  14.9 1.4 %collective-permute-start.3 = (f32[64,256]{1,0:T(8,128)S(1)}, f32[64,256]{1,0:T(8,128)S(1)}, u32[]{:S(2)}, u32[]{:S(2)}) collective-permute-start(f32[64,256]{1,0:T(8,128)S(1)} %sum.1._.refs_0_), channel_id=1, source_target_pairs={{0,9},{1,8},{2,11},{3,10},{4,13},{5,12},{6,15},{7,14},{8,1},{9,0},... | collective-permute-start | bytes 196616 | tf_op jit(solution)/shard_map/ppermute | solution.py:277
  16.2 0.6 %turn.1.refs_4_.probe_t_ref = bf16[8192,64]{1,0:T(8,128)(2,1)S(1)} custom-call(bf16[64,8192]{1,0:T(8,128)(2,1)S(1)} %get-tuple-element.28.probe_ref, f32[64,256]{1,0:T(8,128)S(1)} %sum.1._.refs_0_), custom_call_target="tpu_custom_call" | custom-call | bytes 6291456 | tf_op jit(solution)/shard_map/turn/pallas_call | solution.py:394
  16.9 1.7 %collective-permute-done.5.refs_3_ = f32[64,256]{1,0:T(8,128)S(1)} collective-permute-done((f32[64,256]{1,0:T(8,128)S(1)}, f32[64,256]{1,0:T(8,128)S(1)}, u32[]{:S(2)}, u32[]{:S(2)}) %collective-permute-start.5) | collective-permute-done | bytes 65568 | tf_op jit(solution)/shard_map/ppermute | solution.py:277
  18.6 0.2 collective-permute-done.4.refs_2_
  18.8 0.5 %collective-permute-done.3.refs_1_ = f32[64,256]{1,0:T(8,128)S(1)} collective-permute-done((f32[64,256]{1,0:T(8,128)S(1)}, f32[64,256]{1,0:T(8,128)S(1)}, u32[]{:S(2)}, u32[]{:S(2)}) %collective-permute-start.3) | collective-permute-done | bytes 65568 | tf_op jit(solution)/shard_map/ppermute | solution.py:277
  19.3 0.0 copy-done
  19.3 0.2 mix.1.own_ref
  19.5 0.6 %collective-permute-start.6 = (f32[224,128]{1,0:T(8,128)S(1)}, f32[224,128]{1,0:T(8,128)S(1)}, u32[]{:S(2)}, u32[]{:S(2)}) collective-permute-start(f32[224,128]{1,0:T(8,128)S(1)} %mix.1.own_ref), channel_id=1, source_target_pairs={{0,8},{1,9},{2,10},{3,11},{4,12},{5,13},{6,14},{7,15},{8,0},{9,1},... | collective-permute-start | bytes 344072 | tf_op jit(solution)/shard_map/ppermute | solution.py:277
  20.1 1.0 %collective-permute-done.6.got_ref = f32[224,128]{1,0:T(8,128)S(1)} collective-permute-done((f32[224,128]{1,0:T(8,128)S(1)}, f32[224,128]{1,0:T(8,128)S(1)}, u32[]{:S(2)}, u32[]{:S(2)}) %collective-permute-start.6) | collective-permute-done | bytes 114720 | tf_op jit(solution)/shard_map/ppermute | solution.py:277
  21.0 4.0 %post.1 = bf16[2,8192,128]{2,1,0:T(8,128)(2,1)} custom-call(f32[224,128]{1,0:T(8,128)S(1)} %mix.1.own_ref, f32[224,128]{1,0:T(8,128)S(1)} %collective-permute-done.6.got_ref, bf16[256,768]{1,0:T(8,128)(2,1)S(1)} %get-tuple-element.18.refs_4_.ut3_ref, bf16[768,256]{1,0:T(8,128)(2,1)S(1)} %get-tuple-element.19.refs_5_.w3_ref, ...), custom_call_target="tpu_custom_call" | custom-call | tf_op jit(solution)/shard_map/post/pallas_call | solution.py:406
  (1 shorter events, 0.0 us)
Async XLA Ops:
  0.0 10.1 %copy-start.1 = (f32[8,10]{1,0:T(8,128)S(1)}, f32[8,10]{1,0:T(8,128)}, u32[]{:S(2)}) copy-start(f32[8,10]{1,0:T(8,128)} %constant.4.clone.phase_ref) | copy-start | bytes 964
  2.9 16.4 %copy-start = (f32[8,8,128]{2,1,0:T(8,128)S(1)}, f32[8,8,128]{2,1,0:T(8,128)}, u32[]{:S(2)}) copy-start(f32[8,8,128]{2,1,0:T(8,128)} %constant.5.clone.table_ref) | copy-start | bytes 98308
  3.0 9.6 %collective-permute-start.2 = (f32[64,256]{1,0:T(8,128)S(1)}, f32[64,256]{1,0:T(8,128)S(1)}, u32[]{:S(2)}, u32[]{:S(2)}) collective-permute-start(f32[64,256]{1,0:T(8,128)S(1)} %get-tuple-element.17._.refs_0_), channel_id=1, source_target_pairs={{0,2},{1,3},{2,6},{3,7},{4,0},{5,1},{6,4},{7,5},{8,10},{9,11},{10,... | collective-permute-start | bytes 196616 | tf_op jit(solution)/shard_map/ppermute | solution.py:288
  6.0 7.0 %collective-permute-start.1 = (f32[64,256]{1,0:T(8,128)S(1)}, f32[64,256]{1,0:T(8,128)S(1)}, u32[]{:S(2)}, u32[]{:S(2)}) collective-permute-start(f32[64,256]{1,0:T(8,128)S(1)} %get-tuple-element.17._.refs_0_), channel_id=1, source_target_pairs={{0,6},{1,7},{2,4},{3,5},{4,2},{5,3},{6,0},{7,1},{8,14},{9,15},{10,... | collective-permute-start | bytes 196616 | tf_op jit(solution)/shard_map/ppermute | solution.py:277
  8.5 4.7 %collective-permute-start = (f32[64,256]{1,0:T(8,128)S(1)}, f32[64,256]{1,0:T(8,128)S(1)}, u32[]{:S(2)}, u32[]{:S(2)}) collective-permute-start(f32[64,256]{1,0:T(8,128)S(1)} %get-tuple-element.17._.refs_0_), channel_id=1, source_target_pairs={{0,4},{1,5},{2,0},{3,1},{4,6},{5,7},{6,2},{7,3},{8,12},{9,13},{10,... | collective-permute-start | bytes 196616 | tf_op jit(solution)/shard_map/ppermute | solution.py:288
  13.2 5.3 %collective-permute-start.5 = (f32[64,256]{1,0:T(8,128)S(1)}, f32[64,256]{1,0:T(8,128)S(1)}, u32[]{:S(2)}, u32[]{:S(2)}) collective-permute-start(f32[64,256]{1,0:T(8,128)S(1)} %sum.1._.refs_0_), channel_id=1, source_target_pairs={{0,25},{1,24},{2,27},{3,26},{4,29},{5,28},{6,31},{7,30},{8,17},{9,... | collective-permute-start | bytes 196616 | tf_op jit(solution)/shard_map/ppermute | solution.py:277
  13.8 5.0 %collective-permute-start.4 = (f32[64,256]{1,0:T(8,128)S(1)}, f32[64,256]{1,0:T(8,128)S(1)}, u32[]{:S(2)}, u32[]{:S(2)}) collective-permute-start(f32[64,256]{1,0:T(8,128)S(1)} %sum.1._.refs_0_), channel_id=1, source_target_pairs={{0,16},{1,17},{2,18},{3,19},{4,20},{5,21},{6,22},{7,23},{8,24},{9,... | collective-permute-start | bytes 196616 | tf_op jit(solution)/shard_map/ppermute | solution.py:277
  14.9 4.4 %collective-permute-start.3 = (f32[64,256]{1,0:T(8,128)S(1)}, f32[64,256]{1,0:T(8,128)S(1)}, u32[]{:S(2)}, u32[]{:S(2)}) collective-permute-start(f32[64,256]{1,0:T(8,128)S(1)} %sum.1._.refs_0_), channel_id=1, source_target_pairs={{0,9},{1,8},{2,11},{3,10},{4,13},{5,12},{6,15},{7,14},{8,1},{9,0},... | collective-permute-start | bytes 196616 | tf_op jit(solution)/shard_map/ppermute | solution.py:277
  19.5 1.6 %collective-permute-start.6 = (f32[224,128]{1,0:T(8,128)S(1)}, f32[224,128]{1,0:T(8,128)S(1)}, u32[]{:S(2)}, u32[]{:S(2)}) collective-permute-start(f32[224,128]{1,0:T(8,128)S(1)} %mix.1.own_ref), channel_id=1, source_target_pairs={{0,8},{1,9},{2,10},{3,11},{4,12},{5,13},{6,14},{7,15},{8,0},{9,1},... | collective-permute-start | bytes 344072 | tf_op jit(solution)/shard_map/ppermute | solution.py:277

commit v9 on v8

--- a/solution.py
+++ b/solution.py
@@ -385,22 +385,22 @@
         if ready is None:
             factors = (left_factor, singular[None, :], right_factor, adjoint)
             ready = prep(*(in_hbm(v) for v in factors), phases, value)
-            after = ready
+            probe_t = turn(held, value)
+            after = [*ready, probe_t]
         value = add([value] + got, after)
     others = [(pts, 0) for pts in range(2, n_pts, 2)]
     if n_rows > 1:
         others = [(1, 1)] + others + [(pts ^ 1, 1) for pts, _ in others]
     grams = [value] + [hop(value, n_pts, n_rows, mask) for mask in others]
-    probe_t = turn(held, value)
     rows = (blocks - 1) * width + width // 2
     moments = pl.pallas_call(
         functools.partial(mix_kernel, blocks, [0] + [mask[0] for mask in others]),
         out_shape=jax.ShapeDtypeStruct((rows, width2), F32),
-        in_specs=[vmem] * (1 + len(grams)) + [anyspace],
+        in_specs=[vmem] * (1 + len(grams)),
         out_specs=vmem,
         compiler_params=params,
         name="mix",
-    )(jnp.asarray(moment_table(total, blocks, width)), *grams, probe_t)
+    )(jnp.asarray(moment_table(total, blocks, width)), *grams)
     other = hop(moments, n_pts, n_rows, (1, 0))
     sizes_out = [unit, unit] + [2 * unit] * 7
     return pl.pallas_call(

time: 25.2 us -> 25.3 us (level)
  transfers between devices with their start and end apart: 7 -> 7, of which waited for: 6 -> 4; matrix products, arithmetic and copies ran while one was open for 0% -> 0% of each run, Pallas kernels for 12% -> 12%
where the time goes in v9:
time: 25.3 us; the launch traced here: 25.1 us
  starting transfers between devices  10.7 us (42%)
  Pallas kernels  10.3 us (41%)
  waiting for transfers between devices  4.04 us (16%)
    ppermute x5, starting transfers between devices, hop(): return lax.ppermute(value, ('pts', 'rows'), pairs)  6.06 us
    ppermute x2, starting transfers between devices, ring(): return lax.ppermute(value, ('pts', 'rows'), pairs)  4.65 us
    pallas_call x1, Pallas kernels, per_device(): pl.pallas_call(functools.partial(post_kernel, sizes_out, blocks), out_sha...  4.05 us
    ppermute x5, waiting for transfers between devices, hop(): return lax.ppermute(value, ('pts', 'rows'), pairs)  4.03 us
    pallas_call x1, Pallas kernels, per_device(): pl.pallas_call(functools.partial(gram_kernel, sizes_in), out_shape=(summe...  2.94 us
    pallas_call x1, Pallas kernels, per_device(): ready = prep(*(in_hbm(v) for v in factors), phases, value)  2.46 us
    pallas_call x1, Pallas kernels, per_device(): probe_t = turn(held, value)  0.63 us
  transfers between devices with their start and end apart: 7, of which 4 were waited for; matrix products, arithmetic and copies ran while one was open for 0% of the time, Pallas kernels for 12%

profile of v9, /device:TPU:0, one launch (start us, length us, event | category | flops | bytes accessed | tf_op | source)
XLA Modules:
  0.0 25.1 jit_solution(14511795771219629789)
XLA Ops:
  0.0 0.0 copy-start.1
  0.0 2.9 %gram.1 = (f32[64,256]{1,0:T(8,128)S(1)}, bf16[64,8192]{1,0:T(8,128)(2,1)S(1)}) custom-call(bf16[64,8192]{1,0:T(8,128)(2,1)} %probe_hbm.1, bf16[2,8192,128]{2,1,0:T(8,128)(2,1)} %sol_hbm.1), custom_call_target="tpu_custom_call" | custom-call | tf_op jit(solution)/shard_map/gram/pallas_call | solution.py:305
  2.9 3.1 %collective-permute-start.2 = (f32[64,256]{1,0:T(8,128)S(1)}, f32[64,256]{1,0:T(8,128)S(1)}, u32[]{:S(2)}, u32[]{:S(2)}) collective-permute-start(f32[64,256]{1,0:T(8,128)S(1)} %get-tuple-element.17._.refs_0_), channel_id=1, source_target_pairs={{0,2},{1,3},{2,6},{3,7},{4,0},{5,1},{6,4},{7,5},{8,10},{9,11},{10,... | collective-permute-start | bytes 196616 | tf_op jit(solution)/shard_map/ppermute | solution.py:288
  6.0 2.5 %collective-permute-start.1 = (f32[64,256]{1,0:T(8,128)S(1)}, f32[64,256]{1,0:T(8,128)S(1)}, u32[]{:S(2)}, u32[]{:S(2)}) collective-permute-start(f32[64,256]{1,0:T(8,128)S(1)} %get-tuple-element.17._.refs_0_), channel_id=1, source_target_pairs={{0,6},{1,7},{2,4},{3,5},{4,2},{5,3},{6,0},{7,1},{8,14},{9,15},{10,... | collective-permute-start | bytes 196616 | tf_op jit(solution)/shard_map/ppermute | solution.py:277
  8.5 1.6 %collective-permute-start = (f32[64,256]{1,0:T(8,128)S(1)}, f32[64,256]{1,0:T(8,128)S(1)}, u32[]{:S(2)}, u32[]{:S(2)}) collective-permute-start(f32[64,256]{1,0:T(8,128)S(1)} %get-tuple-element.17._.refs_0_), channel_id=1, source_target_pairs={{0,4},{1,5},{2,0},{3,1},{4,6},{5,7},{6,2},{7,3},{8,12},{9,13},{10,... | collective-permute-start | bytes 196616 | tf_op jit(solution)/shard_map/ppermute | solution.py:288
  10.1 0.6 %turn.1.refs_14_.probe_t_ref = bf16[8192,64]{1,0:T(8,128)(2,1)S(1)} custom-call(bf16[64,8192]{1,0:T(8,128)(2,1)S(1)} %get-tuple-element.28.probe_ref, f32[64,256]{1,0:T(8,128)S(1)} %get-tuple-element.17._.refs_0_), custom_call_target="tpu_custom_call" | custom-call | bytes 6291456 | tf_op jit(solution)/shard_map/turn/pallas_call | solution.py:388
  10.7 0.0 copy-start
  10.7 0.0 copy-done.1
  10.7 2.5 %prep.1 = (bf16[256,768]{1,0:T(8,128)(2,1)S(1)}, bf16[768,256]{1,0:T(8,128)(2,1)S(1)}, bf16[768,256]{1,0:T(8,128)(2,1)S(1)}, bf16[256,768]{1,0:T(8,128)(2,1)S(1)...) custom-call(f32[256,256]{1,0:T(8,128)} %left_hbm.1, ...), custom_call_target="tpu_custom_call" | custom-call | flops 100663296 | bytes 4194304 | tf_op jit(solution)/shard_map/prep/pallas_call | solution.py:387
  13.2 0.0 collective-permute-done.2.refs_3_
  13.2 0.0 collective-permute-done.1.refs_2_
  13.2 0.0 collective-permute-done.refs_1_
  13.3 1.1 %collective-permute-start.5 = (f32[64,256]{1,0:T(8,128)S(1)}, f32[64,256]{1,0:T(8,128)S(1)}, u32[]{:S(2)}, u32[]{:S(2)}) collective-permute-start(f32[64,256]{1,0:T(8,128)S(1)} %sum.1.refs_0_), channel_id=1, source_target_pairs={{0,25},{1,24},{2,27},{3,26},{4,29},{5,28},{6,31},{7,30},{8,17},{9,... | collective-permute-start | bytes 196616 | tf_op jit(solution)/shard_map/ppermute | solution.py:277
  14.4 0.5 %collective-permute-start.4 = (f32[64,256]{1,0:T(8,128)S(1)}, f32[64,256]{1,0:T(8,128)S(1)}, u32[]{:S(2)}, u32[]{:S(2)}) collective-permute-start(f32[64,256]{1,0:T(8,128)S(1)} %sum.1.refs_0_), channel_id=1, source_target_pairs={{0,16},{1,17},{2,18},{3,19},{4,20},{5,21},{6,22},{7,23},{8,24},{9,... | collective-permute-start | bytes 196616 | tf_op jit(solution)/shard_map/ppermute | solution.py:277
  14.9 1.3 %collective-permute-start.3 = (f32[64,256]{1,0:T(8,128)S(1)}, f32[64,256]{1,0:T(8,128)S(1)}, u32[]{:S(2)}, u32[]{:S(2)}) collective-permute-start(f32[64,256]{1,0:T(8,128)S(1)} %sum.1.refs_0_), channel_id=1, source_target_pairs={{0,9},{1,8},{2,11},{3,10},{4,13},{5,12},{6,15},{7,14},{8,1},{9,0},... | collective-permute-start | bytes 196616 | tf_op jit(solution)/shard_map/ppermute | solution.py:277
  16.2 2.3 %collective-permute-done.5.refs_3_ = f32[64,256]{1,0:T(8,128)S(1)} collective-permute-done((f32[64,256]{1,0:T(8,128)S(1)}, f32[64,256]{1,0:T(8,128)S(1)}, u32[]{:S(2)}, u32[]{:S(2)}) %collective-permute-start.5) | collective-permute-done | bytes 65568 | tf_op jit(solution)/shard_map/ppermute | solution.py:277
  18.6 0.4 %collective-permute-done.4.refs_2_ = f32[64,256]{1,0:T(8,128)S(1)} collective-permute-done((f32[64,256]{1,0:T(8,128)S(1)}, f32[64,256]{1,0:T(8,128)S(1)}, u32[]{:S(2)}, u32[]{:S(2)}) %collective-permute-start.4) | collective-permute-done | bytes 65568 | tf_op jit(solution)/shard_map/ppermute | solution.py:277
  18.9 0.4 %collective-permute-done.3.refs_1_ = f32[64,256]{1,0:T(8,128)S(1)} collective-permute-done((f32[64,256]{1,0:T(8,128)S(1)}, f32[64,256]{1,0:T(8,128)S(1)}, u32[]{:S(2)}, u32[]{:S(2)}) %collective-permute-start.3) | collective-permute-done | bytes 65568 | tf_op jit(solution)/shard_map/ppermute | solution.py:277
  19.3 0.0 copy-done
  19.3 0.2 mix.1.own_ref
  19.5 0.6 %collective-permute-start.6 = (f32[224,128]{1,0:T(8,128)S(1)}, f32[224,128]{1,0:T(8,128)S(1)}, u32[]{:S(2)}, u32[]{:S(2)}) collective-permute-start(f32[224,128]{1,0:T(8,128)S(1)} %mix.1.own_ref), channel_id=1, source_target_pairs={{0,8},{1,9},{2,10},{3,11},{4,12},{5,13},{6,14},{7,15},{8,0},{9,1},... | collective-permute-start | bytes 344072 | tf_op jit(solution)/shard_map/ppermute | solution.py:277
  20.1 1.0 %collective-permute-done.6.got_ref = f32[224,128]{1,0:T(8,128)S(1)} collective-permute-done((f32[224,128]{1,0:T(8,128)S(1)}, f32[224,128]{1,0:T(8,128)S(1)}, u32[]{:S(2)}, u32[]{:S(2)}) %collective-permute-start.6) | collective-permute-done | bytes 114720 | tf_op jit(solution)/shard_map/ppermute | solution.py:277
  21.1 4.0 %post.1 = bf16[2,8192,128]{2,1,0:T(8,128)(2,1)} custom-call(f32[224,128]{1,0:T(8,128)S(1)} %mix.1.own_ref, f32[224,128]{1,0:T(8,128)S(1)} %collective-permute-done.6.got_ref, bf16[256,768]{1,0:T(8,128)(2,1)S(1)} %get-tuple-element.18.refs_4_.ut3_ref, bf16[768,256]{1,0:T(8,128)(2,1)S(1)} %get-tuple-element.19.refs_5_.w3_ref, ...), custom_call_target="tpu_custom_call" | custom-call | tf_op jit(solution)/shard_map/post/pallas_call | solution.py:406
  (1 shorter events, 0.0 us)
Async XLA Ops:
  0.0 10.7 %copy-start.1 = (f32[8,10]{1,0:T(8,128)S(1)}, f32[8,10]{1,0:T(8,128)}, u32[]{:S(2)}) copy-start(f32[8,10]{1,0:T(8,128)} %constant.4.clone.phase_ref) | copy-start | bytes 964
  2.9 10.2 %collective-permute-start.2 = (f32[64,256]{1,0:T(8,128)S(1)}, f32[64,256]{1,0:T(8,128)S(1)}, u32[]{:S(2)}, u32[]{:S(2)}) collective-permute-start(f32[64,256]{1,0:T(8,128)S(1)} %get-tuple-element.17._.refs_0_), channel_id=1, source_target_pairs={{0,2},{1,3},{2,6},{3,7},{4,0},{5,1},{6,4},{7,5},{8,10},{9,11},{10,... | collective-permute-start | bytes 196616 | tf_op jit(solution)/shard_map/ppermute | solution.py:288
  6.0 7.2 %collective-permute-start.1 = (f32[64,256]{1,0:T(8,128)S(1)}, f32[64,256]{1,0:T(8,128)S(1)}, u32[]{:S(2)}, u32[]{:S(2)}) collective-permute-start(f32[64,256]{1,0:T(8,128)S(1)} %get-tuple-element.17._.refs_0_), channel_id=1, source_target_pairs={{0,6},{1,7},{2,4},{3,5},{4,2},{5,3},{6,0},{7,1},{8,14},{9,15},{10,... | collective-permute-start | bytes 196616 | tf_op jit(solution)/shard_map/ppermute | solution.py:277
  8.5 4.7 %collective-permute-start = (f32[64,256]{1,0:T(8,128)S(1)}, f32[64,256]{1,0:T(8,128)S(1)}, u32[]{:S(2)}, u32[]{:S(2)}) collective-permute-start(f32[64,256]{1,0:T(8,128)S(1)} %get-tuple-element.17._.refs_0_), channel_id=1, source_target_pairs={{0,4},{1,5},{2,0},{3,1},{4,6},{5,7},{6,2},{7,3},{8,12},{9,13},{10,... | collective-permute-start | bytes 196616 | tf_op jit(solution)/shard_map/ppermute | solution.py:288
  10.7 8.6 %copy-start = (f32[8,8,128]{2,1,0:T(8,128)S(1)}, f32[8,8,128]{2,1,0:T(8,128)}, u32[]{:S(2)}) copy-start(f32[8,8,128]{2,1,0:T(8,128)} %constant.5.clone.table_ref) | copy-start | bytes 98308
  13.3 5.3 %collective-permute-start.5 = (f32[64,256]{1,0:T(8,128)S(1)}, f32[64,256]{1,0:T(8,128)S(1)}, u32[]{:S(2)}, u32[]{:S(2)}) collective-permute-start(f32[64,256]{1,0:T(8,128)S(1)} %sum.1.refs_0_), channel_id=1, source_target_pairs={{0,25},{1,24},{2,27},{3,26},{4,29},{5,28},{6,31},{7,30},{8,17},{9,... | collective-permute-start | bytes 196616 | tf_op jit(solution)/shard_map/ppermute | solution.py:277
  14.4 4.6 %collective-permute-start.4 = (f32[64,256]{1,0:T(8,128)S(1)}, f32[64,256]{1,0:T(8,128)S(1)}, u32[]{:S(2)}, u32[]{:S(2)}) collective-permute-start(f32[64,256]{1,0:T(8,128)S(1)} %sum.1.refs_0_), channel_id=1, source_target_pairs={{0,16},{1,17},{2,18},{3,19},{4,20},{5,21},{6,22},{7,23},{8,24},{9,... | collective-permute-start | bytes 196616 | tf_op jit(solution)/shard_map/ppermute | solution.py:277
  14.9 4.4 %collective-permute-start.3 = (f32[64,256]{1,0:T(8,128)S(1)}, f32[64,256]{1,0:T(8,128)S(1)}, u32[]{:S(2)}, u32[]{:S(2)}) collective-permute-start(f32[64,256]{1,0:T(8,128)S(1)} %sum.1.refs_0_), channel_id=1, source_target_pairs={{0,9},{1,8},{2,11},{3,10},{4,13},{5,12},{6,15},{7,14},{8,1},{9,0},... | collective-permute-start | bytes 196616 | tf_op jit(solution)/shard_map/ppermute | solution.py:277
  19.5 1.6 %collective-permute-start.6 = (f32[224,128]{1,0:T(8,128)S(1)}, f32[224,128]{1,0:T(8,128)S(1)}, u32[]{:S(2)}, u32[]{:S(2)}) collective-permute-start(f32[224,128]{1,0:T(8,128)S(1)} %mix.1.own_ref), channel_id=1, source_target_pairs={{0,8},{1,9},{2,10},{3,11},{4,12},{5,13},{6,14},{7,15},{8,0},{9,1},... | collective-permute-start | bytes 344072 | tf_op jit(solution)/shard_map/ppermute | solution.py:277
